TPU v7x, 512 devices: a whole 4x4x16 slice. The times are simulated.
512 devices in a mesh: frame: 32 (over z_hi, y, x), tensor: 16 (over z_lo, core).
Axes of the slice: x: 4, y: 4, z: 16 (z_hi: 2, z_lo: 8; z = z_hi * 8 + z_lo), core: 2. Of those that a mesh axis runs over, the one named last changes fastest.
Arguments:
- tokens: bfloat16 [16384, 1, 4096], P(('frame', 'tensor')), may hold values from -6 to 6
- norm_gain: float32 [4096], replicated, may hold values from 0.5 to 1.5
- query_weight: bfloat16 [4096, 4096], P(None, 'tensor'), may hold values from -0.09375 to 0.09375
- out_weight: bfloat16 [4096, 4096], P('tensor'), may hold values from -0.09375 to 0.09375
- cache_keys: bfloat16 [1536, 1, 4096], P('frame', None, 'tensor'), may hold values from -420 to 420
- cache_values: bfloat16 [1536, 1, 4096], P('frame', None, 'tensor'), may hold values from -18 to 18
- token_pos: int32 [16384, 1], P('frame'), may hold values from 0 to 1535, as said below
- frame_pad: int32 [1], replicated, may hold values from 0 to 768
Outputs:
- mixed: bfloat16 [16384, 1, 4096], P(('frame', 'tensor'))
Inputs may be any that keep to these rules, and one draw needn't show every extreme that they name: `token_pos`: nondecreasing along each sequence; the last token of every sequence has 1535.
All inputs are finite; a program needn't handle non-finite values.
Results may differ from a plain program's by a relative error of at most 0.018.
Values may be sent and summed in bfloat16 or wider, within the bound.
No kernel may reach another device: no remote copies, remote signals or barrier semaphores. Data moves between devices by JAX's collectives and lax.ppermute only.
A program may use at most 64 MiB of HBM per device.

v0:
```python
import jax
import jax.numpy as jnp
from jax import lax
from jax.sharding import PartitionSpec as P

HEAD_DIM = 128


epsilon = 1e-06
masked_score = -1e30


def normalize(block_rows, norm_gain):
    hidden = block_rows.astype(jnp.float32)
    factor = lax.rsqrt(jnp.mean(hidden * hidden, axis=-1, keepdims=True) + epsilon)
    return (hidden * factor * norm_gain).astype(jnp.bfloat16)


def per_device(
    tokens, norm_gain, query_weight, out_weight, cache_keys, cache_values, token_pos, frame_pad
):
    head_cols = query_weight.shape[1]
    heads_here = head_cols // HEAD_DIM
    seq_count = tokens.shape[1]
    query_scale = HEAD_DIM ** (-0.5)
    outgoing = normalize(tokens, norm_gain)
    queries = (
        jnp.dot(
            lax.all_gather(outgoing, "tensor", axis=0, tiled=True),
            query_weight,
            preferred_element_type=jnp.float32,
        )
        * query_scale
    ).astype(jnp.bfloat16)
    query_rows = queries.shape[0]
    query_heads = queries.reshape(query_rows, seq_count, heads_here, HEAD_DIM)
    all_frames = cache_keys.shape[0] * lax.axis_size("frame")
    valid_frames = all_frames - frame_pad
    start_max = jnp.full((query_rows, seq_count, heads_here), masked_score, jnp.float32)
    running_max = start_max
    key_piece = lax.all_gather(cache_keys, "frame", axis=0, tiled=True)
    value_piece = lax.all_gather(cache_values, "frame", axis=0, tiled=True)
    row_count = key_piece.shape[0]
    frame_index = jnp.arange(row_count, dtype=jnp.int32)
    visible = (frame_index[None, None, :] <= token_pos[:, :, None]) & (
        frame_index[None, None, :] < valid_frames[None, :, None]
    )
    key_heads = key_piece.reshape(row_count, seq_count, heads_here, HEAD_DIM)
    scores = jnp.einsum(
        "rshd,fshd->rshf", query_heads, key_heads, preferred_element_type=jnp.float32
    )
    visible = visible[:, :, None, :]
    scores, visible = (jnp.where(visible, scores, masked_score), visible)
    new_max = jnp.maximum(running_max, jnp.max(scores, axis=-1))
    weights = jnp.where(visible, jnp.exp(scores - new_max[..., None]), 0.0)
    running_sum = jnp.sum(weights, axis=-1)
    value_heads = value_piece.reshape(value_piece.shape[0], seq_count, heads_here, HEAD_DIM)
    accumulated = jnp.einsum(
        "rshf,fshd->rshd",
        weights.astype(jnp.bfloat16),
        value_heads,
        preferred_element_type=jnp.float32,
    )
    running_max, running_sum, accumulated = (new_max, running_sum, accumulated)
    attended = (
        (accumulated / running_sum[..., None])
        .astype(jnp.bfloat16)
        .reshape(query_rows, seq_count, head_cols)
    )
    return lax.psum_scatter(
        jnp.dot(attended, out_weight, preferred_element_type=jnp.float32).astype(jnp.bfloat16),
        "tensor",
        scatter_dimension=0,
        tiled=True,
    )


def solution(mesh):
    placed = (
        P(("frame", "tensor"), None, None),
        P(),
        P(None, "tensor"),
        P("tensor", None),
        P("frame", None, "tensor"),
        P("frame", None, "tensor"),
        P("frame", None),
        P(),
    )
    return jax.shard_map(
        per_device,
        mesh=mesh,
        in_specs=placed,
        out_specs=P(("frame", "tensor"), None, None),
        check_vma=False,
    )
```

profile of v0, /device:TPU:1, one launch (start us, length us, event | category | flops | bytes accessed | tf_op | source)
XLA Modules:
  0.0 458.3 jit_solution(3910015531161201871)
XLA Ops:
  6.5 0.0 copy-start
  6.5 0.0 all-gather.2.cloned.1.call-start
  6.5 1.3 fusion.26
  7.8 1.8 fusion.28
  9.6 0.0 all-gather.2.cloned.1.call-update
  9.6 0.0 reduce-scatter.2.cloned.1.call-start
  10.3 159.1 %all_gather.10 = bf16[1536,1,256]{2,0,1:T(8,128)(2,1)S(1)} all-gather(bf16[48,1,256]{2,0,1:T(8,128)(2,1)} %param.12), channel_id=1, replica_groups=mesh['frame'=32,'tensor'=16] {'frame'}, dimensions={0}, use_global_device_ids=true | all-gather | bytes 811008 | tf_op jit(solution)/shard_map/all_gather | solution.py:41
  169.4 1.2 copy.15
  170.6 141.2 %all_gather.11 = bf16[1536,1,256]{2,0,1:T(8,128)(2,1)S(1)} all-gather(bf16[48,1,256]{2,0,1:T(8,128)(2,1)} %param.13), channel_id=1, replica_groups=mesh['frame'=32,'tensor'=16] {'frame'}, dimensions={0}, use_global_device_ids=true | all-gather | bytes 811008 | tf_op jit(solution)/shard_map/all_gather | solution.py:42
  311.8 1.2 copy.18
  312.9 1.3 fusion.9
  314.2 0.0 all-gather.2.cloned.1.call-done
  314.2 0.0 copy-start.1
  314.2 4.2 fusion.17
  318.5 0.0 copy-done.1
  318.5 0.0 copy-start.2
  318.5 1.4 fusion
  319.9 2.0 fusion.2
  321.9 0.0 copy-done.2
  321.9 1.9 fusion.23
  323.8 0.0 copy-done
  323.8 3.2 fusion.1
  327.0 0.0 reduce-scatter.2.cloned.1.call-update
  327.0 124.4 %reduce-scatter.2.cloned.1.call-done = bf16[32,1,4096]{2,0,1:T(8,128)(2,1)} async-done(((bf16[512,1,4096]{2,0,1:T(8,128)(2,1)}), bf16[32,1,4096]{2,0,1:T(8,128)(2,1)}) %reduce-scatter.2.cloned.1.call-update) | async-done | bytes 262160 | tf_op jit(solution)/shard_map/reduce_scatter | solution.py:70
  (3 shorter events, 0.0 us)
Async XLA Ops:
  6.5 317.3 %copy-start = (bf16[256,4096]{1,0:T(8,128)(2,1)S(1)}, bf16[256,4096]{1,0:T(8,128)(2,1)}, u32[]{:S(2)}) copy-start(bf16[256,4096]{1,0:T(8,128)(2,1)} %param.11) | copy-start | bytes 6291460
  6.5 307.7 %all-gather.2.cloned.1.call-start = ((), (), s32[]{:S(2)}) async-start(), calls=%async_computation.1 | async-start | bytes 4456448 | tf_op jit(solution)/shard_map/all_gather | solution.py:29
  9.6 441.8 %reduce-scatter.2.cloned.1.call-start = ((), (), s32[]{:S(2)}) async-start(), calls=%async_computation.2 | async-start | bytes 4456448 | tf_op jit(solution)/shard_map/reduce_scatter | solution.py:70
  314.2 4.2 copy-start.1
  318.5 3.4 copy-start.2
Sparse Core Ops, SparseCore 0:
  9.7 112.2 all-gather.1
  327.2 124.2 reduce-scatter.1
where the time goes:
time: 465 us; the launch traced here: 458 us
  blocking collectives  300 us (65%)
  waiting for transfers between devices  124 us (27%)
  between operations  14.1 us (3%)
  matrix products  10.7 us (2%)
  other arithmetic  6.36 us (1%)
    all_gather x1, blocking collectives, per_device(): key_piece = lax.all_gather(cache_keys, 'frame', axis=0, tiled=True)  159 us
    all_gather x1, blocking collectives, per_device(): value_piece = lax.all_gather(cache_values, 'frame', axis=0, tiled=True)  141 us
    reduce_scatter x1, waiting for transfers between devices, per_device(): lax.psum_scatter(jnp.dot(attended, out_weight, preferred_element_type=jnp...  124 us
  transfers between devices with their start and end apart: 2, of which 1 were waited for; matrix products, arithmetic and copies ran while one was open for 1% of the time, Pallas kernels for 0%

commit v1 on v0

v1 whole, which is shorter than its diff:
```python
import jax
import jax.numpy as jnp
from jax import lax
from jax.sharding import Mesh, PartitionSpec as P

HEAD_DIM = 128
EPSILON = 1e-06
MASKED = -1e30
RING = ("zh", "zl")
SWAP = [(0, 1), (1, 0)]


def shift(step):
    return [(i, (i + step) % 16) for i in range(16)]


def opposite(step):
    return [
        (2 * i + c, 2 * ((i + (step if c == 0 else -step)) % 16) + c)
        for i in range(16)
        for c in range(2)
    ]


def normalize(rows, gain):
    hidden = rows.astype(jnp.float32)
    factor = lax.rsqrt(jnp.mean(hidden * hidden, axis=-1, keepdims=True) + EPSILON)
    return (hidden * factor * gain).astype(jnp.bfloat16)


def up(x):
    return lax.ppermute(x, RING, shift(1))


def down(x):
    return lax.ppermute(x, RING, shift(-1))


def per_device(tokens, gain, wq, wo, keys, values, token_pos, frame_pad):
    rows = tokens.shape[0]
    zh, zl, core = (lax.axis_index(a) for a in ("zh", "zl", "c"))
    z = zh * 8 + zl

    pos = token_pos.reshape(2, 256)
    mine = jnp.concatenate(
        [
            keys.reshape(48, 256),
            values.reshape(48, 256),
            (pos // 8).astype(jnp.bfloat16),
            (pos % 8).astype(jnp.bfloat16),
            jnp.zeros((4, 256), jnp.bfloat16),
        ]
    )
    theirs = lax.ppermute(mine, "zh", SWAP)
    other_pos = (
        theirs[96:98].astype(jnp.int32) * 8 + theirs[98:100].astype(jnp.int32)
    ).reshape(512)
    kv = jnp.stack([mine[:96], theirs[:96]]).reshape(2, 2, 48, 256)
    kv = lax.all_gather(kv, "x", axis=0)
    k_own = lax.all_gather(kv[:, :, 0], "y", axis=0).reshape(1536, 256)
    v_own = lax.all_gather(kv[:, :, 1], "y", axis=0).reshape(1536, 256)
    k_oth = lax.ppermute(k_own, "c", SWAP)
    v_oth = lax.ppermute(v_own, "c", SWAP)
    index = jnp.arange(1536, dtype=jnp.int32)
    half = (index // 48) % 2
    half = jnp.where(half == 0, zh, 1 - zh)
    frame = (half * 16 + index // 96) * 48 + index % 48

    wq_oth = lax.ppermute(wq, "c", SWAP)
    wo_oth = lax.ppermute(wo, "c", SWAP)

    own = normalize(tokens.reshape(rows, -1), gain)
    p1, m1 = up(own), down(own)
    p2, m2 = up(p1), down(m1)
    p3, m3 = up(p2), down(m2)
    far = lax.ppermute(jnp.where(core == 0, p3, m3), RING + ("c",), opposite(1))
    blocks = [far, p3, m3, p2, m2, p1, m1, own]
    x = jnp.concatenate(blocks)
    sign = jnp.where(core == 0, -4, 4)

    both = jnp.where(zh == 0, jnp.stack([token_pos[:, 0], other_pos]), jnp.stack([other_pos, token_pos[:, 0]])).reshape(16, 2, rows)
    at = jnp.stack([(z + d) % 16 for d in (sign, -3, 3, -2, 2, -1, 1, 0)])
    where = jnp.concatenate([lax.dynamic_slice(both, (at[i], core, 0), (1, 1, rows)).reshape(rows) for i in range(8)])

    visible = (frame[None, :] <= where[:, None]) & (frame[None, :] < 1536 - frame_pad[0])
    outs = []
    for w, k, v in ((wq, k_own, v_own), (wq_oth, k_oth, v_oth)):
        q = (jnp.dot(x, w, preferred_element_type=jnp.float32) * HEAD_DIM**-0.5).astype(jnp.bfloat16)
        q = q.reshape(-1, 2, HEAD_DIM)
        k = k.reshape(-1, 2, HEAD_DIM)
        v = v.reshape(-1, 2, HEAD_DIM)
        s = jnp.einsum("rhd,fhd->rhf", q, k, preferred_element_type=jnp.float32)
        s = jnp.where(visible[:, None, :], s, MASKED)
        top = jnp.max(s, axis=-1, keepdims=True)
        e = jnp.where(visible[:, None, :], jnp.exp(s - top), 0.0)
        total = jnp.sum(e, axis=-1)
        a = jnp.einsum("rhf,fhd->rhd", e.astype(jnp.bfloat16), v, preferred_element_type=jnp.float32)
        outs.append((a / total[..., None]).astype(jnp.bfloat16).reshape(-1, 256))
    part = jnp.dot(outs[0], wo, preferred_element_type=jnp.float32) + jnp.dot(
        outs[1], wo_oth, preferred_element_type=jnp.float32
    )
    rfar, r3p, r3m, r2p, r2m, r1p, r1m, mine_out = jnp.split(part, 8)
    bf = lambda v: v.astype(jnp.bfloat16)
    back = lax.ppermute(bf(rfar), RING + ("c",), opposite(-1)).astype(jnp.float32)
    zero = jnp.zeros_like(back)
    ap = down(bf(r3p + jnp.where(core == 0, back, zero)))
    am = up(bf(r3m + jnp.where(core == 0, zero, back)))
    ap, am = down(bf(r2p + ap)), up(bf(r2m + am))
    ap, am = down(bf(r1p + ap)), up(bf(r1m + am))
    out = mine_out + ap.astype(jnp.float32) + am.astype(jnp.float32)
    return out.astype(jnp.bfloat16).reshape(rows, 1, -1)


def solution(mesh):
    fine = Mesh(mesh.devices.reshape(2, 4, 4, 8, 2), ("zh", "y", "x", "zl", "c"))
    frame, tensor = ("zh", "y", "x"), ("zl", "c")
    placed = (
        P(frame + tensor, None, None),
        P(),
        P(None, tensor),
        P(tensor, None),
        P(frame, None, tensor),
        P(frame, None, tensor),
        P(frame, None),
        P(),
    )
    return jax.shard_map(
        per_device,
        mesh=fine,
        in_specs=placed,
        out_specs=P(frame + tensor, None, None),
        check_vma=False,
    )
```

time: 465 us -> 178 us (0.38)
  the two profiles are of different devices: /device:TPU:1 before, /device:TPU:10 now
where the time goes in v1:
time: 178 us; the launch traced here: 177 us
  starting transfers between devices  73 us (41%)
  blocking collectives  41 us (23%)
  waiting for transfers between devices  21.6 us (12%)
  matrix products  18.7 us (11%)
  local copies, waits for them, and re-layouts  13.1 us (7%)
  other arithmetic  8.2 us (5%)
    ppermute x6, starting transfers between devices, down(): return lax.ppermute(x, RING, shift(-1))  34.5 us
    ppermute x6, starting transfers between devices, up(): return lax.ppermute(x, RING, shift(1))  14.8 us
    all_gather x1, blocking collectives, per_device(): v_own = lax.all_gather(kv[:, :, 1], 'y', axis=0).reshape(1536, 256)  14.1 us
    all_gather x1, blocking collectives, per_device(): k_own = lax.all_gather(kv[:, :, 0], 'y', axis=0).reshape(1536, 256)  14 us
    all_gather x1, blocking collectives, per_device(): kv = lax.all_gather(kv, 'x', axis=0)  12.9 us
    ppermute x6, waiting for transfers between devices, up(): return lax.ppermute(x, RING, shift(1))  9.82 us
    ppermute x1, starting transfers between devices, per_device(): theirs = lax.ppermute(mine, 'zh', SWAP)  9.44 us
    ppermute x6, waiting for transfers between devices, down(): return lax.ppermute(x, RING, shift(-1))  6.25 us
  transfers between devices with their start and end apart: 19, of which 6 were waited for; matrix products, arithmetic and copies ran while one was open for 19% of the time, Pallas kernels for 0%

profile of v1, /device:TPU:10, one launch (start us, length us, event | category | flops | bytes accessed | tf_op | source)
XLA Modules:
  0.0 177.0 jit_solution(796738333729940636)
XLA Ops:
  2.2 3.8 %collective-permute-start.1 = (bf16[32,4096]{1,0:T(8,128)(2,1)S(1)}, bf16[32,4096]{1,0:T(8,128)(2,1)S(1)}, u32[]{:S(2)}, u32[]{:S(2)}) collective-permute-start(bf16[32,4096]{1,0:T(8,128)(2,1)S(1)} %fusion.42), channel_id=1, source_target_pairs={{0,2},{2,4},{4,6},{6,8},{8,10},{10,12},{12,14},{14,256},{256,258},... | collective-permute-start | bytes 786440 | tf_op jit(solution)/shard_map/ppermute | solution.py:32
  6.1 9.5 %collective-permute-start.4 = (bf16[32,4096]{1,0:T(8,128)(2,1)S(1)}, bf16[32,4096]{1,0:T(8,128)(2,1)S(1)}, u32[]{:S(2)}, u32[]{:S(2)}) collective-permute-start(bf16[32,4096]{1,0:T(8,128)(2,1)S(1)} %fusion.42), channel_id=1, source_target_pairs={{0,270},{2,0},{4,2},{6,4},{8,6},{10,8},{12,10},{14,12},{256,14},{2... | collective-permute-start | bytes 786440 | tf_op jit(solution)/shard_map/ppermute | solution.py:36
  19.0 9.4 %collective-permute-start = (bf16[104,256]{1,0:T(8,128)(2,1)S(1)}, bf16[104,256]{1,0:T(8,128)(2,1)S(1)}, u32[]{:S(2)}, u32[]{:S(2)}) collective-permute-start(bf16[104,256]{1,0:T(8,128)(2,1)S(1)} %concatenate.14), channel_id=1, source_target_pairs={{0,256},{256,0},{1,257},{257,1},{2,258},{258,2},{3,259},{259,3},{4... | collective-permute-start | bytes 159752 | tf_op jit(solution)/shard_map/ppermute | solution.py:54
  30.4 2.4 %collective-permute-start.11 = (bf16[256,4096]{1,0:T(8,128)(2,1)}, bf16[256,4096]{1,0:T(8,128)(2,1)}, u32[]{:S(2)}, u32[]{:S(2)}) collective-permute-start(bf16[256,4096]{1,0:T(8,128)(2,1)} %param.11), channel_id=1, source_target_pairs={{0,1},{1,0},{2,3},{3,2},{4,5},{5,4},{6,7},{7,6},{8,9},{9,8},{10,11... | collective-permute-start | bytes 6291464 | tf_op jit(solution)/shard_map/ppermute | solution.py:70
  34.5 12.9 %all_gather.9 = bf16[4,2,2,48,256]{4,3,2,1,0:T(8,128)(2,1)S(1)} all-gather(bf16[1,2,2,48,256]{4,3,2,1,0:T(8,128)(2,1)S(1)} %pad_maximum_fusion), channel_id=1, replica_groups=mesh['zh'=2,'y'=4,'x'=4,'zl'=8,'c'=2] {'x'}, dimensions={0}, use_global_device_ids=true | all-gather | bytes 491520 | tf_op jit(solution)/shard_map/all_gather | solution.py:59
  49.5 5.1 %collective-permute-start.5 = (bf16[32,4096]{1,0:T(8,128)(2,1)S(1)}, bf16[32,4096]{1,0:T(8,128)(2,1)}, u32[]{:S(2)}, u32[]{:S(2)}) collective-permute-start(bf16[32,4096]{1,0:T(8,128)(2,1)S(1)} %collective-permute-done.4), channel_id=1, source_target_pairs={{0,270},{2,0},{4,2},{6,4},{8,6},{10,8},{12,10},{14,12},{256,14},{2... | collective-permute-start | bytes 786440 | tf_op jit(solution)/shard_map/ppermute | solution.py:36
  54.6 14.0 %all-gather.1 = bf16[16,2,1,48,256]{4,3,2,1,0:T(8,128)(2,1)S(1)} all-gather(bf16[4,2,1,48,256]{4,3,2,1,0:T(8,128)(2,1)S(1)} %get-tuple-element.9), channel_id=3, replica_groups=mesh['zh'=2,'y'=4,'x'=4,'zl'=8,'c'=2] {'y'}, dimensions={0}, use_global_device_ids=true | all-gather | bytes 983040 | tf_op jit(solution)/shard_map/all_gather | solution.py:60
  72.7 5.1 %collective-permute-start.6 = (bf16[32,4096]{1,0:T(8,128)(2,1)}, bf16[32,4096]{1,0:T(8,128)(2,1)S(1)}, u32[]{:S(2)}, u32[]{:S(2)}) collective-permute-start(bf16[32,4096]{1,0:T(8,128)(2,1)} %collective-permute-done.5), channel_id=1, source_target_pairs={{0,270},{2,0},{4,2},{6,4},{8,6},{10,8},{12,10},{14,12},{256,14},{2... | collective-permute-start | bytes 786440 | tf_op jit(solution)/shard_map/ppermute | solution.py:36
  77.9 14.1 %all-gather = bf16[16,2,1,48,256]{4,3,2,1,0:T(8,128)(2,1)S(1)} all-gather(bf16[4,2,1,48,256]{4,3,2,1,0:T(8,128)(2,1)S(1)} %get-tuple-element.10), channel_id=2, replica_groups=mesh['zh'=2,'y'=4,'x'=4,'zl'=8,'c'=2] {'y'}, dimensions={0}, use_global_device_ids=true | all-gather | bytes 983040 | tf_op jit(solution)/shard_map/all_gather | solution.py:61
  101.9 2.4 %copy.37 = bf16[1536,256]{0,1:T(8,128)(2,1)} copy(bf16[1536,256]{1,0:T(8,128)(2,1)} %collective-permute-done.8) | data formatting | bytes 1572864 | tf_op jit(solution)/shard_map/ppermute | solution.py:63
  113.1 2.8 %fusion.31 = bf16[256,2,128]{0,2,1:T(8,128)(2,1)S(1)} fusion(bf16[1536,2,128]{2,1,0:T(2,128)(2,1)} %reshape_reshape.6, pred[256,1536]{0,1:T(8,128)(4,1)S(1)} %copy-done.4, bf16[256,2,128]{0,2,1:T(8,128)(2,1)S(1)} %bitcast.113, bf16[1536,2,128]{2,1,0:T(2,128)(2,1)S(1)} %reshape_reshape.7, f32[256,2]{0,1:T(2,128)S(1)} %fusion.95), kind=kOutput, calls=%fused_computation.27 | convolution fusion | flops 405932032 | bytes 2230272 | tf_op jit(solution)/shard_map/rhf,fhd->rhd/dot_general | solution.py:97
  115.8 4.3 %fusion.99 = f32[256,4096]{1,0:T(8,128)} fusion(bf16[256,256]{0,1:T(8,128)(2,1)S(1)} %bitcast.111, bf16[256,4096]{1,0:T(8,128)(2,1)} %param.11), kind=kOutput, calls=%fused_computation.131 | convolution fusion | flops 536870912 | bytes 6422528 | tf_op jit(solution)/shard_map/dot_general | solution.py:99
  120.1 2.6 %fusion.27 = bf16[256,256]{0,1:T(8,128)(2,1)S(1)} fusion(bf16[256,4096]{1,0:T(8,128)(2,1)S(1)} %constant_dynamic-update-slice_fusion, bf16[4096,256]{1,0:T(8,128)(2,1)} %collective-permute-done.10), kind=kOutput, calls=%fused_computation.25 | convolution fusion | flops 537001984 | bytes 4325376 | tf_op jit(solution)/shard_map/dot_general | solution.py:88
  125.9 3.6 %convolution_add_fusion = f32[256,4096]{1,0:T(8,128)S(1)} fusion(f32[256,4096]{1,0:T(8,128)} %fusion.99, bf16[256,256]{0,1:T(8,128)(2,1)S(1)} %bitcast.114, bf16[256,4096]{1,0:T(8,128)(2,1)} %collective-permute-done.11), kind=kOutput, calls=%fused_computation.2 | convolution fusion | flops 537919488 | bytes 10616832 | tf_op jit(solution)/shard_map/dot_general | solution.py:99
  129.5 4.0 %collective-permute-start.12 = (bf16[32,4096]{1,0:T(8,128)(2,1)S(1)}, bf16[32,4096]{1,0:T(8,128)(2,1)S(1)}, u32[]{:S(2)}, u32[]{:S(2)}) collective-permute-start(bf16[32,4096]{1,0:T(8,128)(2,1)S(1)} %split.63), channel_id=1, source_target_pairs={{0,270},{1,3},{2,0},{3,5},{4,2},{5,7},{6,4},{7,9},{8,6},{9,11},{10... | collective-permute-start | bytes 786440 | tf_op jit(solution)/shard_map/ppermute | solution.py:104
  133.6 4.2 %collective-permute-done.12 = bf16[32,4096]{1,0:T(8,128)(2,1)S(1)} collective-permute-done((bf16[32,4096]{1,0:T(8,128)(2,1)S(1)}, bf16[32,4096]{1,0:T(8,128)(2,1)S(1)}, u32[]{:S(2)}, u32[]{:S(2)}) %collective-permute-start.12) | collective-permute-done | bytes 262176 | tf_op jit(solution)/shard_map/ppermute | solution.py:104
  137.9 5.2 %collective-permute-start.13 = (bf16[32,4096]{1,0:T(8,128)(2,1)S(1)}, bf16[32,4096]{1,0:T(8,128)(2,1)S(1)}, u32[]{:S(2)}, u32[]{:S(2)}) collective-permute-start(bf16[32,4096]{1,0:T(8,128)(2,1)S(1)} %get-tuple-element.5), channel_id=1, source_target_pairs={{0,270},{2,0},{4,2},{6,4},{8,6},{10,8},{12,10},{14,12},{256,14},{2... | collective-permute-start | bytes 786440 | tf_op jit(solution)/shard_map/ppermute | solution.py:36
  145.1 2.4 %collective-permute-done.13 = bf16[32,4096]{1,0:T(8,128)(2,1)S(1)} collective-permute-done((bf16[32,4096]{1,0:T(8,128)(2,1)S(1)}, bf16[32,4096]{1,0:T(8,128)(2,1)S(1)}, u32[]{:S(2)}, u32[]{:S(2)}) %collective-permute-start.13) | collective-permute-done | bytes 262176 | tf_op jit(solution)/shard_map/ppermute | solution.py:36
  147.6 5.2 %collective-permute-start.14 = (bf16[32,4096]{1,0:T(8,128)(2,1)S(1)}, bf16[32,4096]{1,0:T(8,128)(2,1)S(1)}, u32[]{:S(2)}, u32[]{:S(2)}) collective-permute-start(bf16[32,4096]{1,0:T(8,128)(2,1)S(1)} %fusion.45), channel_id=1, source_target_pairs={{0,270},{2,0},{4,2},{6,4},{8,6},{10,8},{12,10},{14,12},{256,14},{2... | collective-permute-start | bytes 786440 | tf_op jit(solution)/shard_map/ppermute | solution.py:36
  152.7 3.9 %collective-permute-done.14 = bf16[32,4096]{1,0:T(8,128)(2,1)S(1)} collective-permute-done((bf16[32,4096]{1,0:T(8,128)(2,1)S(1)}, bf16[32,4096]{1,0:T(8,128)(2,1)S(1)}, u32[]{:S(2)}, u32[]{:S(2)}) %collective-permute-start.14) | collective-permute-done | bytes 262176 | tf_op jit(solution)/shard_map/ppermute | solution.py:36
  156.7 3.2 %collective-permute-start.17 = (bf16[32,4096]{1,0:T(8,128)(2,1)S(1)}, bf16[32,4096]{1,0:T(8,128)(2,1)S(1)}, u32[]{:S(2)}, u32[]{:S(2)}) collective-permute-start(bf16[32,4096]{1,0:T(8,128)(2,1)S(1)} %get-tuple-element.8), channel_id=1, source_target_pairs={{0,2},{2,4},{4,6},{6,8},{8,10},{10,12},{12,14},{14,256},{256,258},... | collective-permute-start | bytes 786440 | tf_op jit(solution)/shard_map/ppermute | solution.py:32
  159.9 4.4 %collective-permute-start.15 = (bf16[32,4096]{1,0:T(8,128)(2,1)S(1)}, bf16[32,4096]{1,0:T(8,128)(2,1)S(1)}, u32[]{:S(2)}, u32[]{:S(2)}) collective-permute-start(bf16[32,4096]{1,0:T(8,128)(2,1)S(1)} %get-tuple-element.7), channel_id=1, source_target_pairs={{0,270},{2,0},{4,2},{6,4},{8,6},{10,8},{12,10},{14,12},{256,14},{2... | collective-permute-start | bytes 786440 | tf_op jit(solution)/shard_map/ppermute | solution.py:36
  164.2 2.4 %collective-permute-done.17 = bf16[32,4096]{1,0:T(8,128)(2,1)S(1)} collective-permute-done((bf16[32,4096]{1,0:T(8,128)(2,1)S(1)}, bf16[32,4096]{1,0:T(8,128)(2,1)S(1)}, u32[]{:S(2)}, u32[]{:S(2)}) %collective-permute-start.17) | collective-permute-done | bytes 262176 | tf_op jit(solution)/shard_map/ppermute | solution.py:32
  168.8 7.4 %collective-permute-done.18 = bf16[32,4096]{1,0:T(8,128)(2,1)S(1)} collective-permute-done((bf16[32,4096]{1,0:T(8,128)(2,1)S(1)}, bf16[32,4096]{1,0:T(8,128)(2,1)S(1)}, u32[]{:S(2)}, u32[]{:S(2)}) %collective-permute-start.18) | collective-permute-done | bytes 262176 | tf_op jit(solution)/shard_map/ppermute | solution.py:32
  (88 shorter events, 41.5 us)
Async XLA Ops:
  0.0 47.4 %copy-start.10 = (s32[512,1]{0,1:T(1,128)S(1)}, s32[512,1]{0,1:T(1,128)}, u32[]{:S(2)}) copy-start(s32[512,1]{0,1:T(1,128)} %param.14) | copy-start | bytes 6148
  2.2 45.3 %collective-permute-start.1 = (bf16[32,4096]{1,0:T(8,128)(2,1)S(1)}, bf16[32,4096]{1,0:T(8,128)(2,1)S(1)}, u32[]{:S(2)}, u32[]{:S(2)}) collective-permute-start(bf16[32,4096]{1,0:T(8,128)(2,1)S(1)} %fusion.42), channel_id=1, source_target_pairs={{0,2},{2,4},{4,6},{6,8},{8,10},{10,12},{12,14},{14,256},{256,258},... | collective-permute-start | bytes 786440 | tf_op jit(solution)/shard_map/ppermute | solution.py:32
  6.1 43.4 %collective-permute-start.4 = (bf16[32,4096]{1,0:T(8,128)(2,1)S(1)}, bf16[32,4096]{1,0:T(8,128)(2,1)S(1)}, u32[]{:S(2)}, u32[]{:S(2)}) collective-permute-start(bf16[32,4096]{1,0:T(8,128)(2,1)S(1)} %fusion.42), channel_id=1, source_target_pairs={{0,270},{2,0},{4,2},{6,4},{8,6},{10,8},{12,10},{14,12},{256,14},{2... | collective-permute-start | bytes 786440 | tf_op jit(solution)/shard_map/ppermute | solution.py:36
  19.0 15.4 %collective-permute-start = (bf16[104,256]{1,0:T(8,128)(2,1)S(1)}, bf16[104,256]{1,0:T(8,128)(2,1)S(1)}, u32[]{:S(2)}, u32[]{:S(2)}) collective-permute-start(bf16[104,256]{1,0:T(8,128)(2,1)S(1)} %concatenate.14), channel_id=1, source_target_pairs={{0,256},{256,0},{1,257},{257,1},{2,258},{258,2},{3,259},{259,3},{4... | collective-permute-start | bytes 159752 | tf_op jit(solution)/shard_map/ppermute | solution.py:54
  28.4 91.7 %collective-permute-start.10 = (bf16[4096,256]{1,0:T(8,128)(2,1)}, bf16[4096,256]{1,0:T(8,128)(2,1)}, u32[]{:S(2)}, u32[]{:S(2)}) collective-permute-start(bf16[4096,256]{1,0:T(8,128)(2,1)} %param.10), channel_id=1, source_target_pairs={{0,1},{1,0},{2,3},{3,2},{4,5},{5,4},{6,7},{7,6},{8,9},{9,8},{10,11... | collective-permute-start | bytes 6291464 | tf_op jit(solution)/shard_map/ppermute | solution.py:69
  30.4 95.6 %collective-permute-start.11 = (bf16[256,4096]{1,0:T(8,128)(2,1)}, bf16[256,4096]{1,0:T(8,128)(2,1)}, u32[]{:S(2)}, u32[]{:S(2)}) collective-permute-start(bf16[256,4096]{1,0:T(8,128)(2,1)} %param.11), channel_id=1, source_target_pairs={{0,1},{1,0},{2,3},{3,2},{4,5},{5,4},{6,7},{7,6},{8,9},{9,8},{10,11... | collective-permute-start | bytes 6291464 | tf_op jit(solution)/shard_map/ppermute | solution.py:70
  47.5 30.3 %copy-start.6 = (bf16[32,4096]{1,0:T(8,128)(2,1)}, bf16[32,4096]{1,0:T(8,128)(2,1)S(1)}, u32[]{:S(2)}) copy-start(bf16[32,4096]{1,0:T(8,128)(2,1)S(1)} %collective-permute-done.1) | copy-start | bytes 786436
  47.6 23.2 %collective-permute-start.2 = (bf16[32,4096]{1,0:T(8,128)(2,1)S(1)}, bf16[32,4096]{1,0:T(8,128)(2,1)S(1)}, u32[]{:S(2)}, u32[]{:S(2)}) collective-permute-start(bf16[32,4096]{1,0:T(8,128)(2,1)S(1)} %collective-permute-done.1), channel_id=1, source_target_pairs={{0,2},{2,4},{4,6},{6,8},{8,10},{10,12},{12,14},{14,256},{256,258},... | collective-permute-start | bytes 786440 | tf_op jit(solution)/shard_map/ppermute | solution.py:32
  49.5 23.2 %copy-start.7 = (bf16[32,4096]{1,0:T(8,128)(2,1)}, bf16[32,4096]{1,0:T(8,128)(2,1)S(1)}, u32[]{:S(2)}) copy-start(bf16[32,4096]{1,0:T(8,128)(2,1)S(1)} %collective-permute-done.4) | copy-start | bytes 786436
  49.5 23.2 %collective-permute-start.5 = (bf16[32,4096]{1,0:T(8,128)(2,1)S(1)}, bf16[32,4096]{1,0:T(8,128)(2,1)}, u32[]{:S(2)}, u32[]{:S(2)}) collective-permute-start(bf16[32,4096]{1,0:T(8,128)(2,1)S(1)} %collective-permute-done.4), channel_id=1, source_target_pairs={{0,270},{2,0},{4,2},{6,4},{8,6},{10,8},{12,10},{14,12},{256,14},{2... | collective-permute-start | bytes 786440 | tf_op jit(solution)/shard_map/ppermute | solution.py:36
  68.8 30.8 %collective-permute-start.9 = (bf16[1536,256]{1,0:T(8,128)(2,1)S(1)}, bf16[1536,256]{1,0:T(8,128)(2,1)}, u32[]{:S(2)}, u32[]{:S(2)}) collective-permute-start(bf16[1536,256]{1,0:T(8,128)(2,1)S(1)} %bitcast.102), channel_id=1, source_target_pairs={{0,1},{1,0},{2,3},{3,2},{4,5},{5,4},{6,7},{7,6},{8,9},{9,8},{10,11... | collective-permute-start | bytes 2359304 | tf_op jit(solution)/shard_map/ppermute | solution.py:62
  70.8 31.2 %copy-start.8 = (bf16[32,4096]{1,0:T(8,128)(2,1)}, bf16[32,4096]{1,0:T(8,128)(2,1)S(1)}, u32[]{:S(2)}) copy-start(bf16[32,4096]{1,0:T(8,128)(2,1)S(1)} %collective-permute-done.2) | copy-start | bytes 786436
  70.8 22.3 %collective-permute-start.3 = (bf16[32,4096]{1,0:T(8,128)(2,1)S(1)}, bf16[32,4096]{1,0:T(8,128)(2,1)S(1)}, u32[]{:S(2)}, u32[]{:S(2)}) collective-permute-start(bf16[32,4096]{1,0:T(8,128)(2,1)S(1)} %collective-permute-done.2), channel_id=1, source_target_pairs={{0,2},{2,4},{4,6},{6,8},{8,10},{10,12},{12,14},{14,256},{256,258},... | collective-permute-start | bytes 786440 | tf_op jit(solution)/shard_map/ppermute | solution.py:32
  72.7 22.3 %collective-permute-start.6 = (bf16[32,4096]{1,0:T(8,128)(2,1)}, bf16[32,4096]{1,0:T(8,128)(2,1)S(1)}, u32[]{:S(2)}, u32[]{:S(2)}) collective-permute-start(bf16[32,4096]{1,0:T(8,128)(2,1)} %collective-permute-done.5), channel_id=1, source_target_pairs={{0,270},{2,0},{4,2},{6,4},{8,6},{10,8},{12,10},{14,12},{256,14},{2... | collective-permute-start | bytes 786440 | tf_op jit(solution)/shard_map/ppermute | solution.py:36
  93.1 8.8 %collective-permute-start.8 = (bf16[1536,256]{1,0:T(8,128)(2,1)S(1)}, bf16[1536,256]{1,0:T(8,128)(2,1)}, u32[]{:S(2)}, u32[]{:S(2)}) collective-permute-start(bf16[1536,256]{1,0:T(8,128)(2,1)S(1)} %bitcast.103), channel_id=1, source_target_pairs={{0,1},{1,0},{2,3},{3,2},{4,5},{5,4},{6,7},{7,6},{8,9},{9,8},{10,11... | collective-permute-start | bytes 2359304 | tf_op jit(solution)/shard_map/ppermute | solution.py:63
  95.8 9.8 %collective-permute-start.7 = (bf16[32,4096]{1,0:T(8,128)(2,1)}, bf16[32,4096]{1,0:T(8,128)(2,1)}, u32[]{:S(2)}, u32[]{:S(2)}) collective-permute-start(bf16[32,4096]{1,0:T(8,128)(2,1)} %broadcast_select_fusion), channel_id=1, source_target_pairs={{0,2},{1,271},{2,4},{3,1},{4,6},{5,3},{6,8},{7,5},{8,10},{9,7},{10... | collective-permute-start | bytes 786440 | tf_op jit(solution)/shard_map/ppermute | solution.py:76
  104.3 6.3 %copy-start.1 = (bf16[4096,256]{1,0:T(8,128)(2,1)S(1)}, bf16[4096,256]{1,0:T(8,128)(2,1)}, u32[]{:S(2)}) copy-start(bf16[4096,256]{1,0:T(8,128)(2,1)} %param.10) | copy-start | bytes 6291460
  129.5 8.3 %collective-permute-start.12 = (bf16[32,4096]{1,0:T(8,128)(2,1)S(1)}, bf16[32,4096]{1,0:T(8,128)(2,1)S(1)}, u32[]{:S(2)}, u32[]{:S(2)}) collective-permute-start(bf16[32,4096]{1,0:T(8,128)(2,1)S(1)} %split.63), channel_id=1, source_target_pairs={{0,270},{1,3},{2,0},{3,5},{4,2},{5,7},{6,4},{7,9},{8,6},{9,11},{10... | collective-permute-start | bytes 786440 | tf_op jit(solution)/shard_map/ppermute | solution.py:104
  137.9 9.6 %collective-permute-start.13 = (bf16[32,4096]{1,0:T(8,128)(2,1)S(1)}, bf16[32,4096]{1,0:T(8,128)(2,1)S(1)}, u32[]{:S(2)}, u32[]{:S(2)}) collective-permute-start(bf16[32,4096]{1,0:T(8,128)(2,1)S(1)} %get-tuple-element.5), channel_id=1, source_target_pairs={{0,270},{2,0},{4,2},{6,4},{8,6},{10,8},{12,10},{14,12},{256,14},{2... | collective-permute-start | bytes 786440 | tf_op jit(solution)/shard_map/ppermute | solution.py:36
  143.2 9.5 %collective-permute-start.16 = (bf16[32,4096]{1,0:T(8,128)(2,1)S(1)}, bf16[32,4096]{1,0:T(8,128)(2,1)S(1)}, u32[]{:S(2)}, u32[]{:S(2)}) collective-permute-start(bf16[32,4096]{1,0:T(8,128)(2,1)S(1)} %get-tuple-element.6), channel_id=1, source_target_pairs={{0,2},{2,4},{4,6},{6,8},{8,10},{10,12},{12,14},{14,256},{256,258},... | collective-permute-start | bytes 786440 | tf_op jit(solution)/shard_map/ppermute | solution.py:32
  147.6 9.0 %collective-permute-start.14 = (bf16[32,4096]{1,0:T(8,128)(2,1)S(1)}, bf16[32,4096]{1,0:T(8,128)(2,1)S(1)}, u32[]{:S(2)}, u32[]{:S(2)}) collective-permute-start(bf16[32,4096]{1,0:T(8,128)(2,1)S(1)} %fusion.45), channel_id=1, source_target_pairs={{0,270},{2,0},{4,2},{6,4},{8,6},{10,8},{12,10},{14,12},{256,14},{2... | collective-permute-start | bytes 786440 | tf_op jit(solution)/shard_map/ppermute | solution.py:36
  156.7 9.9 %collective-permute-start.17 = (bf16[32,4096]{1,0:T(8,128)(2,1)S(1)}, bf16[32,4096]{1,0:T(8,128)(2,1)S(1)}, u32[]{:S(2)}, u32[]{:S(2)}) collective-permute-start(bf16[32,4096]{1,0:T(8,128)(2,1)S(1)} %get-tuple-element.8), channel_id=1, source_target_pairs={{0,2},{2,4},{4,6},{6,8},{8,10},{10,12},{12,14},{14,256},{256,258},... | collective-permute-start | bytes 786440 | tf_op jit(solution)/shard_map/ppermute | solution.py:32
  159.9 8.9 %collective-permute-start.15 = (bf16[32,4096]{1,0:T(8,128)(2,1)S(1)}, bf16[32,4096]{1,0:T(8,128)(2,1)S(1)}, u32[]{:S(2)}, u32[]{:S(2)}) collective-permute-start(bf16[32,4096]{1,0:T(8,128)(2,1)S(1)} %get-tuple-element.7), channel_id=1, source_target_pairs={{0,270},{2,0},{4,2},{6,4},{8,6},{10,8},{12,10},{14,12},{256,14},{2... | collective-permute-start | bytes 786440 | tf_op jit(solution)/shard_map/ppermute | solution.py:36
  166.7 9.5 %collective-permute-start.18 = (bf16[32,4096]{1,0:T(8,128)(2,1)S(1)}, bf16[32,4096]{1,0:T(8,128)(2,1)S(1)}, u32[]{:S(2)}, u32[]{:S(2)}) collective-permute-start(bf16[32,4096]{1,0:T(8,128)(2,1)S(1)} %fusion.44), channel_id=1, source_target_pairs={{0,2},{2,4},{4,6},{6,8},{8,10},{10,12},{12,14},{14,256},{256,258},... | collective-permute-start | bytes 786440 | tf_op jit(solution)/shard_map/ppermute | solution.py:32
  (6 other events, 20.2 us)

commit v2 on v1

v2 whole, which is shorter than its diff:
```python
import functools

import jax
import jax.numpy as jnp
from jax import lax
from jax.experimental import pallas as pl
from jax.experimental.pallas import tpu as pltpu
from jax.sharding import Mesh, PartitionSpec as P

HEAD_DIM = 128
EPSILON = 1e-06
MASKED = -1e30
RING = ("zh", "zl")
SWAP = [(0, 1), (1, 0)]
TURNS = (0, 1, 3, 2)
VMEM = pl.BlockSpec(memory_space=pltpu.VMEM)


def shift(step, size=16):
    return [(i, (i + step) % size) for i in range(size)]


def opposite(step):
    return [
        (2 * i + c, 2 * ((i + (step if c == 0 else -step)) % 16) + c)
        for i in range(16)
        for c in range(2)
    ]


def up(x):
    return lax.ppermute(x, RING, shift(1))


def down(x):
    return lax.ppermute(x, RING, shift(-1))


def prepare_kernel(tokens, gain, keys, values, pos, normed, payload):
    hidden = tokens[...].astype(jnp.float32)
    factor = lax.rsqrt(jnp.mean(hidden * hidden, axis=-1, keepdims=True) + EPSILON)
    normed[...] = (hidden * factor * gain[...]).astype(jnp.bfloat16)
    payload[0:48, :] = keys[...]
    payload[48:96, :] = values[...]
    high = lax.shift_right_logical(pos[...], 3)
    low = pos[...] - high * 8
    parts = [high[:, :256], high[:, 256:], low[:, :256], low[:, 256:]]
    parts = jnp.concatenate(parts + [jnp.zeros((12, 256), jnp.int32)], axis=0)
    payload[96:112, :] = parts.astype(jnp.float32).astype(jnp.bfloat16)


def attend_kernel(count, first, *refs):
    blocks = refs[:count]
    wq, wo, kv, bound, frame, out = (
        refs[count : count + 2],
        refs[count + 2 : count + 4],
        refs[count + 4 : count + 6],
        refs[count + 6],
        refs[count + 7],
        refs[count + 8],
    )
    rows = out.shape[0]
    x = jnp.concatenate([b[...] for b in blocks], axis=0)
    column = jnp.transpose(jnp.broadcast_to(bound[...].astype(jnp.float32), (8, 256)))
    column = column[first : first + rows, 0:1]
    bias = jnp.where(frame[...].astype(jnp.float32) <= column, 0.0, MASKED)
    groups = []
    for g in range(2):
        q = jnp.dot(x, wq[g][...], preferred_element_type=jnp.float32)
        q = (q * HEAD_DIM**-0.5).astype(jnp.bfloat16)
        heads = []
        for h in range(2):
            cols = slice(h * HEAD_DIM, (h + 1) * HEAD_DIM)
            s = [
                lax.dot_general(
                    q[:, cols],
                    kv[g][t, 0, :, cols],
                    (((1,), (1,)), ((), ())),
                    preferred_element_type=jnp.float32,
                )
                for t in range(4)
            ]
            s = jnp.concatenate(s, axis=1) + bias
            e = jnp.exp(s - jnp.max(s, axis=1, keepdims=True))
            total = jnp.sum(e, axis=1, keepdims=True)
            e = e.astype(jnp.bfloat16)
            a = sum(
                jnp.dot(
                    e[:, t * 384 : (t + 1) * 384],
                    kv[g][t, 1, :, cols],
                    preferred_element_type=jnp.float32,
                )
                for t in range(4)
            )
            heads.append((a / total).astype(jnp.bfloat16))
        groups.append(jnp.concatenate(heads, axis=1))
    for n in range(0, 4096, 1024):
        cols = slice(n, n + 1024)
        total = jnp.dot(groups[0], wo[0][:, cols], preferred_element_type=jnp.float32)
        total += jnp.dot(groups[1], wo[1][:, cols], preferred_element_type=jnp.float32)
        out[:, cols] = total.astype(jnp.bfloat16)


def attend(blocks, first, wq, wo, kv, bound, frame):
    count = len(blocks)
    rows = 32 * count
    return pl.pallas_call(
        functools.partial(attend_kernel, count, first),
        out_shape=jax.ShapeDtypeStruct((rows, 4096), jnp.bfloat16),
        in_specs=[VMEM] * (count + 8),
        out_specs=VMEM,
        compiler_params=pltpu.CompilerParams(vmem_limit_bytes=40 * 2**20),
        cost_estimate=pl.CostEstimate(
            flops=rows * 12 * 2**20, bytes_accessed=12 * 2**20, transcendentals=rows * 6144
        ),
        name="attend%d" % count,
    )(*blocks, *wq, *wo, *kv, bound, frame)


def per_device(tokens, gain, wq, wo, keys, values, token_pos, frame_pad):
    rows = tokens.shape[0]
    zh, y, x, zl, core = (lax.axis_index(a) for a in ("zh", "y", "x", "zl", "c"))
    z = zh * 8 + zl
    pos = token_pos.T
    own, mine = pl.pallas_call(
        prepare_kernel,
        out_shape=(
            jax.ShapeDtypeStruct((rows, 4096), jnp.bfloat16),
            jax.ShapeDtypeStruct((112, 256), jnp.bfloat16),
        ),
        in_specs=[VMEM] * 5,
        out_specs=(VMEM, VMEM),
        name="prepare",
    )(tokens.reshape(rows, 4096), gain.reshape(1, 4096), keys.reshape(48, 256), values.reshape(48, 256), pos)

    p1, m1 = up(own), down(own)
    p2, m2 = up(p1), down(m1)
    p3, m3 = up(p2), down(m2)
    far = lax.ppermute(jnp.where(core == 0, p3, m3), RING + ("c",), opposite(1))

    theirs = lax.ppermute(mine, "zh", SWAP)
    kv = jnp.stack([mine[:96].reshape(2, 48, 256), theirs[:96].reshape(2, 48, 256)], axis=1)
    kv = jnp.stack([kv] + [lax.ppermute(kv, "x", shift(s, 4)) for s in TURNS[1:]], axis=1)
    kv = kv.reshape(2, 384, 256)
    kv = jnp.stack([kv] + [lax.ppermute(kv, "y", shift(s, 4)) for s in TURNS[1:]])
    kv_other = lax.ppermute(kv, "c", SWAP)
    wq_other = lax.ppermute(wq, "c", SWAP)
    wo_other = lax.ppermute(wo, "c", SWAP)

    turns = jnp.array(TURNS, jnp.int32)
    ys, xs, halves = (y - turns) % 4, (x - turns) % 4, jnp.array([0, 1], jnp.int32) ^ zh
    place = halves[None, None, :] * 16 + ys[:, None, None] * 4 + xs[None, :, None]
    frame = (place[..., None] * 48 + jnp.arange(48, dtype=jnp.int32)).reshape(1, 1536)

    other = theirs[96:98].astype(jnp.int32) * 8 + theirs[98:100].astype(jnp.int32)
    other = other.reshape(1, 512)
    both = jnp.where(zh == 0, jnp.concatenate([pos, other]), jnp.concatenate([other, pos]))
    both = both.reshape(16, 2, rows)
    steps = (jnp.where(core == 0, -4, 4), -3, 3, -2, 2, -1, 1, 0)
    bound = jnp.concatenate(
        [lax.dynamic_slice(both, ((z + d) % 16, core, 0), (1, 1, rows)).reshape(1, rows) for d in steps],
        axis=1,
    )
    bound = jnp.minimum(bound, 1535 - frame_pad[0])

    given = ((wq, wq_other), (wo, wo_other), (kv, kv_other), bound, frame)
    part = attend([far, p3, m3], 0, *given)
    near = attend([p2, m2, p1, m1, own], 96, *given)
    wide = lambda v: v.astype(jnp.float32)
    thin = lambda v: v.astype(jnp.bfloat16)
    back = wide(lax.ppermute(part[:32], RING + ("c",), opposite(-1)))
    zero = jnp.zeros_like(back)
    ap = down(thin(wide(part[32:64]) + jnp.where(core == 0, back, zero)))
    am = up(thin(wide(part[64:96]) + jnp.where(core == 0, zero, back)))
    ap, am = down(thin(wide(near[:32]) + wide(ap))), up(thin(wide(near[32:64]) + wide(am)))
    ap, am = down(thin(wide(near[64:96]) + wide(ap))), up(thin(wide(near[96:128]) + wide(am)))
    out = wide(near[128:160]) + wide(ap) + wide(am)
    return thin(out).reshape(rows, 1, 4096)


def solution(mesh):
    fine = Mesh(mesh.devices.reshape(2, 4, 4, 8, 2), ("zh", "y", "x", "zl", "c"))
    frame, tensor = ("zh", "y", "x"), ("zl", "c")
    placed = (
        P(frame + tensor, None, None),
        P(),
        P(None, tensor),
        P(tensor, None),
        P(frame, None, tensor),
        P(frame, None, tensor),
        P(frame, None),
        P(),
    )
    return jax.shard_map(
        per_device,
        mesh=fine,
        in_specs=placed,
        out_specs=P(frame + tensor, None, None),
        check_vma=False,
    )
```

time: 178 us -> 165 us (0.927)
  the two profiles are of different devices: /device:TPU:10 before, /device:TPU:24 now
where the time goes in v2:
time: 165 us; the launch traced here: 164 us
  starting transfers between devices  89.9 us (54%)
  waiting for transfers between devices  48.9 us (30%)
  Pallas kernels  16.6 us (10%)
  local copies, waits for them, and re-layouts  4.35 us (3%)
  other arithmetic  3.12 us (2%)
    ppermute x6, starting transfers between devices, down(): return lax.ppermute(x, RING, shift(-1))  33.7 us
    ppermute x6, waiting for transfers between devices, up(): return lax.ppermute(x, RING, shift(1))  15.1 us
    ppermute x6, starting transfers between devices, up(): return lax.ppermute(x, RING, shift(1))  14.8 us
    pallas_call x2, Pallas kernels, attend(): pl.pallas_call(functools.partial(attend_kernel, count, first), out_shape=...  14.7 us
    ppermute x3, waiting for transfers between devices, per_device(): lax.ppermute(kv, 'y', shift(s, 4))  13.3 us
    ppermute x3, starting transfers between devices, per_device(): lax.ppermute(kv, 'x', shift(s, 4))  10.8 us
    ppermute x1, starting transfers between devices, per_device(): theirs = lax.ppermute(mine, 'zh', SWAP)  9.45 us
    ppermute x3, starting transfers between devices, per_device(): lax.ppermute(kv, 'y', shift(s, 4))  8.99 us
  transfers between devices with their start and end apart: 24, of which 10 were waited for; matrix products, arithmetic and copies ran while one was open for 2% of the time, Pallas kernels for 5%

profile of v2, /device:TPU:24, one launch (start us, length us, event | category | flops | bytes accessed | tf_op | source)
XLA Modules:
  0.0 164.2 jit_solution(15542966629603435089)
XLA Ops:
  1.9 3.8 %collective-permute-start = (bf16[32,4096]{1,0:T(8,128)(2,1)}, bf16[32,4096]{1,0:T(8,128)(2,1)S(1)}, u32[]{:S(2)}, u32[]{:S(2)}) collective-permute-start(bf16[32,4096]{1,0:T(8,128)(2,1)} %get-tuple-element.7.refs_4_), channel_id=1, source_target_pairs={{0,2},{2,4},{4,6},{6,8},{8,10},{10,12},{12,14},{14,256},{256,258},... | collective-permute-start | bytes 786440 | tf_op jit(solution)/shard_map/ppermute | solution.py:32
  5.7 9.5 %collective-permute-start.2 = (bf16[32,4096]{1,0:T(8,128)(2,1)}, bf16[32,4096]{1,0:T(8,128)(2,1)S(1)}, u32[]{:S(2)}, u32[]{:S(2)}) collective-permute-start(bf16[32,4096]{1,0:T(8,128)(2,1)} %get-tuple-element.7.refs_4_), channel_id=1, source_target_pairs={{0,270},{2,0},{4,2},{6,4},{8,6},{10,8},{12,10},{14,12},{256,14},{2... | collective-permute-start | bytes 786440 | tf_op jit(solution)/shard_map/ppermute | solution.py:36
  15.2 9.5 %collective-permute-start.6 = (bf16[112,256]{1,0:T(8,128)(2,1)}, bf16[112,256]{1,0:T(8,128)(2,1)S(1)}, u32[]{:S(2)}, u32[]{:S(2)}) collective-permute-start(bf16[112,256]{1,0:T(8,128)(2,1)} %get-tuple-element.8), channel_id=1, source_target_pairs={{0,256},{256,0},{1,257},{257,1},{2,258},{258,2},{3,259},{259,3},{4... | collective-permute-start | bytes 172040 | tf_op jit(solution)/shard_map/ppermute | solution.py:141
  26.1 4.7 %collective-permute-done.6 = bf16[112,256]{1,0:T(8,128)(2,1)S(1)} collective-permute-done((bf16[112,256]{1,0:T(8,128)(2,1)}, bf16[112,256]{1,0:T(8,128)(2,1)S(1)}, u32[]{:S(2)}, u32[]{:S(2)}) %collective-permute-start.6) | collective-permute-done | bytes 57376 | tf_op jit(solution)/shard_map/ppermute | solution.py:141
  30.8 3.4 %collective-permute-start.7 = (bf16[2,2,48,256]{3,2,1,0:T(8,128)(2,1)S(1)}, bf16[2,2,48,256]{3,2,1,0:T(8,128)(2,1)S(1)}, u32[]{:S(2)}, u32[]{:S(2)}) collective-permute-start(bf16[2,2,48,256]{3,2,1,0:T(8,128)(2,1)S(1)} %get-tuple-element.14), channel_id=1, source_target_pairs={{0,16},{16,32},{32,48},{48,0},{1,17},{17,33},{33,49},{49,1},{2,18}... | collective-permute-start | bytes 294920 | tf_op jit(solution)/shard_map/ppermute | solution.py:143
  34.2 3.7 %collective-permute-start.8 = (bf16[2,2,48,256]{3,2,1,0:T(8,128)(2,1)S(1)}, bf16[2,2,48,256]{3,2,1,0:T(8,128)(2,1)S(1)}, u32[]{:S(2)}, u32[]{:S(2)}) collective-permute-start(bf16[2,2,48,256]{3,2,1,0:T(8,128)(2,1)S(1)} %get-tuple-element.14), channel_id=1, source_target_pairs={{0,48},{16,0},{32,16},{48,32},{1,49},{17,1},{33,17},{49,33},{2,50}... | collective-permute-start | bytes 294920 | tf_op jit(solution)/shard_map/ppermute | solution.py:143
  37.9 3.7 %collective-permute-start.9 = (bf16[2,2,48,256]{3,2,1,0:T(8,128)(2,1)S(1)}, bf16[2,2,48,256]{3,2,1,0:T(8,128)(2,1)S(1)}, u32[]{:S(2)}, u32[]{:S(2)}) collective-permute-start(bf16[2,2,48,256]{3,2,1,0:T(8,128)(2,1)S(1)} %get-tuple-element.14), channel_id=1, source_target_pairs={{0,32},{16,48},{32,0},{48,16},{1,33},{17,49},{33,1},{49,17},{2,34}... | collective-permute-start | bytes 294920 | tf_op jit(solution)/shard_map/ppermute | solution.py:143
  41.6 3.3 %collective-permute-start.1 = (bf16[32,4096]{1,0:T(8,128)(2,1)S(1)}, bf16[32,4096]{1,0:T(8,128)(2,1)}, u32[]{:S(2)}, u32[]{:S(2)}) collective-permute-start(bf16[32,4096]{1,0:T(8,128)(2,1)S(1)} %collective-permute-done.refs_2_), channel_id=1, source_target_pairs={{0,2},{2,4},{4,6},{6,8},{8,10},{10,12},{12,14},{14,256},{256,258},... | collective-permute-start | bytes 786440 | tf_op jit(solution)/shard_map/ppermute | solution.py:32
  45.0 4.2 %collective-permute-start.3 = (bf16[32,4096]{1,0:T(8,128)(2,1)S(1)}, bf16[32,4096]{1,0:T(8,128)(2,1)}, u32[]{:S(2)}, u32[]{:S(2)}) collective-permute-start(bf16[32,4096]{1,0:T(8,128)(2,1)S(1)} %collective-permute-done.2.refs_3_), channel_id=1, source_target_pairs={{0,270},{2,0},{4,2},{6,4},{8,6},{10,8},{12,10},{14,12},{256,14},{2... | collective-permute-start | bytes 786440 | tf_op jit(solution)/shard_map/ppermute | solution.py:36
  56.6 3.7 %collective-permute-start.11 = (bf16[2,384,256]{2,1,0:T(8,128)(2,1)S(1)}, bf16[2,384,256]{2,1,0:T(8,128)(2,1)S(1)}, u32[]{:S(2)}, u32[]{:S(2)}) collective-permute-start(bf16[2,384,256]{2,1,0:T(8,128)(2,1)S(1)} %bitcast.51), channel_id=1, source_target_pairs={{0,192},{64,0},{128,64},{192,128},{1,193},{65,1},{129,65},{193,129... | collective-permute-start | bytes 1179656 | tf_op jit(solution)/shard_map/ppermute | solution.py:145
  60.3 3.1 %collective-permute-start.12 = (bf16[2,384,256]{2,1,0:T(8,128)(2,1)S(1)}, bf16[2,384,256]{2,1,0:T(8,128)(2,1)S(1)}, u32[]{:S(2)}, u32[]{:S(2)}) collective-permute-start(bf16[2,384,256]{2,1,0:T(8,128)(2,1)S(1)} %bitcast.52), channel_id=1, source_target_pairs={{0,128},{64,192},{128,0},{192,64},{1,129},{65,193},{129,1},{193,65... | collective-permute-start | bytes 1179656 | tf_op jit(solution)/shard_map/ppermute | solution.py:145
  63.8 4.5 %collective-permute-done.10 = bf16[2,384,256]{2,1,0:T(8,128)(2,1)S(1)} collective-permute-done((bf16[2,384,256]{2,1,0:T(8,128)(2,1)S(1)}, bf16[2,384,256]{2,1,0:T(8,128)(2,1)S(1)}, u32[]{:S(2)}, u32[]{:S(2)}) %collective-permute-start.10) | collective-permute-done | bytes 393248 | tf_op jit(solution)/shard_map/ppermute | solution.py:145
  70.3 8.7 %collective-permute-done.11 = bf16[2,384,256]{2,1,0:T(8,128)(2,1)S(1)} collective-permute-done((bf16[2,384,256]{2,1,0:T(8,128)(2,1)S(1)}, bf16[2,384,256]{2,1,0:T(8,128)(2,1)S(1)}, u32[]{:S(2)}, u32[]{:S(2)}) %collective-permute-start.11) | collective-permute-done | bytes 393248 | tf_op jit(solution)/shard_map/ppermute | solution.py:145
  79.0 3.9 %collective-permute-start.15 = (bf16[32,4096]{1,0:T(8,128)(2,1)}, bf16[32,4096]{1,0:T(8,128)(2,1)}, u32[]{:S(2)}, u32[]{:S(2)}) collective-permute-start(bf16[32,4096]{1,0:T(8,128)(2,1)} %collective-permute-done.3.refs_1_), channel_id=1, source_target_pairs={{0,270},{2,0},{4,2},{6,4},{8,6},{10,8},{12,10},{14,12},{256,14},{2... | collective-permute-start | bytes 786440 | tf_op jit(solution)/shard_map/ppermute | solution.py:36
  90.3 7.7 %collective-permute-done.16.refs_0_ = bf16[32,4096]{1,0:T(8,128)(2,1)} collective-permute-done((bf16[32,4096]{1,0:T(8,128)(2,1)}, bf16[32,4096]{1,0:T(8,128)(2,1)}, u32[]{:S(2)}, u32[]{:S(2)}) %collective-permute-start.16) | collective-permute-done | bytes 262176 | tf_op jit(solution)/shard_map/ppermute | solution.py:139
  101.2 7.0 %attend3.1 = bf16[96,4096]{1,0:T(8,128)(2,1)S(1)} custom-call(bf16[32,4096]{1,0:T(8,128)(2,1)} %collective-permute-done.16.refs_0_, bf16[32,4096]{1,0:T(8,128)(2,1)S(1)} %collective-permute-done.14.refs_1_, bf16[32,4096]{1,0:T(8,128)(2,1)} %collective-permute-done.15.refs_2_, bf16[4096,256]{1,0:T(8,128)(2,1)S(1)} %copy-done, ...), custom_call_target="tpu_custom_call" | custom-call | flops 1207959552 | bytes 12582912 | tf_op jit(solution)/shard_map/attend3/pallas_call | solution.py:107
  108.3 4.1 %collective-permute-start.17 = (bf16[32,4096]{1,0:T(8,128)(2,1)S(1)}, bf16[32,4096]{1,0:T(8,128)(2,1)S(1)}, u32[]{:S(2)}, u32[]{:S(2)}) collective-permute-start(bf16[32,4096]{1,0:T(8,128)(2,1)S(1)} %slice.55), channel_id=1, source_target_pairs={{0,270},{1,3},{2,0},{3,5},{4,2},{5,7},{6,4},{7,9},{8,6},{9,11},{10... | collective-permute-start | bytes 786440 | tf_op jit(solution)/shard_map/ppermute | solution.py:171
  112.4 4.3 %collective-permute-done.17 = bf16[32,4096]{1,0:T(8,128)(2,1)S(1)} collective-permute-done((bf16[32,4096]{1,0:T(8,128)(2,1)S(1)}, bf16[32,4096]{1,0:T(8,128)(2,1)S(1)}, u32[]{:S(2)}, u32[]{:S(2)}) %collective-permute-start.17) | collective-permute-done | bytes 262176 | tf_op jit(solution)/shard_map/ppermute | solution.py:171
  116.9 5.3 %collective-permute-start.18 = (bf16[32,4096]{1,0:T(8,128)(2,1)S(1)}, bf16[32,4096]{1,0:T(8,128)(2,1)S(1)}, u32[]{:S(2)}, u32[]{:S(2)}) collective-permute-start(bf16[32,4096]{1,0:T(8,128)(2,1)S(1)} %get-tuple-element.11), channel_id=1, source_target_pairs={{0,270},{2,0},{4,2},{6,4},{8,6},{10,8},{12,10},{14,12},{256,14},{2... | collective-permute-start | bytes 786440 | tf_op jit(solution)/shard_map/ppermute | solution.py:36
  122.2 7.7 %attend5.1 = bf16[160,4096]{1,0:T(8,128)(2,1)S(1)} custom-call(bf16[32,4096]{1,0:T(8,128)(2,1)} %collective-permute-done.1.refs_0_, bf16[32,4096]{1,0:T(8,128)(2,1)} %collective-permute-done.3.refs_1_, bf16[32,4096]{1,0:T(8,128)(2,1)S(1)} %copy-done.6, bf16[32,4096]{1,0:T(8,128)(2,1)S(1)} %copy-done.8, bf16[32,4096]{1,0:T(8,128)(2,1)S(1)} %copy-done.4, ...), custom_call_target="tpu_custom_call" | custom-call | flops 2013265920 | bytes 12582912 | tf_op jit(solution)/shard_map/attend5/pallas_call | solution.py:107
  132.0 5.1 %collective-permute-start.19 = (bf16[32,4096]{1,0:T(8,128)(2,1)S(1)}, bf16[32,4096]{1,0:T(8,128)(2,1)S(1)}, u32[]{:S(2)}, u32[]{:S(2)}) collective-permute-start(bf16[32,4096]{1,0:T(8,128)(2,1)S(1)} %add_convert_fusion.4), channel_id=1, source_target_pairs={{0,270},{2,0},{4,2},{6,4},{8,6},{10,8},{12,10},{14,12},{256,14},{2... | collective-permute-start | bytes 786440 | tf_op jit(solution)/shard_map/ppermute | solution.py:36
  143.1 5.6 %collective-permute-start.20 = (bf16[32,4096]{1,0:T(8,128)(2,1)S(1)}, bf16[32,4096]{1,0:T(8,128)(2,1)S(1)}, u32[]{:S(2)}, u32[]{:S(2)}) collective-permute-start(bf16[32,4096]{1,0:T(8,128)(2,1)S(1)} %get-tuple-element.9), channel_id=1, source_target_pairs={{0,270},{2,0},{4,2},{6,4},{8,6},{10,8},{12,10},{14,12},{256,14},{2... | collective-permute-start | bytes 786440 | tf_op jit(solution)/shard_map/ppermute | solution.py:36
  148.7 5.2 %collective-permute-done.22 = bf16[32,4096]{1,0:T(8,128)(2,1)S(1)} collective-permute-done((bf16[32,4096]{1,0:T(8,128)(2,1)S(1)}, bf16[32,4096]{1,0:T(8,128)(2,1)S(1)}, u32[]{:S(2)}, u32[]{:S(2)}) %collective-permute-start.22) | collective-permute-done | bytes 262176 | tf_op jit(solution)/shard_map/ppermute | solution.py:32
  155.9 7.5 %collective-permute-done.23 = bf16[32,4096]{1,0:T(8,128)(2,1)S(1)} collective-permute-done((bf16[32,4096]{1,0:T(8,128)(2,1)S(1)}, bf16[32,4096]{1,0:T(8,128)(2,1)S(1)}, u32[]{:S(2)}, u32[]{:S(2)}) %collective-permute-start.23) | collective-permute-done | bytes 262176 | tf_op jit(solution)/shard_map/ppermute | solution.py:32
  (72 shorter events, 33.5 us)
Async XLA Ops:
  1.9 39.8 %collective-permute-start = (bf16[32,4096]{1,0:T(8,128)(2,1)}, bf16[32,4096]{1,0:T(8,128)(2,1)S(1)}, u32[]{:S(2)}, u32[]{:S(2)}) collective-permute-start(bf16[32,4096]{1,0:T(8,128)(2,1)} %get-tuple-element.7.refs_4_), channel_id=1, source_target_pairs={{0,2},{2,4},{4,6},{6,8},{8,10},{10,12},{12,14},{14,256},{256,258},... | collective-permute-start | bytes 786440 | tf_op jit(solution)/shard_map/ppermute | solution.py:32
  5.7 39.3 %collective-permute-start.2 = (bf16[32,4096]{1,0:T(8,128)(2,1)}, bf16[32,4096]{1,0:T(8,128)(2,1)S(1)}, u32[]{:S(2)}, u32[]{:S(2)}) collective-permute-start(bf16[32,4096]{1,0:T(8,128)(2,1)} %get-tuple-element.7.refs_4_), channel_id=1, source_target_pairs={{0,270},{2,0},{4,2},{6,4},{8,6},{10,8},{12,10},{14,12},{256,14},{2... | collective-permute-start | bytes 786440 | tf_op jit(solution)/shard_map/ppermute | solution.py:36
  15.2 15.6 %collective-permute-start.6 = (bf16[112,256]{1,0:T(8,128)(2,1)}, bf16[112,256]{1,0:T(8,128)(2,1)S(1)}, u32[]{:S(2)}, u32[]{:S(2)}) collective-permute-start(bf16[112,256]{1,0:T(8,128)(2,1)} %get-tuple-element.8), channel_id=1, source_target_pairs={{0,256},{256,0},{1,257},{257,1},{2,258},{258,2},{3,259},{259,3},{4... | collective-permute-start | bytes 172040 | tf_op jit(solution)/shard_map/ppermute | solution.py:141
  30.8 19.2 %collective-permute-start.7 = (bf16[2,2,48,256]{3,2,1,0:T(8,128)(2,1)S(1)}, bf16[2,2,48,256]{3,2,1,0:T(8,128)(2,1)S(1)}, u32[]{:S(2)}, u32[]{:S(2)}) collective-permute-start(bf16[2,2,48,256]{3,2,1,0:T(8,128)(2,1)S(1)} %get-tuple-element.14), channel_id=1, source_target_pairs={{0,16},{16,32},{32,48},{48,0},{1,17},{17,33},{33,49},{49,1},{2,18}... | collective-permute-start | bytes 294920 | tf_op jit(solution)/shard_map/ppermute | solution.py:143
  34.2 17.7 %collective-permute-start.8 = (bf16[2,2,48,256]{3,2,1,0:T(8,128)(2,1)S(1)}, bf16[2,2,48,256]{3,2,1,0:T(8,128)(2,1)S(1)}, u32[]{:S(2)}, u32[]{:S(2)}) collective-permute-start(bf16[2,2,48,256]{3,2,1,0:T(8,128)(2,1)S(1)} %get-tuple-element.14), channel_id=1, source_target_pairs={{0,48},{16,0},{32,16},{48,32},{1,49},{17,1},{33,17},{49,33},{2,50}... | collective-permute-start | bytes 294920 | tf_op jit(solution)/shard_map/ppermute | solution.py:143
  37.9 16.5 %collective-permute-start.9 = (bf16[2,2,48,256]{3,2,1,0:T(8,128)(2,1)S(1)}, bf16[2,2,48,256]{3,2,1,0:T(8,128)(2,1)S(1)}, u32[]{:S(2)}, u32[]{:S(2)}) collective-permute-start(bf16[2,2,48,256]{3,2,1,0:T(8,128)(2,1)S(1)} %get-tuple-element.14), channel_id=1, source_target_pairs={{0,32},{16,48},{32,0},{48,16},{1,33},{17,49},{33,1},{49,17},{2,34}... | collective-permute-start | bytes 294920 | tf_op jit(solution)/shard_map/ppermute | solution.py:143
  41.6 15.0 %collective-permute-start.1 = (bf16[32,4096]{1,0:T(8,128)(2,1)S(1)}, bf16[32,4096]{1,0:T(8,128)(2,1)}, u32[]{:S(2)}, u32[]{:S(2)}) collective-permute-start(bf16[32,4096]{1,0:T(8,128)(2,1)S(1)} %collective-permute-done.refs_2_), channel_id=1, source_target_pairs={{0,2},{2,4},{4,6},{6,8},{8,10},{10,12},{12,14},{14,256},{256,258},... | collective-permute-start | bytes 786440 | tf_op jit(solution)/shard_map/ppermute | solution.py:32
  45.0 15.3 %collective-permute-start.3 = (bf16[32,4096]{1,0:T(8,128)(2,1)S(1)}, bf16[32,4096]{1,0:T(8,128)(2,1)}, u32[]{:S(2)}, u32[]{:S(2)}) collective-permute-start(bf16[32,4096]{1,0:T(8,128)(2,1)S(1)} %collective-permute-done.2.refs_3_), channel_id=1, source_target_pairs={{0,270},{2,0},{4,2},{6,4},{8,6},{10,8},{12,10},{14,12},{256,14},{2... | collective-permute-start | bytes 786440 | tf_op jit(solution)/shard_map/ppermute | solution.py:36
  50.0 48.0 %collective-permute-start.4 = (bf16[4096,256]{1,0:T(8,128)(2,1)}, bf16[4096,256]{1,0:T(8,128)(2,1)}, u32[]{:S(2)}, u32[]{:S(2)}) collective-permute-start(bf16[4096,256]{1,0:T(8,128)(2,1)} %refs_3_.1), channel_id=1, source_target_pairs={{0,1},{1,0},{2,3},{3,2},{4,5},{5,4},{6,7},{7,6},{8,9},{9,8},{10,11... | collective-permute-start | bytes 6291464 | tf_op jit(solution)/shard_map/ppermute | solution.py:147
  52.0 46.1 %collective-permute-start.5 = (bf16[256,4096]{1,0:T(8,128)(2,1)}, bf16[256,4096]{1,0:T(8,128)(2,1)}, u32[]{:S(2)}, u32[]{:S(2)}) collective-permute-start(bf16[256,4096]{1,0:T(8,128)(2,1)} %refs_5_.3), channel_id=1, source_target_pairs={{0,1},{1,0},{2,3},{3,2},{4,5},{5,4},{6,7},{7,6},{8,9},{9,8},{10,11... | collective-permute-start | bytes 6291464 | tf_op jit(solution)/shard_map/ppermute | solution.py:148
  54.5 13.9 %collective-permute-start.10 = (bf16[2,384,256]{2,1,0:T(8,128)(2,1)S(1)}, bf16[2,384,256]{2,1,0:T(8,128)(2,1)S(1)}, u32[]{:S(2)}, u32[]{:S(2)}) collective-permute-start(bf16[2,384,256]{2,1,0:T(8,128)(2,1)S(1)} %bitcast.50), channel_id=1, source_target_pairs={{0,64},{64,128},{128,192},{192,0},{1,65},{65,129},{129,193},{193,1... | collective-permute-start | bytes 1179656 | tf_op jit(solution)/shard_map/ppermute | solution.py:145
  56.6 22.4 %collective-permute-start.11 = (bf16[2,384,256]{2,1,0:T(8,128)(2,1)S(1)}, bf16[2,384,256]{2,1,0:T(8,128)(2,1)S(1)}, u32[]{:S(2)}, u32[]{:S(2)}) collective-permute-start(bf16[2,384,256]{2,1,0:T(8,128)(2,1)S(1)} %bitcast.51), channel_id=1, source_target_pairs={{0,192},{64,0},{128,64},{192,128},{1,193},{65,1},{129,65},{193,129... | collective-permute-start | bytes 1179656 | tf_op jit(solution)/shard_map/ppermute | solution.py:145
  60.3 22.5 %collective-permute-start.12 = (bf16[2,384,256]{2,1,0:T(8,128)(2,1)S(1)}, bf16[2,384,256]{2,1,0:T(8,128)(2,1)S(1)}, u32[]{:S(2)}, u32[]{:S(2)}) collective-permute-start(bf16[2,384,256]{2,1,0:T(8,128)(2,1)S(1)} %bitcast.52), channel_id=1, source_target_pairs={{0,128},{64,192},{128,0},{192,64},{1,129},{65,193},{129,1},{193,65... | collective-permute-start | bytes 1179656 | tf_op jit(solution)/shard_map/ppermute | solution.py:145
  68.3 16.9 %collective-permute-start.14 = (bf16[32,4096]{1,0:T(8,128)(2,1)}, bf16[32,4096]{1,0:T(8,128)(2,1)S(1)}, u32[]{:S(2)}, u32[]{:S(2)}) collective-permute-start(bf16[32,4096]{1,0:T(8,128)(2,1)} %collective-permute-done.1.refs_0_), channel_id=1, source_target_pairs={{0,2},{2,4},{4,6},{6,8},{8,10},{10,12},{12,14},{14,256},{256,258},... | collective-permute-start | bytes 786440 | tf_op jit(solution)/shard_map/ppermute | solution.py:32
  79.0 8.6 %collective-permute-start.15 = (bf16[32,4096]{1,0:T(8,128)(2,1)}, bf16[32,4096]{1,0:T(8,128)(2,1)}, u32[]{:S(2)}, u32[]{:S(2)}) collective-permute-start(bf16[32,4096]{1,0:T(8,128)(2,1)} %collective-permute-done.3.refs_1_), channel_id=1, source_target_pairs={{0,270},{2,0},{4,2},{6,4},{8,6},{10,8},{12,10},{14,12},{256,14},{2... | collective-permute-start | bytes 786440 | tf_op jit(solution)/shard_map/ppermute | solution.py:36
  83.1 14.9 %collective-permute-start.13 = (bf16[4,2,384,256]{3,2,1,0:T(8,128)(2,1)S(1)}, bf16[4,2,384,256]{3,2,1,0:T(8,128)(2,1)S(1)}, u32[]{:S(2)}, u32[]{:S(2)}) collective-permute-start(bf16[4,2,384,256]{3,2,1,0:T(8,128)(2,1)S(1)} %pad_maximum_fusion.refs_9_.refs_7_), channel_id=1, source_target_pairs={{0,1},{1,0},{2,3},{3,2},{4,5},{5,4},{6,7},{7,6},{8,9},{9,8},{10,11... | collective-permute-start | bytes 4718600 | tf_op jit(solution)/shard_map/ppermute | solution.py:146
  88.3 9.8 %collective-permute-start.16 = (bf16[32,4096]{1,0:T(8,128)(2,1)}, bf16[32,4096]{1,0:T(8,128)(2,1)}, u32[]{:S(2)}, u32[]{:S(2)}) collective-permute-start(bf16[32,4096]{1,0:T(8,128)(2,1)} %broadcast_select_fusion), channel_id=1, source_target_pairs={{0,2},{1,271},{2,4},{3,1},{4,6},{5,3},{6,8},{7,5},{8,10},{9,7},{10... | collective-permute-start | bytes 786440 | tf_op jit(solution)/shard_map/ppermute | solution.py:139
  108.3 8.4 %collective-permute-start.17 = (bf16[32,4096]{1,0:T(8,128)(2,1)S(1)}, bf16[32,4096]{1,0:T(8,128)(2,1)S(1)}, u32[]{:S(2)}, u32[]{:S(2)}) collective-permute-start(bf16[32,4096]{1,0:T(8,128)(2,1)S(1)} %slice.55), channel_id=1, source_target_pairs={{0,270},{1,3},{2,0},{3,5},{4,2},{5,7},{6,4},{7,9},{8,6},{9,11},{10... | collective-permute-start | bytes 786440 | tf_op jit(solution)/shard_map/ppermute | solution.py:171
  116.9 15.0 %collective-permute-start.18 = (bf16[32,4096]{1,0:T(8,128)(2,1)S(1)}, bf16[32,4096]{1,0:T(8,128)(2,1)S(1)}, u32[]{:S(2)}, u32[]{:S(2)}) collective-permute-start(bf16[32,4096]{1,0:T(8,128)(2,1)S(1)} %get-tuple-element.11), channel_id=1, source_target_pairs={{0,270},{2,0},{4,2},{6,4},{8,6},{10,8},{12,10},{14,12},{256,14},{2... | collective-permute-start | bytes 786440 | tf_op jit(solution)/shard_map/ppermute | solution.py:36
  130.0 9.5 %collective-permute-start.21 = (bf16[32,4096]{1,0:T(8,128)(2,1)S(1)}, bf16[32,4096]{1,0:T(8,128)(2,1)S(1)}, u32[]{:S(2)}, u32[]{:S(2)}) collective-permute-start(bf16[32,4096]{1,0:T(8,128)(2,1)S(1)} %get-tuple-element.12), channel_id=1, source_target_pairs={{0,2},{2,4},{4,6},{6,8},{8,10},{10,12},{12,14},{14,256},{256,258},... | collective-permute-start | bytes 786440 | tf_op jit(solution)/shard_map/ppermute | solution.py:32
  132.0 9.0 %collective-permute-start.19 = (bf16[32,4096]{1,0:T(8,128)(2,1)S(1)}, bf16[32,4096]{1,0:T(8,128)(2,1)S(1)}, u32[]{:S(2)}, u32[]{:S(2)}) collective-permute-start(bf16[32,4096]{1,0:T(8,128)(2,1)S(1)} %add_convert_fusion.4), channel_id=1, source_target_pairs={{0,270},{2,0},{4,2},{6,4},{8,6},{10,8},{12,10},{14,12},{256,14},{2... | collective-permute-start | bytes 786440 | tf_op jit(solution)/shard_map/ppermute | solution.py:36
  141.1 12.7 %collective-permute-start.22 = (bf16[32,4096]{1,0:T(8,128)(2,1)S(1)}, bf16[32,4096]{1,0:T(8,128)(2,1)S(1)}, u32[]{:S(2)}, u32[]{:S(2)}) collective-permute-start(bf16[32,4096]{1,0:T(8,128)(2,1)S(1)} %get-tuple-element.10), channel_id=1, source_target_pairs={{0,2},{2,4},{4,6},{6,8},{8,10},{10,12},{12,14},{14,256},{256,258},... | collective-permute-start | bytes 786440 | tf_op jit(solution)/shard_map/ppermute | solution.py:32
  143.1 12.8 %collective-permute-start.20 = (bf16[32,4096]{1,0:T(8,128)(2,1)S(1)}, bf16[32,4096]{1,0:T(8,128)(2,1)S(1)}, u32[]{:S(2)}, u32[]{:S(2)}) collective-permute-start(bf16[32,4096]{1,0:T(8,128)(2,1)S(1)} %get-tuple-element.9), channel_id=1, source_target_pairs={{0,270},{2,0},{4,2},{6,4},{8,6},{10,8},{12,10},{14,12},{256,14},{2... | collective-permute-start | bytes 786440 | tf_op jit(solution)/shard_map/ppermute | solution.py:36
  153.9 9.5 %collective-permute-start.23 = (bf16[32,4096]{1,0:T(8,128)(2,1)S(1)}, bf16[32,4096]{1,0:T(8,128)(2,1)S(1)}, u32[]{:S(2)}, u32[]{:S(2)}) collective-permute-start(bf16[32,4096]{1,0:T(8,128)(2,1)S(1)} %add_convert_fusion.1), channel_id=1, source_target_pairs={{0,2},{2,4},{4,6},{6,8},{8,10},{10,12},{12,14},{14,256},{256,258},... | collective-permute-start | bytes 786440 | tf_op jit(solution)/shard_map/ppermute | solution.py:32
  (10 other events, 168.2 us)

commit v3 on v2

--- a/solution.py
+++ b/solution.py
@@ -12,12 +12,8 @@
 MASKED = -1e30
 RING = ("zh", "zl")
 SWAP = [(0, 1), (1, 0)]
-TURNS = (0, 1, 3, 2)
 VMEM = pl.BlockSpec(memory_space=pltpu.VMEM)
-
-
-def shift(step, size=16):
-    return [(i, (i + step) % size) for i in range(size)]
+HELD = pl.BlockSpec(memory_space=pl.ANY)
 
 
 def opposite(step):
@@ -28,12 +24,8 @@
     ]
 
 
-def up(x):
-    return lax.ppermute(x, RING, shift(1))
-
-
-def down(x):
-    return lax.ppermute(x, RING, shift(-1))
+def along(x, step):
+    return lax.ppermute(x, RING + ("c",), opposite(step))
 
 
 def prepare_kernel(tokens, gain, keys, values, pos, normed, payload):
@@ -51,10 +43,16 @@
 
 def attend_kernel(count, first, *refs):
     blocks = refs[:count]
+    sem = refs[-1]
+    held = refs[count + 9 : count + 14]
+    far = refs[count : count + 4] + (refs[count + 5],)
+    copies = [pltpu.make_async_copy(far[i], held[i], sem.at[i]) for i in (0, 1, 4, 2, 3)]
+    for copy in copies:
+        copy.start()
     wq, wo, kv, bound, frame, out = (
-        refs[count : count + 2],
-        refs[count + 2 : count + 4],
-        refs[count + 4 : count + 6],
+        held[0:2],
+        held[2:4],
+        (refs[count + 4], held[4]),
         refs[count + 6],
         refs[count + 7],
         refs[count + 8],
@@ -66,6 +64,9 @@
     bias = jnp.where(frame[...].astype(jnp.float32) <= column, 0.0, MASKED)
     groups = []
     for g in range(2):
+        copies[g].wait()
+        if g == 1:
+            copies[2].wait()
         q = jnp.dot(x, wq[g][...], preferred_element_type=jnp.float32)
         q = (q * HEAD_DIM**-0.5).astype(jnp.bfloat16)
         heads = []
@@ -74,7 +75,7 @@
             s = [
                 lax.dot_general(
                     q[:, cols],
-                    kv[g][t, 0, :, cols],
+                    kv[g][4 * t : 4 * t + 4, 0, :, :, cols].reshape(384, HEAD_DIM),
                     (((1,), (1,)), ((), ())),
                     preferred_element_type=jnp.float32,
                 )
@@ -87,13 +88,15 @@
             a = sum(
                 jnp.dot(
                     e[:, t * 384 : (t + 1) * 384],
-                    kv[g][t, 1, :, cols],
+                    kv[g][4 * t : 4 * t + 4, 1, :, :, cols].reshape(384, HEAD_DIM),
                     preferred_element_type=jnp.float32,
                 )
                 for t in range(4)
             )
             heads.append((a / total).astype(jnp.bfloat16))
         groups.append(jnp.concatenate(heads, axis=1))
+    copies[3].wait()
+    copies[4].wait()
     for n in range(0, 4096, 1024):
         cols = slice(n, n + 1024)
         total = jnp.dot(groups[0], wo[0][:, cols], preferred_element_type=jnp.float32)
@@ -107,8 +110,16 @@
     return pl.pallas_call(
         functools.partial(attend_kernel, count, first),
         out_shape=jax.ShapeDtypeStruct((rows, 4096), jnp.bfloat16),
-        in_specs=[VMEM] * (count + 8),
+        in_specs=[VMEM] * count + [HELD] * 4 + [VMEM, HELD, VMEM, VMEM],
         out_specs=VMEM,
+        scratch_shapes=[
+            pltpu.VMEM((4096, 256), jnp.bfloat16),
+            pltpu.VMEM((4096, 256), jnp.bfloat16),
+            pltpu.VMEM((256, 4096), jnp.bfloat16),
+            pltpu.VMEM((256, 4096), jnp.bfloat16),
+            pltpu.VMEM((16, 2, 2, 48, 256), jnp.bfloat16),
+            pltpu.SemaphoreType.DMA((5,)),
+        ],
         compiler_params=pltpu.CompilerParams(vmem_limit_bytes=40 * 2**20),
         cost_estimate=pl.CostEstimate(
             flops=rows * 12 * 2**20, bytes_accessed=12 * 2**20, transcendentals=rows * 6144
@@ -119,7 +130,7 @@
 
 def per_device(tokens, gain, wq, wo, keys, values, token_pos, frame_pad):
     rows = tokens.shape[0]
-    zh, y, x, zl, core = (lax.axis_index(a) for a in ("zh", "y", "x", "zl", "c"))
+    zh, zl, core = (lax.axis_index(a) for a in ("zh", "zl", "c"))
     z = zh * 8 + zl
     pos = token_pos.T
     own, mine = pl.pallas_call(
@@ -133,30 +144,31 @@
         name="prepare",
     )(tokens.reshape(rows, 4096), gain.reshape(1, 4096), keys.reshape(48, 256), values.reshape(48, 256), pos)
 
-    p1, m1 = up(own), down(own)
-    p2, m2 = up(p1), down(m1)
-    p3, m3 = up(p2), down(m2)
-    far = lax.ppermute(jnp.where(core == 0, p3, m3), RING + ("c",), opposite(1))
+    a1, b1 = along(own, 1), along(own, -1)
 
     theirs = lax.ppermute(mine, "zh", SWAP)
     kv = jnp.stack([mine[:96].reshape(2, 48, 256), theirs[:96].reshape(2, 48, 256)], axis=1)
-    kv = jnp.stack([kv] + [lax.ppermute(kv, "x", shift(s, 4)) for s in TURNS[1:]], axis=1)
-    kv = kv.reshape(2, 384, 256)
-    kv = jnp.stack([kv] + [lax.ppermute(kv, "y", shift(s, 4)) for s in TURNS[1:]])
+    kv, a1, b1 = lax.optimization_barrier((kv, a1, b1))
+    kv = jnp.broadcast_to(kv[None], (16, 2, 2, 48, 256))
+    kv = lax.all_to_all(kv, ("y", "x"), 0, 0, tiled=True)
+    a2, b2 = along(a1, 1), along(b1, -1)
+    a3, b3 = along(a2, 1), along(b2, -1)
+    kv, a3, b3 = lax.optimization_barrier((kv, a3, b3))
+    a4 = along(a3, 1)
     kv_other = lax.ppermute(kv, "c", SWAP)
     wq_other = lax.ppermute(wq, "c", SWAP)
     wo_other = lax.ppermute(wo, "c", SWAP)
 
-    turns = jnp.array(TURNS, jnp.int32)
-    ys, xs, halves = (y - turns) % 4, (x - turns) % 4, jnp.array([0, 1], jnp.int32) ^ zh
-    place = halves[None, None, :] * 16 + ys[:, None, None] * 4 + xs[None, :, None]
+    halves = jnp.array([0, 1], jnp.int32) ^ zh
+    place = halves[None, :] * 16 + jnp.arange(16, dtype=jnp.int32)[:, None]
     frame = (place[..., None] * 48 + jnp.arange(48, dtype=jnp.int32)).reshape(1, 1536)
 
     other = theirs[96:98].astype(jnp.int32) * 8 + theirs[98:100].astype(jnp.int32)
     other = other.reshape(1, 512)
     both = jnp.where(zh == 0, jnp.concatenate([pos, other]), jnp.concatenate([other, pos]))
     both = both.reshape(16, 2, rows)
-    steps = (jnp.where(core == 0, -4, 4), -3, 3, -2, 2, -1, 1, 0)
+    sign = 2 * core - 1
+    steps = [sign * d for d in (4, 3, -3, 2, -2, 1, -1, 0)]
     bound = jnp.concatenate(
         [lax.dynamic_slice(both, ((z + d) % 16, core, 0), (1, 1, rows)).reshape(1, rows) for d in steps],
         axis=1,
@@ -164,17 +176,20 @@
     bound = jnp.minimum(bound, 1535 - frame_pad[0])
 
     given = ((wq, wq_other), (wo, wo_other), (kv, kv_other), bound, frame)
-    part = attend([far, p3, m3], 0, *given)
-    near = attend([p2, m2, p1, m1, own], 96, *given)
+    pair = attend([a3, b3], 32, *given)
+    last = attend([a4], 0, *given)
+    near = attend([a2, b2, a1, b1, own], 96, *given)
     wide = lambda v: v.astype(jnp.float32)
     thin = lambda v: v.astype(jnp.bfloat16)
-    back = wide(lax.ppermute(part[:32], RING + ("c",), opposite(-1)))
-    zero = jnp.zeros_like(back)
-    ap = down(thin(wide(part[32:64]) + jnp.where(core == 0, back, zero)))
-    am = up(thin(wide(part[64:96]) + jnp.where(core == 0, zero, back)))
-    ap, am = down(thin(wide(near[:32]) + wide(ap))), up(thin(wide(near[32:64]) + wide(am)))
-    ap, am = down(thin(wide(near[64:96]) + wide(ap))), up(thin(wide(near[96:128]) + wide(am)))
-    out = wide(near[128:160]) + wide(ap) + wide(am)
+    plus = lambda u, v: thin(wide(u) + wide(v))
+    ap, bp = along(last, -1), along(pair[32:64], 1)
+    ap, bp, near = lax.optimization_barrier((ap, bp, near))
+    ap, bp = along(plus(pair[:32], ap), -1), along(plus(near[32:64], bp), 1)
+    ap, bp = lax.optimization_barrier((ap, bp))
+    ap, bp = along(plus(near[:32], ap), -1), along(plus(near[96:128], bp), 1)
+    ap, bp = lax.optimization_barrier((ap, bp))
+    ap = along(plus(near[64:96], ap), -1)
+    out = wide(near[128:160]) + wide(ap) + wide(bp)
     return thin(out).reshape(rows, 1, 4096)
 
 

time: 165 us -> 136 us (0.82)
  the two profiles are of different devices: /device:TPU:24 before, /device:TPU:1 now
where the time goes in v3:
time: 136 us; the launch traced here: 133 us
  starting transfers between devices  74.4 us (55%)
  waiting for transfers between devices  28.2 us (21%)
  Pallas kernels  18.6 us (14%)
  local copies, waits for them, and re-layouts  9.72 us (7%)
    ppermute x14, starting transfers between devices, along(): return lax.ppermute(x, RING + ('c',), opposite(step))  53.1 us
    ppermute x14, waiting for transfers between devices, along(): return lax.ppermute(x, RING + ('c',), opposite(step))  22.8 us
    pallas_call x3, Pallas kernels, attend(): pl.pallas_call(functools.partial(attend_kernel, count, first), out_shape=...  16.7 us
    ppermute x1, starting transfers between devices, per_device(): theirs = lax.ppermute(mine, 'zh', SWAP)  7.68 us
    unnamed x29, local copies, waits for them, and re-layouts  7.23 us
    all_to_all x1, starting transfers between devices, per_device(): kv = lax.all_to_all(kv, ('y', 'x'), 0, 0, tiled=True)  6.89 us
    ppermute x1, waiting for transfers between devices, per_device(): theirs = lax.ppermute(mine, 'zh', SWAP)  5.34 us
    ppermute x1, starting transfers between devices, per_device(): wq_other = lax.ppermute(wq, 'c', SWAP)  2.91 us
  transfers between devices with their start and end apart: 19, of which 7 were waited for; matrix products, arithmetic and copies ran while one was open for 1% of the time, Pallas kernels for 13%

profile of v3, /device:TPU:1, one launch (start us, length us, event | category | flops | bytes accessed | tf_op | source)
XLA Modules:
  0.0 133.4 jit_solution(2508838401010054867)
XLA Ops:
  1.9 11.9 %collective-permute-start.1 = (bf16[32,4096]{1,0:T(8,128)(2,1)}, bf16[32,4096]{1,0:T(8,128)(2,1)S(1)}, u32[]{:S(2)}, u32[]{:S(2)}) collective-permute-start(bf16[32,4096]{1,0:T(8,128)(2,1)} %get-tuple-element.21.refs_4_), channel_id=1, source_target_pairs={{0,2},{1,271},{2,4},{3,1},{4,6},{5,3},{6,8},{7,5},{8,10},{9,7},{10... | collective-permute-start | bytes 786440 | tf_op jit(solution)/shard_map/ppermute | solution.py:28
  15.7 7.7 %collective-permute-start = (bf16[112,256]{1,0:T(8,128)(2,1)}, bf16[112,256]{1,0:T(8,128)(2,1)S(1)}, u32[]{:S(2)}, u32[]{:S(2)}) collective-permute-start(bf16[112,256]{1,0:T(8,128)(2,1)} %get-tuple-element.20), channel_id=1, source_target_pairs={{0,256},{256,0},{1,257},{257,1},{2,258},{258,2},{3,259},{259,3},{4... | collective-permute-start | bytes 172040 | tf_op jit(solution)/shard_map/ppermute | solution.py:149
  24.2 5.3 %collective-permute-done = bf16[112,256]{1,0:T(8,128)(2,1)S(1)} collective-permute-done((bf16[112,256]{1,0:T(8,128)(2,1)}, bf16[112,256]{1,0:T(8,128)(2,1)S(1)}, u32[]{:S(2)}, u32[]{:S(2)}) %collective-permute-start) | collective-permute-done | bytes 57376 | tf_op jit(solution)/shard_map/ppermute | solution.py:149
  31.0 6.9 %all-to-all-start = ((bf16[16,2,2,48,256]{4,3,2,1,0:T(8,128)(2,1)}), bf16[16,2,2,48,256]{4,3,2,1,0:T(8,128)(2,1)S(1)}, u32[]{:S(2)}, u32[]{:S(2)}) async-start(bf16[16,2,2,48,256]{4,3,2,1,0:T(8,128)(2,1)} %broadcast_in_dim.2), calls=%async_computation | async-start | bytes 3145728 | tf_op jit(solution)/shard_map/all_to_all | solution.py:153
  37.9 7.3 %collective-permute-start.3 = (bf16[32,4096]{1,0:T(8,128)(2,1)S(1)}, bf16[32,4096]{1,0:T(8,128)(2,1)S(1)}, u32[]{:S(2)}, u32[]{:S(2)}) collective-permute-start(bf16[32,4096]{1,0:T(8,128)(2,1)S(1)} %collective-permute-done.1.refs_2_), channel_id=1, source_target_pairs={{0,2},{1,271},{2,4},{3,1},{4,6},{5,3},{6,8},{7,5},{8,10},{9,7},{10... | collective-permute-start | bytes 786440 | tf_op jit(solution)/shard_map/ppermute | solution.py:28
  45.2 1.9 %collective-permute-start.5 = (bf16[32,4096]{1,0:T(8,128)(2,1)S(1)}, bf16[32,4096]{1,0:T(8,128)(2,1)S(1)}, u32[]{:S(2)}, u32[]{:S(2)}) collective-permute-start(bf16[32,4096]{1,0:T(8,128)(2,1)S(1)} %collective-permute-done.2.refs_3_), channel_id=1, source_target_pairs={{0,270},{1,3},{2,0},{3,5},{4,2},{5,7},{6,4},{7,9},{8,6},{9,11},{10... | collective-permute-start | bytes 786440 | tf_op jit(solution)/shard_map/ppermute | solution.py:28
  47.1 2.9 %collective-permute-start.8 = (bf16[4096,256]{1,0:T(8,128)(2,1)}, bf16[4096,256]{1,0:T(8,128)(2,1)}, u32[]{:S(2)}, u32[]{:S(2)}) collective-permute-start(bf16[4096,256]{1,0:T(8,128)(2,1)} %refs_5_.1), channel_id=1, source_target_pairs={{0,1},{1,0},{2,3},{3,2},{4,5},{5,4},{6,7},{7,6},{8,9},{9,8},{10,11... | collective-permute-start | bytes 6291464 | tf_op jit(solution)/shard_map/ppermute | solution.py:159
  50.1 1.9 %collective-permute-start.9 = (bf16[256,4096]{1,0:T(8,128)(2,1)}, bf16[256,4096]{1,0:T(8,128)(2,1)}, u32[]{:S(2)}, u32[]{:S(2)}) collective-permute-start(bf16[256,4096]{1,0:T(8,128)(2,1)} %refs_7_.1), channel_id=1, source_target_pairs={{0,1},{1,0},{2,3},{3,2},{4,5},{5,4},{6,7},{7,6},{8,9},{9,8},{10,11... | collective-permute-start | bytes 6291464 | tf_op jit(solution)/shard_map/ppermute | solution.py:160
  52.0 4.1 %collective-permute-start.4 = (bf16[32,4096]{1,0:T(8,128)(2,1)S(1)}, bf16[32,4096]{1,0:T(8,128)(2,1)S(1)}, u32[]{:S(2)}, u32[]{:S(2)}) collective-permute-start(bf16[32,4096]{1,0:T(8,128)(2,1)S(1)} %collective-permute-done.3.refs_0_), channel_id=1, source_target_pairs={{0,2},{1,271},{2,4},{3,1},{4,6},{5,3},{6,8},{7,5},{8,10},{9,7},{10... | collective-permute-start | bytes 786440 | tf_op jit(solution)/shard_map/ppermute | solution.py:28
  59.4 5.7 %collective-permute-done.6.refs_1_ = bf16[32,4096]{1,0:T(8,128)(2,1)S(1)} collective-permute-done((bf16[32,4096]{1,0:T(8,128)(2,1)S(1)}, bf16[32,4096]{1,0:T(8,128)(2,1)S(1)}, u32[]{:S(2)}, u32[]{:S(2)}) %collective-permute-start.6) | collective-permute-done | bytes 262176 | tf_op jit(solution)/shard_map/ppermute | solution.py:28
  69.1 4.9 %collective-permute-start.7 = (bf16[32,4096]{1,0:T(8,128)(2,1)}, bf16[32,4096]{1,0:T(8,128)(2,1)S(1)}, u32[]{:S(2)}, u32[]{:S(2)}) collective-permute-start(bf16[32,4096]{1,0:T(8,128)(2,1)} %copy-done.9), channel_id=1, source_target_pairs={{0,2},{1,271},{2,4},{3,1},{4,6},{5,3},{6,8},{7,5},{8,10},{9,7},{10... | collective-permute-start | bytes 786440 | tf_op jit(solution)/shard_map/ppermute | solution.py:28
  79.2 5.3 %attend2.1 = bf16[64,4096]{1,0:T(8,128)(2,1)S(1)} custom-call(bf16[32,4096]{1,0:T(8,128)(2,1)S(1)} %copy-done.10, bf16[32,4096]{1,0:T(8,128)(2,1)S(1)} %copy-done.12, bf16[4096,256]{1,0:T(8,128)(2,1)S(1)} %copy-done, bf16[4096,256]{1,0:T(8,128)(2,1)} %collective-permute-done.8.refs_2_.refs_3_.refs_6_, bf16[256,4096]{1,0:T(8,128)(2,1)S(1)} %copy-done.1, ...), custom_call_target="tpu_custom_call" | custom-call | flops 805306368 | bytes 12582912 | tf_op jit(solution)/shard_map/attend2/pallas_call | solution.py:110
  84.5 2.1 %collective-permute-start.12 = (bf16[32,4096]{1,0:T(8,128)(2,1)S(1)}, bf16[32,4096]{1,0:T(8,128)(2,1)S(1)}, u32[]{:S(2)}, u32[]{:S(2)}) collective-permute-start(bf16[32,4096]{1,0:T(8,128)(2,1)S(1)} %slice.47), channel_id=1, source_target_pairs={{0,2},{1,271},{2,4},{3,1},{4,6},{5,3},{6,8},{7,5},{8,10},{9,7},{10... | collective-permute-start | bytes 786440 | tf_op jit(solution)/shard_map/ppermute | solution.py:28
  86.6 5.1 %attend1.1 = bf16[32,4096]{1,0:T(8,128)(2,1)S(1)} custom-call(bf16[32,4096]{1,0:T(8,128)(2,1)S(1)} %collective-permute-done.7.refs_0_, bf16[4096,256]{1,0:T(8,128)(2,1)S(1)} %copy-done, bf16[4096,256]{1,0:T(8,128)(2,1)} %collective-permute-done.8.refs_2_.refs_3_.refs_6_, bf16[256,4096]{1,0:T(8,128)(2,1)S(1)} %copy-done.1, ...), custom_call_target="tpu_custom_call" | custom-call | flops 402653184 | bytes 12582912 | tf_op jit(solution)/shard_map/attend1/pallas_call | solution.py:110
  91.7 3.4 %collective-permute-start.11 = (bf16[32,4096]{1,0:T(8,128)(2,1)S(1)}, bf16[32,4096]{1,0:T(8,128)(2,1)S(1)}, u32[]{:S(2)}, u32[]{:S(2)}) collective-permute-start(bf16[32,4096]{1,0:T(8,128)(2,1)S(1)} %attend1.1), channel_id=1, source_target_pairs={{0,270},{1,3},{2,0},{3,5},{4,2},{5,7},{6,4},{7,9},{8,6},{9,11},{10... | collective-permute-start | bytes 786440 | tf_op jit(solution)/shard_map/ppermute | solution.py:28
  95.1 6.4 %attend5.1 = bf16[160,4096]{1,0:T(8,128)(2,1)S(1)} custom-call(bf16[32,4096]{1,0:T(8,128)(2,1)S(1)} %copy-done.6, bf16[32,4096]{1,0:T(8,128)(2,1)S(1)} %copy-done.8, bf16[32,4096]{1,0:T(8,128)(2,1)S(1)} %collective-permute-done.1.refs_2_, bf16[32,4096]{1,0:T(8,128)(2,1)S(1)} %copy-done.4, bf16[32,4096]{1,0:T(8,128)(2,1)S(1)} %copy-done.2, ...), custom_call_target="tpu_custom_call" | custom-call | flops 2013265920 | bytes 12582912 | tf_op jit(solution)/shard_map/attend5/pallas_call | solution.py:110
  101.5 3.1 %collective-permute-start.14 = (bf16[32,4096]{1,0:T(8,128)(2,1)S(1)}, bf16[32,4096]{1,0:T(8,128)(2,1)S(1)}, u32[]{:S(2)}, u32[]{:S(2)}) collective-permute-start(bf16[32,4096]{1,0:T(8,128)(2,1)S(1)} %add_convert_fusion.4), channel_id=1, source_target_pairs={{0,2},{1,271},{2,4},{3,1},{4,6},{5,3},{6,8},{7,5},{8,10},{9,7},{10... | collective-permute-start | bytes 786440 | tf_op jit(solution)/shard_map/ppermute | solution.py:28
  104.7 2.2 %collective-permute-start.13 = (bf16[32,4096]{1,0:T(8,128)(2,1)S(1)}, bf16[32,4096]{1,0:T(8,128)(2,1)S(1)}, u32[]{:S(2)}, u32[]{:S(2)}) collective-permute-start(bf16[32,4096]{1,0:T(8,128)(2,1)S(1)} %add_convert_fusion.5), channel_id=1, source_target_pairs={{0,270},{1,3},{2,0},{3,5},{4,2},{5,7},{6,4},{7,9},{8,6},{9,11},{10... | collective-permute-start | bytes 786440 | tf_op jit(solution)/shard_map/ppermute | solution.py:28
  106.9 3.1 %collective-permute-done.14 = bf16[32,4096]{1,0:T(8,128)(2,1)S(1)} collective-permute-done((bf16[32,4096]{1,0:T(8,128)(2,1)S(1)}, bf16[32,4096]{1,0:T(8,128)(2,1)S(1)}, u32[]{:S(2)}, u32[]{:S(2)}) %collective-permute-start.14) | collective-permute-done | bytes 262176 | tf_op jit(solution)/shard_map/ppermute | solution.py:28
  110.0 3.1 %collective-permute-done.13 = bf16[32,4096]{1,0:T(8,128)(2,1)S(1)} collective-permute-done((bf16[32,4096]{1,0:T(8,128)(2,1)S(1)}, bf16[32,4096]{1,0:T(8,128)(2,1)S(1)}, u32[]{:S(2)}, u32[]{:S(2)}) %collective-permute-start.13) | collective-permute-done | bytes 262176 | tf_op jit(solution)/shard_map/ppermute | solution.py:28
  113.2 1.9 %collective-permute-start.15 = (bf16[32,4096]{1,0:T(8,128)(2,1)S(1)}, bf16[32,4096]{1,0:T(8,128)(2,1)S(1)}, u32[]{:S(2)}, u32[]{:S(2)}) collective-permute-start(bf16[32,4096]{1,0:T(8,128)(2,1)S(1)} %get-tuple-element.36), channel_id=1, source_target_pairs={{0,270},{1,3},{2,0},{3,5},{4,2},{5,7},{6,4},{7,9},{8,6},{9,11},{10... | collective-permute-start | bytes 786440 | tf_op jit(solution)/shard_map/ppermute | solution.py:28
  115.1 4.6 %collective-permute-start.16 = (bf16[32,4096]{1,0:T(8,128)(2,1)S(1)}, bf16[32,4096]{1,0:T(8,128)(2,1)S(1)}, u32[]{:S(2)}, u32[]{:S(2)}) collective-permute-start(bf16[32,4096]{1,0:T(8,128)(2,1)S(1)} %get-tuple-element.35), channel_id=1, source_target_pairs={{0,2},{1,271},{2,4},{3,1},{4,6},{5,3},{6,8},{7,5},{8,10},{9,7},{10... | collective-permute-start | bytes 786440 | tf_op jit(solution)/shard_map/ppermute | solution.py:28
  121.5 2.3 %collective-permute-done.16 = bf16[32,4096]{1,0:T(8,128)(2,1)S(1)} collective-permute-done((bf16[32,4096]{1,0:T(8,128)(2,1)S(1)}, bf16[32,4096]{1,0:T(8,128)(2,1)S(1)}, u32[]{:S(2)}, u32[]{:S(2)}) %collective-permute-start.16) | collective-permute-done | bytes 262176 | tf_op jit(solution)/shard_map/ppermute | solution.py:28
  125.8 6.9 %collective-permute-done.17 = bf16[32,4096]{1,0:T(8,128)(2,1)S(1)} collective-permute-done((bf16[32,4096]{1,0:T(8,128)(2,1)S(1)}, bf16[32,4096]{1,0:T(8,128)(2,1)S(1)}, u32[]{:S(2)}, u32[]{:S(2)}) %collective-permute-start.17) | collective-permute-done | bytes 262176 | tf_op jit(solution)/shard_map/ppermute | solution.py:28
  (67 shorter events, 22.3 us)
Async XLA Ops:
  1.9 27.7 %collective-permute-start.1 = (bf16[32,4096]{1,0:T(8,128)(2,1)}, bf16[32,4096]{1,0:T(8,128)(2,1)S(1)}, u32[]{:S(2)}, u32[]{:S(2)}) collective-permute-start(bf16[32,4096]{1,0:T(8,128)(2,1)} %get-tuple-element.21.refs_4_), channel_id=1, source_target_pairs={{0,2},{1,271},{2,4},{3,1},{4,6},{5,3},{6,8},{7,5},{8,10},{9,7},{10... | collective-permute-start | bytes 786440 | tf_op jit(solution)/shard_map/ppermute | solution.py:28
  13.8 15.8 %collective-permute-start.2 = (bf16[32,4096]{1,0:T(8,128)(2,1)}, bf16[32,4096]{1,0:T(8,128)(2,1)S(1)}, u32[]{:S(2)}, u32[]{:S(2)}) collective-permute-start(bf16[32,4096]{1,0:T(8,128)(2,1)} %get-tuple-element.21.refs_4_), channel_id=1, source_target_pairs={{0,270},{1,3},{2,0},{3,5},{4,2},{5,7},{6,4},{7,9},{8,6},{9,11},{10... | collective-permute-start | bytes 786440 | tf_op jit(solution)/shard_map/ppermute | solution.py:28
  15.7 13.8 %collective-permute-start = (bf16[112,256]{1,0:T(8,128)(2,1)}, bf16[112,256]{1,0:T(8,128)(2,1)S(1)}, u32[]{:S(2)}, u32[]{:S(2)}) collective-permute-start(bf16[112,256]{1,0:T(8,128)(2,1)} %get-tuple-element.20), channel_id=1, source_target_pairs={{0,256},{256,0},{1,257},{257,1},{2,258},{258,2},{3,259},{259,3},{4... | collective-permute-start | bytes 172040 | tf_op jit(solution)/shard_map/ppermute | solution.py:149
  29.6 15.6 %copy-start.3 = (bf16[32,4096]{1,0:T(8,128)(2,1)}, bf16[32,4096]{1,0:T(8,128)(2,1)S(1)}, u32[]{:S(2)}) copy-start(bf16[32,4096]{1,0:T(8,128)(2,1)S(1)} %collective-permute-done.2.refs_3_) | copy-start | bytes 786436
  31.0 37.9 %copy-start.13 = (s32[512,1]{0,1:T(1,128)S(1)}, s32[512,1]{0,1:T(1,128)}, u32[]{:S(2)}) copy-start(s32[512,1]{0,1:T(1,128)} %param.15) | copy-start | bytes 6148
  31.0 34.8 %all-to-all-start = ((bf16[16,2,2,48,256]{4,3,2,1,0:T(8,128)(2,1)}), bf16[16,2,2,48,256]{4,3,2,1,0:T(8,128)(2,1)S(1)}, u32[]{:S(2)}, u32[]{:S(2)}) async-start(bf16[16,2,2,48,256]{4,3,2,1,0:T(8,128)(2,1)} %broadcast_in_dim.2), calls=%async_computation | async-start | bytes 3145728 | tf_op jit(solution)/shard_map/all_to_all | solution.py:153
  37.9 14.1 %collective-permute-start.3 = (bf16[32,4096]{1,0:T(8,128)(2,1)S(1)}, bf16[32,4096]{1,0:T(8,128)(2,1)S(1)}, u32[]{:S(2)}, u32[]{:S(2)}) collective-permute-start(bf16[32,4096]{1,0:T(8,128)(2,1)S(1)} %collective-permute-done.1.refs_2_), channel_id=1, source_target_pairs={{0,2},{1,271},{2,4},{3,1},{4,6},{5,3},{6,8},{7,5},{8,10},{9,7},{10... | collective-permute-start | bytes 786440 | tf_op jit(solution)/shard_map/ppermute | solution.py:28
  45.2 11.6 %collective-permute-start.5 = (bf16[32,4096]{1,0:T(8,128)(2,1)S(1)}, bf16[32,4096]{1,0:T(8,128)(2,1)S(1)}, u32[]{:S(2)}, u32[]{:S(2)}) collective-permute-start(bf16[32,4096]{1,0:T(8,128)(2,1)S(1)} %collective-permute-done.2.refs_3_), channel_id=1, source_target_pairs={{0,270},{1,3},{2,0},{3,5},{4,2},{5,7},{6,4},{7,9},{8,6},{9,11},{10... | collective-permute-start | bytes 786440 | tf_op jit(solution)/shard_map/ppermute | solution.py:28
  47.1 26.9 %collective-permute-start.8 = (bf16[4096,256]{1,0:T(8,128)(2,1)}, bf16[4096,256]{1,0:T(8,128)(2,1)}, u32[]{:S(2)}, u32[]{:S(2)}) collective-permute-start(bf16[4096,256]{1,0:T(8,128)(2,1)} %refs_5_.1), channel_id=1, source_target_pairs={{0,1},{1,0},{2,3},{3,2},{4,5},{5,4},{6,7},{7,6},{8,9},{9,8},{10,11... | collective-permute-start | bytes 6291464 | tf_op jit(solution)/shard_map/ppermute | solution.py:159
  50.1 24.0 %collective-permute-start.9 = (bf16[256,4096]{1,0:T(8,128)(2,1)}, bf16[256,4096]{1,0:T(8,128)(2,1)}, u32[]{:S(2)}, u32[]{:S(2)}) collective-permute-start(bf16[256,4096]{1,0:T(8,128)(2,1)} %refs_7_.1), channel_id=1, source_target_pairs={{0,1},{1,0},{2,3},{3,2},{4,5},{5,4},{6,7},{7,6},{8,9},{9,8},{10,11... | collective-permute-start | bytes 6291464 | tf_op jit(solution)/shard_map/ppermute | solution.py:160
  52.0 7.4 %collective-permute-start.4 = (bf16[32,4096]{1,0:T(8,128)(2,1)S(1)}, bf16[32,4096]{1,0:T(8,128)(2,1)S(1)}, u32[]{:S(2)}, u32[]{:S(2)}) collective-permute-start(bf16[32,4096]{1,0:T(8,128)(2,1)S(1)} %collective-permute-done.3.refs_0_), channel_id=1, source_target_pairs={{0,2},{1,271},{2,4},{3,1},{4,6},{5,3},{6,8},{7,5},{8,10},{9,7},{10... | collective-permute-start | bytes 786440 | tf_op jit(solution)/shard_map/ppermute | solution.py:28
  56.8 8.3 %collective-permute-start.6 = (bf16[32,4096]{1,0:T(8,128)(2,1)S(1)}, bf16[32,4096]{1,0:T(8,128)(2,1)S(1)}, u32[]{:S(2)}, u32[]{:S(2)}) collective-permute-start(bf16[32,4096]{1,0:T(8,128)(2,1)S(1)} %collective-permute-done.5.refs_1_), channel_id=1, source_target_pairs={{0,270},{1,3},{2,0},{3,5},{4,2},{5,7},{6,4},{7,9},{8,6},{9,11},{10... | collective-permute-start | bytes 786440 | tf_op jit(solution)/shard_map/ppermute | solution.py:28
  65.8 8.2 %collective-permute-start.10 = (bf16[16,2,2,48,256]{4,3,2,1,0:T(8,128)(2,1)S(1)}, bf16[16,2,2,48,256]{4,3,2,1,0:T(8,128)(2,1)S(1)}, u32[]{:S(2)}, u32[]{:S(2)}) collective-permute-start(bf16[16,2,2,48,256]{4,3,2,1,0:T(8,128)(2,1)S(1)} %all-to-all-done.refs_5_.refs_6_.refs_9_), channel_id=1, source_target_pairs={{0,1},{1,0},{2,3},{3,2},{4,5},{5,4},{6,7},{7,6},{8,9},{9,8},{10,11... | collective-permute-start | bytes 4718600 | tf_op jit(solution)/shard_map/ppermute | solution.py:158
  69.1 17.5 %collective-permute-start.7 = (bf16[32,4096]{1,0:T(8,128)(2,1)}, bf16[32,4096]{1,0:T(8,128)(2,1)S(1)}, u32[]{:S(2)}, u32[]{:S(2)}) collective-permute-start(bf16[32,4096]{1,0:T(8,128)(2,1)} %copy-done.9), channel_id=1, source_target_pairs={{0,2},{1,271},{2,4},{3,1},{4,6},{5,3},{6,8},{7,5},{8,10},{9,7},{10... | collective-permute-start | bytes 786440 | tf_op jit(solution)/shard_map/ppermute | solution.py:28
  84.5 10.5 %copy-start.2 = (bf16[32,4096]{1,0:T(8,128)(2,1)S(1)}, bf16[32,4096]{1,0:T(8,128)(2,1)}, u32[]{:S(2)}) copy-start(bf16[32,4096]{1,0:T(8,128)(2,1)} %get-tuple-element.21.refs_4_) | copy-start | bytes 786436
  84.5 10.5 %copy-start.4 = (bf16[32,4096]{1,0:T(8,128)(2,1)S(1)}, bf16[32,4096]{1,0:T(8,128)(2,1)}, u32[]{:S(2)}) copy-start(bf16[32,4096]{1,0:T(8,128)(2,1)} %copy-done.3) | copy-start | bytes 786436
  84.5 10.5 %copy-start.6 = (bf16[32,4096]{1,0:T(8,128)(2,1)S(1)}, bf16[32,4096]{1,0:T(8,128)(2,1)}, u32[]{:S(2)}) copy-start(bf16[32,4096]{1,0:T(8,128)(2,1)} %copy-done.5) | copy-start | bytes 786436
  84.5 16.9 %collective-permute-start.12 = (bf16[32,4096]{1,0:T(8,128)(2,1)S(1)}, bf16[32,4096]{1,0:T(8,128)(2,1)S(1)}, u32[]{:S(2)}, u32[]{:S(2)}) collective-permute-start(bf16[32,4096]{1,0:T(8,128)(2,1)S(1)} %slice.47), channel_id=1, source_target_pairs={{0,2},{1,271},{2,4},{3,1},{4,6},{5,3},{6,8},{7,5},{8,10},{9,7},{10... | collective-permute-start | bytes 786440 | tf_op jit(solution)/shard_map/ppermute | solution.py:28
  91.7 9.8 %collective-permute-start.11 = (bf16[32,4096]{1,0:T(8,128)(2,1)S(1)}, bf16[32,4096]{1,0:T(8,128)(2,1)S(1)}, u32[]{:S(2)}, u32[]{:S(2)}) collective-permute-start(bf16[32,4096]{1,0:T(8,128)(2,1)S(1)} %attend1.1), channel_id=1, source_target_pairs={{0,270},{1,3},{2,0},{3,5},{4,2},{5,7},{6,4},{7,9},{8,6},{9,11},{10... | collective-permute-start | bytes 786440 | tf_op jit(solution)/shard_map/ppermute | solution.py:28
  101.5 8.4 %collective-permute-start.14 = (bf16[32,4096]{1,0:T(8,128)(2,1)S(1)}, bf16[32,4096]{1,0:T(8,128)(2,1)S(1)}, u32[]{:S(2)}, u32[]{:S(2)}) collective-permute-start(bf16[32,4096]{1,0:T(8,128)(2,1)S(1)} %add_convert_fusion.4), channel_id=1, source_target_pairs={{0,2},{1,271},{2,4},{3,1},{4,6},{5,3},{6,8},{7,5},{8,10},{9,7},{10... | collective-permute-start | bytes 786440 | tf_op jit(solution)/shard_map/ppermute | solution.py:28
  104.7 8.3 %collective-permute-start.13 = (bf16[32,4096]{1,0:T(8,128)(2,1)S(1)}, bf16[32,4096]{1,0:T(8,128)(2,1)S(1)}, u32[]{:S(2)}, u32[]{:S(2)}) collective-permute-start(bf16[32,4096]{1,0:T(8,128)(2,1)S(1)} %add_convert_fusion.5), channel_id=1, source_target_pairs={{0,270},{1,3},{2,0},{3,5},{4,2},{5,7},{6,4},{7,9},{8,6},{9,11},{10... | collective-permute-start | bytes 786440 | tf_op jit(solution)/shard_map/ppermute | solution.py:28
  113.2 8.3 %collective-permute-start.15 = (bf16[32,4096]{1,0:T(8,128)(2,1)S(1)}, bf16[32,4096]{1,0:T(8,128)(2,1)S(1)}, u32[]{:S(2)}, u32[]{:S(2)}) collective-permute-start(bf16[32,4096]{1,0:T(8,128)(2,1)S(1)} %get-tuple-element.36), channel_id=1, source_target_pairs={{0,270},{1,3},{2,0},{3,5},{4,2},{5,7},{6,4},{7,9},{8,6},{9,11},{10... | collective-permute-start | bytes 786440 | tf_op jit(solution)/shard_map/ppermute | solution.py:28
  115.1 8.7 %collective-permute-start.16 = (bf16[32,4096]{1,0:T(8,128)(2,1)S(1)}, bf16[32,4096]{1,0:T(8,128)(2,1)S(1)}, u32[]{:S(2)}, u32[]{:S(2)}) collective-permute-start(bf16[32,4096]{1,0:T(8,128)(2,1)S(1)} %get-tuple-element.35), channel_id=1, source_target_pairs={{0,2},{1,271},{2,4},{3,1},{4,6},{5,3},{6,8},{7,5},{8,10},{9,7},{10... | collective-permute-start | bytes 786440 | tf_op jit(solution)/shard_map/ppermute | solution.py:28
  123.9 8.8 %collective-permute-start.17 = (bf16[32,4096]{1,0:T(8,128)(2,1)S(1)}, bf16[32,4096]{1,0:T(8,128)(2,1)S(1)}, u32[]{:S(2)}, u32[]{:S(2)}) collective-permute-start(bf16[32,4096]{1,0:T(8,128)(2,1)S(1)} %add_convert_fusion.1), channel_id=1, source_target_pairs={{0,270},{1,3},{2,0},{3,5},{4,2},{5,7},{6,4},{7,9},{8,6},{9,11},{10... | collective-permute-start | bytes 786440 | tf_op jit(solution)/shard_map/ppermute | solution.py:28
  (9 other events, 23.5 us)

commit v4 on v3

v4 whole, which is shorter than its diff:
```python
import functools

import jax
import jax.numpy as jnp
from jax import lax
from jax.experimental import pallas as pl
from jax.experimental.pallas import tpu as pltpu
from jax.sharding import Mesh, PartitionSpec as P

HEAD_DIM = 128
EPSILON = 1e-06
MASKED = -1e30
LIMIT = 48
STEPS = (4, 3, -3, 2, -2, 1, -1, 0)
RING = ("zh", "zl")
SWAP = [(0, 1), (1, 0)]
VMEM = pl.BlockSpec(memory_space=pltpu.VMEM)
HELD = pl.BlockSpec(memory_space=pltpu.HBM)


def opposite(step):
    return [
        (2 * i + c, 2 * ((i + (step if c == 0 else -step)) % 16) + c)
        for i in range(16)
        for c in range(2)
    ]


def along(x, step):
    return lax.ppermute(x, RING + ("c",), opposite(step))


def prepare_kernel(tokens, gain, keys, values, pos, normed, payload):
    hidden = tokens[...].astype(jnp.float32)
    factor = lax.rsqrt(jnp.mean(hidden * hidden, axis=-1, keepdims=True) + EPSILON)
    normed[...] = (hidden * factor * gain[...]).astype(jnp.bfloat16)
    payload[0:48, :] = keys[...]
    payload[48:96, :] = values[...]
    place = jnp.concatenate([pos[:, 32 * i : 32 * i + 32] for i in range(16)], axis=0)
    high = lax.shift_right_logical(place, 3)
    low = place - high * 8
    gap = jnp.zeros((16, 96), jnp.int32)
    parts = jnp.concatenate([high, gap, low, gap], axis=1)
    payload[96:112, :] = parts.astype(jnp.float32).astype(jnp.bfloat16)


def pack_kernel(frame_pad, mine, theirs, spread, bound):
    for i in range(16):
        for part in range(2):
            for half, source in enumerate((mine, theirs)):
                spread[i, part, half] = source[48 * part : 48 * part + 48, :]
    zh, zl, core = (lax.axis_index(a) for a in ("zh", "zl", "c"))
    places = []
    for source in (mine, theirs):
        parts = source[96:112, :].astype(jnp.float32)
        places.append(parts[:, 0:32] * 8.0 + parts[:, 128:160])
    row = lax.broadcasted_iota(jnp.int32, (16, 32), 0)
    found = []
    for step in STEPS:
        z = (zh * 8 + zl + step * (2 * core - 1) + 16) % 16
        place = jnp.where(z // 8 == zh, places[0], places[1])
        place = jnp.where(row == z % 8 * 2 + core, place, 0.0)
        found.append(jnp.sum(place, axis=0, keepdims=True))
    last = (1535 - frame_pad[0]).astype(jnp.float32)
    bound[...] = jnp.minimum(jnp.concatenate(found, axis=1), last)


def attend_kernel(count, first, *refs):
    blocks, outs = refs[:count], refs[count + 7 : 2 * count + 7]
    held, sem = refs[2 * count + 7 : 2 * count + 11], refs[-1]
    copies = [pltpu.make_async_copy(refs[count + i], held[i], sem.at[i]) for i in range(4)]
    for copy in copies:
        copy.start()
    wq, wo, kv = held[:2], held[2:], refs[count + 4 : count + 6]
    bound = refs[count + 6]
    rows = 32 * count
    x = jnp.concatenate([b[...] for b in blocks], axis=0)
    column = jnp.transpose(jnp.broadcast_to(bound[...], (8, 256)))
    column = column[first : first + rows, 0:1]
    zh = lax.axis_index("zh")
    index = lax.broadcasted_iota(jnp.int32, (1, 1536), 1)
    shard = lax.shift_right_logical(index * 1366, 16)
    half = (shard & 1) ^ zh
    frame = half * 768 + lax.shift_right_logical(shard, 1) * 48 + (index - shard * 48)
    bias = jnp.where(frame.astype(jnp.float32) <= column, 0.0, MASKED)
    groups = []
    for g in range(2):
        copies[g].wait()
        q = jnp.dot(x, wq[g][...], preferred_element_type=jnp.float32)
        q = (q * HEAD_DIM**-0.5).astype(jnp.bfloat16)
        heads = []
        for h in range(2):
            cols = slice(h * HEAD_DIM, (h + 1) * HEAD_DIM)
            s = [
                lax.dot_general(
                    q[:, cols],
                    kv[g][4 * t : 4 * t + 4, 0, :, :, cols].reshape(384, HEAD_DIM),
                    (((1,), (1,)), ((), ())),
                    preferred_element_type=jnp.float32,
                )
                for t in range(4)
            ]
            s = jnp.concatenate(s, axis=1) + bias
            e = jnp.exp(s - jnp.max(s, axis=1, keepdims=True))
            total = jnp.sum(e, axis=1, keepdims=True)
            e = e.astype(jnp.bfloat16)
            a = sum(
                jnp.dot(
                    e[:, t * 384 : (t + 1) * 384],
                    kv[g][4 * t : 4 * t + 4, 1, :, :, cols].reshape(384, HEAD_DIM),
                    preferred_element_type=jnp.float32,
                )
                for t in range(4)
            )
            heads.append((a / total).astype(jnp.bfloat16))
        groups.append(jnp.concatenate(heads, axis=1))
    copies[2].wait()
    copies[3].wait()
    for n in range(0, 4096, 1024):
        cols = slice(n, n + 1024)
        total = jnp.dot(groups[0], wo[0][:, cols], preferred_element_type=jnp.float32)
        total += jnp.dot(groups[1], wo[1][:, cols], preferred_element_type=jnp.float32)
        total = total.astype(jnp.bfloat16)
        for i in range(count):
            outs[i][:, cols] = total[32 * i : 32 * i + 32, :]


def attend(blocks, first, wq, wo, kv, bound):
    count = len(blocks)
    rows = 32 * count
    return pl.pallas_call(
        functools.partial(attend_kernel, count, first),
        out_shape=[jax.ShapeDtypeStruct((32, 4096), jnp.bfloat16)] * count,
        in_specs=[VMEM] * count + [HELD] * 4 + [VMEM] * 3,
        out_specs=[VMEM] * count,
        scratch_shapes=[pltpu.VMEM((4096, 256), jnp.bfloat16)] * 2
        + [pltpu.VMEM((256, 4096), jnp.bfloat16)] * 2
        + [pltpu.SemaphoreType.DMA((4,))],
        compiler_params=pltpu.CompilerParams(vmem_limit_bytes=LIMIT * 2**20),
        cost_estimate=pl.CostEstimate(
            flops=rows * 12 * 2**20, bytes_accessed=12 * 2**20, transcendentals=rows * 6144
        ),
        name="attend%d" % count,
    )(*blocks, *wq, *wo, *kv, bound)


def per_device(tokens, gain, wq, wo, keys, values, token_pos, frame_pad):
    rows = tokens.shape[0]
    pos = token_pos.T
    own, mine = pl.pallas_call(
        prepare_kernel,
        out_shape=(
            jax.ShapeDtypeStruct((rows, 4096), jnp.bfloat16),
            jax.ShapeDtypeStruct((112, 256), jnp.bfloat16),
        ),
        in_specs=[VMEM] * 5,
        out_specs=(VMEM, VMEM),
        name="prepare",
    )(tokens.reshape(rows, 4096), gain.reshape(1, 4096), keys.reshape(48, 256), values.reshape(48, 256), pos)

    a1, b1 = along(own, 1), along(own, -1)

    theirs = lax.ppermute(mine, "zh", SWAP)
    theirs, a1, b1 = lax.optimization_barrier((theirs, a1, b1))
    wq_other = lax.ppermute(wq, "c", SWAP)
    wo_other = lax.ppermute(wo, "c", SWAP)
    kv, bound = pl.pallas_call(
        pack_kernel,
        out_shape=(
            jax.ShapeDtypeStruct((16, 2, 2, 48, 256), jnp.bfloat16),
            jax.ShapeDtypeStruct((1, 256), jnp.float32),
        ),
        in_specs=[pl.BlockSpec(memory_space=pltpu.SMEM), VMEM, VMEM],
        out_specs=(VMEM, VMEM),
        compiler_params=pltpu.CompilerParams(vmem_limit_bytes=8 * 2**20),
        name="pack",
    )(frame_pad, mine, theirs)
    kv = lax.all_to_all(kv, ("y", "x"), 0, 0, tiled=True)
    a2, b2 = along(a1, 1), along(b1, -1)
    a3, b3 = along(a2, 1), along(b2, -1)
    a4 = along(a2, 2)
    kv, a3, a4, b3 = lax.optimization_barrier((kv, a3, a4, b3))
    kv_other = lax.ppermute(kv, "c", SWAP)

    given = ((wq, wq_other), (wo, wo_other), (kv, kv_other), bound)
    far = attend([a4, a3, b3], 0, *given)
    near = attend([a2, b2, a1, b1, own], 96, *given)
    wide = lambda v: v.astype(jnp.float32)
    thin = lambda v: v.astype(jnp.bfloat16)
    plus = lambda u, v: thin(wide(u) + wide(v))
    ap, bp, mid = along(far[1], -1), along(far[2], 1), along(far[0], -2)
    ap, bp, mid, near = lax.optimization_barrier((ap, bp, mid, near))
    ap, bp = along(thin(wide(near[0]) + wide(ap) + wide(mid)), -1), along(plus(near[1], bp), 1)
    ap, bp = lax.optimization_barrier((ap, bp))
    ap, bp = along(plus(near[2], ap), -1), along(plus(near[3], bp), 1)
    out = wide(near[4]) + wide(ap) + wide(bp)
    return thin(out).reshape(rows, 1, 4096)


def solution(mesh):
    fine = Mesh(mesh.devices.reshape(2, 4, 4, 8, 2), ("zh", "y", "x", "zl", "c"))
    frame, tensor = ("zh", "y", "x"), ("zl", "c")
    placed = (
        P(frame + tensor, None, None),
        P(),
        P(None, tensor),
        P(tensor, None),
        P(frame, None, tensor),
        P(frame, None, tensor),
        P(frame, None),
        P(),
    )
    return jax.shard_map(
        per_device,
        mesh=fine,
        in_specs=placed,
        out_specs=P(frame + tensor, None, None),
        check_vma=False,
    )
```

time: 136 us -> 126 us (0.926); the launches traced: 133 us -> 125 us
  local copies, waits for them, and re-layouts: 9.72 us -> 0.82 us
  waiting for transfers between devices: 28.2 us -> 32.5 us
  Pallas kernels: 18.6 us -> 16.8 us
  starting transfers between devices: 74.4 us -> 73 us
    unnamed x29 -> x4, local copies, waits for them, and re-layouts: 7.23 us -> 0.82 us
    ppermute x14, starting transfers between devices: 53.1 us -> 49.2 us  [along(): return lax.ppermute(x, RING + ('c',), opposite(step))]
    ppermute x1, waiting for transfers between devices: 0.01 us -> 3.35 us  [per_device(): kv_other = lax.ppermute(kv, 'c', SWAP)]
    pallas_call x3 -> x2, Pallas kernels: 16.7 us -> 13.7 us  [attend(): pl.pallas_call(functools.partial(attend_kernel, count, first), out_shape=...]
    ppermute x14, waiting for transfers between devices: 22.8 us -> 24.9 us  [along(): return lax.ppermute(x, RING + ('c',), opposite(step))]
    ppermute x1, starting transfers between devices: 2.91 us -> 4.34 us  [per_device(): wq_other = lax.ppermute(wq, 'c', SWAP)]
  transfers between devices with their start and end apart: 19 -> 19, of which waited for: 7 -> 9; matrix products, arithmetic and copies ran while one was open for 1% -> 0% of each run, Pallas kernels for 13% -> 6%
where the time goes in v4:
time: 126 us; the launch traced here: 125 us
  starting transfers between devices  73 us (58%)
  waiting for transfers between devices  32.5 us (26%)
  Pallas kernels  16.8 us (13%)
    ppermute x14, starting transfers between devices, along(): return lax.ppermute(x, RING + ('c',), opposite(step))  49.2 us
    ppermute x14, waiting for transfers between devices, along(): return lax.ppermute(x, RING + ('c',), opposite(step))  24.9 us
    pallas_call x2, Pallas kernels, attend(): pl.pallas_call(functools.partial(attend_kernel, count, first), out_shape=...  13.7 us
    ppermute x1, starting transfers between devices, per_device(): theirs = lax.ppermute(mine, 'zh', SWAP)  8.89 us
    all_to_all x1, starting transfers between devices, per_device(): kv = lax.all_to_all(kv, ('y', 'x'), 0, 0, tiled=True)  6.75 us
    ppermute x1, starting transfers between devices, per_device(): wq_other = lax.ppermute(wq, 'c', SWAP)  4.34 us
    ppermute x1, waiting for transfers between devices, per_device(): theirs = lax.ppermute(mine, 'zh', SWAP)  4.3 us
    ppermute x1, waiting for transfers between devices, per_device(): kv_other = lax.ppermute(kv, 'c', SWAP)  3.35 us
  transfers between devices with their start and end apart: 19, of which 9 were waited for; matrix products, arithmetic and copies ran while one was open for 0% of the time, Pallas kernels for 6%

profile of v4, /device:TPU:1, one launch (start us, length us, event | category | flops | bytes accessed | tf_op | source)
XLA Modules:
  0.0 125.2 jit_solution(3427729648826682576)
XLA Ops:
  1.9 4.4 %collective-permute-start.2 = (bf16[32,4096]{1,0:T(8,128)(2,1)}, bf16[32,4096]{1,0:T(8,128)(2,1)S(1)}, u32[]{:S(2)}, u32[]{:S(2)}) collective-permute-start(bf16[32,4096]{1,0:T(8,128)(2,1)} %get-tuple-element.35.refs_4_), channel_id=1, source_target_pairs={{0,270},{1,3},{2,0},{3,5},{4,2},{5,7},{6,4},{7,9},{8,6},{9,11},{10... | collective-permute-start | bytes 786440 | tf_op jit(solution)/shard_map/ppermute | solution.py:30
  6.2 9.5 %collective-permute-start.1 = (bf16[32,4096]{1,0:T(8,128)(2,1)}, bf16[32,4096]{1,0:T(8,128)(2,1)S(1)}, u32[]{:S(2)}, u32[]{:S(2)}) collective-permute-start(bf16[32,4096]{1,0:T(8,128)(2,1)} %get-tuple-element.35.refs_4_), channel_id=1, source_target_pairs={{0,2},{1,271},{2,4},{3,1},{4,6},{5,3},{6,8},{7,5},{8,10},{9,7},{10... | collective-permute-start | bytes 786440 | tf_op jit(solution)/shard_map/ppermute | solution.py:30
  15.7 8.9 %collective-permute-start = (bf16[112,256]{1,0:T(8,128)(2,1)}, bf16[112,256]{1,0:T(8,128)(2,1)S(1)}, u32[]{:S(2)}, u32[]{:S(2)}) collective-permute-start(bf16[112,256]{1,0:T(8,128)(2,1)} %get-tuple-element.34.mine), channel_id=1, source_target_pairs={{0,256},{256,0},{1,257},{257,1},{2,258},{258,2},{3,259},{259,3},{4... | collective-permute-start | bytes 172040 | tf_op jit(solution)/shard_map/ppermute | solution.py:163
  25.3 4.3 %collective-permute-done.theirs = bf16[112,256]{1,0:T(8,128)(2,1)S(1)} collective-permute-done((bf16[112,256]{1,0:T(8,128)(2,1)}, bf16[112,256]{1,0:T(8,128)(2,1)S(1)}, u32[]{:S(2)}, u32[]{:S(2)}) %collective-permute-start) | collective-permute-done | bytes 57376 | tf_op jit(solution)/shard_map/ppermute | solution.py:163
  31.7 6.8 %all-to-all-start = ((bf16[16,2,2,48,256]{4,3,2,1,0:T(8,128)(2,1)}), bf16[16,2,2,48,256]{4,3,2,1,0:T(8,128)(2,1)S(1)}, u32[]{:S(2)}, u32[]{:S(2)}) async-start(bf16[16,2,2,48,256]{4,3,2,1,0:T(8,128)(2,1)} %get-tuple-element.37), calls=%async_computation | async-start | bytes 3145728 | tf_op jit(solution)/shard_map/all_to_all | solution.py:178
  38.5 5.7 %collective-permute-start.3 = (bf16[32,4096]{1,0:T(8,128)(2,1)S(1)}, bf16[32,4096]{1,0:T(8,128)(2,1)S(1)}, u32[]{:S(2)}, u32[]{:S(2)}) collective-permute-start(bf16[32,4096]{1,0:T(8,128)(2,1)S(1)} %collective-permute-done.1.refs_2_), channel_id=1, source_target_pairs={{0,2},{1,271},{2,4},{3,1},{4,6},{5,3},{6,8},{7,5},{8,10},{9,7},{10... | collective-permute-start | bytes 786440 | tf_op jit(solution)/shard_map/ppermute | solution.py:30
  44.2 1.9 %collective-permute-start.6 = (bf16[32,4096]{1,0:T(8,128)(2,1)S(1)}, bf16[32,4096]{1,0:T(8,128)(2,1)S(1)}, u32[]{:S(2)}, u32[]{:S(2)}) collective-permute-start(bf16[32,4096]{1,0:T(8,128)(2,1)S(1)} %collective-permute-done.2.refs_3_), channel_id=1, source_target_pairs={{0,270},{1,3},{2,0},{3,5},{4,2},{5,7},{6,4},{7,9},{8,6},{9,11},{10... | collective-permute-start | bytes 786440 | tf_op jit(solution)/shard_map/ppermute | solution.py:30
  46.1 4.3 %collective-permute-start.8 = (bf16[4096,256]{1,0:T(8,128)(2,1)}, bf16[4096,256]{1,0:T(8,128)(2,1)}, u32[]{:S(2)}, u32[]{:S(2)}) collective-permute-start(bf16[4096,256]{1,0:T(8,128)(2,1)} %refs_5_.3), channel_id=1, source_target_pairs={{0,1},{1,0},{2,3},{3,2},{4,5},{5,4},{6,7},{7,6},{8,9},{9,8},{10,11... | collective-permute-start | bytes 6291464 | tf_op jit(solution)/shard_map/ppermute | solution.py:165
  50.5 1.9 %collective-permute-start.9 = (bf16[256,4096]{1,0:T(8,128)(2,1)}, bf16[256,4096]{1,0:T(8,128)(2,1)}, u32[]{:S(2)}, u32[]{:S(2)}) collective-permute-start(bf16[256,4096]{1,0:T(8,128)(2,1)} %refs_7_.1), channel_id=1, source_target_pairs={{0,1},{1,0},{2,3},{3,2},{4,5},{5,4},{6,7},{7,6},{8,9},{9,8},{10,11... | collective-permute-start | bytes 6291464 | tf_op jit(solution)/shard_map/ppermute | solution.py:166
  52.4 3.5 %collective-permute-start.5 = (bf16[32,4096]{1,0:T(8,128)(2,1)S(1)}, bf16[32,4096]{1,0:T(8,128)(2,1)S(1)}, u32[]{:S(2)}, u32[]{:S(2)}) collective-permute-start(bf16[32,4096]{1,0:T(8,128)(2,1)S(1)} %collective-permute-done.3.refs_0_), channel_id=1, source_target_pairs={{0,4},{1,269},{2,6},{3,271},{4,8},{5,1},{6,10},{7,3},{8,12},{9,5},... | collective-permute-start | bytes 786440 | tf_op jit(solution)/shard_map/ppermute | solution.py:30
  55.9 3.1 %collective-permute-start.4 = (bf16[32,4096]{1,0:T(8,128)(2,1)S(1)}, bf16[32,4096]{1,0:T(8,128)(2,1)S(1)}, u32[]{:S(2)}, u32[]{:S(2)}) collective-permute-start(bf16[32,4096]{1,0:T(8,128)(2,1)S(1)} %collective-permute-done.3.refs_0_), channel_id=1, source_target_pairs={{0,2},{1,271},{2,4},{3,1},{4,6},{5,3},{6,8},{7,5},{8,10},{9,7},{10... | collective-permute-start | bytes 786440 | tf_op jit(solution)/shard_map/ppermute | solution.py:30
  59.0 2.1 %collective-permute-start.7 = (bf16[32,4096]{1,0:T(8,128)(2,1)S(1)}, bf16[32,4096]{1,0:T(8,128)(2,1)S(1)}, u32[]{:S(2)}, u32[]{:S(2)}) collective-permute-start(bf16[32,4096]{1,0:T(8,128)(2,1)S(1)} %collective-permute-done.6.refs_1_), channel_id=1, source_target_pairs={{0,270},{1,3},{2,0},{3,5},{4,2},{5,7},{6,4},{7,9},{8,6},{9,11},{10... | collective-permute-start | bytes 786440 | tf_op jit(solution)/shard_map/ppermute | solution.py:30
  61.8 7.5 %collective-permute-done.4.refs_1_ = bf16[32,4096]{1,0:T(8,128)(2,1)S(1)} collective-permute-done((bf16[32,4096]{1,0:T(8,128)(2,1)S(1)}, bf16[32,4096]{1,0:T(8,128)(2,1)S(1)}, u32[]{:S(2)}, u32[]{:S(2)}) %collective-permute-start.4) | collective-permute-done | bytes 262176 | tf_op jit(solution)/shard_map/ppermute | solution.py:30
  71.3 3.4 %collective-permute-done.10.refs_8_.refs_10_ = bf16[16,2,2,48,256]{4,3,2,1,0:T(8,128)(2,1)S(1)} collective-permute-done((bf16[16,2,2,48,256]{4,3,2,1,0:T(8,128)(2,1)S(1)}, bf16[16,2,2,48,256]{4,3,2,1,0:T(8,128)(2,1)S(1)}, u32[]{:S(2)}, u32[]{:S(2)}) %collective-permute-start.10) | collective-permute-done | bytes 1572896 | tf_op jit(solution)/shard_map/ppermute | solution.py:183
  74.6 6.4 %attend3.1 = (bf16[32,4096]{1,0:T(8,128)(2,1)S(1)}, bf16[32,4096]{1,0:T(8,128)(2,1)S(1)}, bf16[32,4096]{1,0:T(8,128)(2,1)S(1)}) custom-call(bf16[32,4096]{1,0:T(8,128)(2,1)S(1)} %collective-permute-done.5.refs_0_, bf16[32,4096]{1,0:T(8,128)(2,1)S(1)} %collective-permute-done.4.refs_1_, bf16[32,4096]{1,0:T(8,128)(2,1)S(1)} %collective-permute-done.7.refs_2_, ...), custom_call_target="tpu_custom_call" | custom-call | flops 1207959552 | bytes 12582912 | tf_op jit(solution)/shard_map/attend3/pallas_call | solution.py:131
  83.0 4.6 %collective-permute-start.12 = (bf16[32,4096]{1,0:T(8,128)(2,1)S(1)}, bf16[32,4096]{1,0:T(8,128)(2,1)S(1)}, u32[]{:S(2)}, u32[]{:S(2)}) collective-permute-start(bf16[32,4096]{1,0:T(8,128)(2,1)S(1)} %get-tuple-element.46), channel_id=1, source_target_pairs={{0,2},{1,271},{2,4},{3,1},{4,6},{5,3},{6,8},{7,5},{8,10},{9,7},{10... | collective-permute-start | bytes 786440 | tf_op jit(solution)/shard_map/ppermute | solution.py:30
  89.5 7.2 %attend5.1 = (bf16[32,4096]{1,0:T(8,128)(2,1)S(1)}, bf16[32,4096]{1,0:T(8,128)(2,1)S(1)}, bf16[32,4096]{1,0:T(8,128)(2,1)S(1)}, bf16[32,4096]{1,0:T(8,128)(2,1)S(1)}, bf16[32,4096]{1,0:T(8,128)(2,1)S(1)}) custom-call(bf16[32,4096]{1,0:T(8,128)(2,1)S(1)} %collective-permute-done.3.refs_0_, bf16[32,4096]{1,0:T(8,128)(2,1)S(1)} %collective-permute-done.6.refs_1_, ...), custom_call_target="tpu_custom_call" | custom-call | flops 2013265920 | bytes 12582912 | tf_op jit(solution)/shard_map/attend5/pallas_call | solution.py:131
  96.7 2.7 %collective-permute-done.13 = bf16[32,4096]{1,0:T(8,128)(2,1)S(1)} collective-permute-done((bf16[32,4096]{1,0:T(8,128)(2,1)S(1)}, bf16[32,4096]{1,0:T(8,128)(2,1)S(1)}, u32[]{:S(2)}, u32[]{:S(2)}) %collective-permute-start.13) | collective-permute-done | bytes 262176 | tf_op jit(solution)/shard_map/ppermute | solution.py:30
  101.5 3.4 %collective-permute-start.14 = (bf16[32,4096]{1,0:T(8,128)(2,1)S(1)}, bf16[32,4096]{1,0:T(8,128)(2,1)S(1)}, u32[]{:S(2)}, u32[]{:S(2)}) collective-permute-start(bf16[32,4096]{1,0:T(8,128)(2,1)S(1)} %add_convert_fusion.4), channel_id=1, source_target_pairs={{0,270},{1,3},{2,0},{3,5},{4,2},{5,7},{6,4},{7,9},{8,6},{9,11},{10... | collective-permute-start | bytes 786440 | tf_op jit(solution)/shard_map/ppermute | solution.py:30
  106.6 5.8 %collective-permute-done.14 = bf16[32,4096]{1,0:T(8,128)(2,1)S(1)} collective-permute-done((bf16[32,4096]{1,0:T(8,128)(2,1)S(1)}, bf16[32,4096]{1,0:T(8,128)(2,1)S(1)}, u32[]{:S(2)}, u32[]{:S(2)}) %collective-permute-start.14) | collective-permute-done | bytes 262176 | tf_op jit(solution)/shard_map/ppermute | solution.py:30
  112.4 3.0 %collective-permute-start.17 = (bf16[32,4096]{1,0:T(8,128)(2,1)S(1)}, bf16[32,4096]{1,0:T(8,128)(2,1)S(1)}, u32[]{:S(2)}, u32[]{:S(2)}) collective-permute-start(bf16[32,4096]{1,0:T(8,128)(2,1)S(1)} %add_convert_fusion.1), channel_id=1, source_target_pairs={{0,2},{1,271},{2,4},{3,1},{4,6},{5,3},{6,8},{7,5},{8,10},{9,7},{10... | collective-permute-start | bytes 786440 | tf_op jit(solution)/shard_map/ppermute | solution.py:30
  115.5 2.3 %collective-permute-start.16 = (bf16[32,4096]{1,0:T(8,128)(2,1)S(1)}, bf16[32,4096]{1,0:T(8,128)(2,1)S(1)}, u32[]{:S(2)}, u32[]{:S(2)}) collective-permute-start(bf16[32,4096]{1,0:T(8,128)(2,1)S(1)} %add_convert_fusion.2), channel_id=1, source_target_pairs={{0,270},{1,3},{2,0},{3,5},{4,2},{5,7},{6,4},{7,9},{8,6},{9,11},{10... | collective-permute-start | bytes 786440 | tf_op jit(solution)/shard_map/ppermute | solution.py:30
  117.8 2.0 %collective-permute-done.17 = bf16[32,4096]{1,0:T(8,128)(2,1)S(1)} collective-permute-done((bf16[32,4096]{1,0:T(8,128)(2,1)S(1)}, bf16[32,4096]{1,0:T(8,128)(2,1)S(1)}, u32[]{:S(2)}, u32[]{:S(2)}) %collective-permute-start.17) | collective-permute-done | bytes 262176 | tf_op jit(solution)/shard_map/ppermute | solution.py:30
  119.8 4.6 %collective-permute-done.16 = bf16[32,4096]{1,0:T(8,128)(2,1)S(1)} collective-permute-done((bf16[32,4096]{1,0:T(8,128)(2,1)S(1)}, bf16[32,4096]{1,0:T(8,128)(2,1)S(1)}, u32[]{:S(2)}, u32[]{:S(2)}) %collective-permute-start.16) | collective-permute-done | bytes 262176 | tf_op jit(solution)/shard_map/ppermute | solution.py:30
  (27 shorter events, 15.1 us)
Async XLA Ops:
  1.9 27.7 %collective-permute-start.2 = (bf16[32,4096]{1,0:T(8,128)(2,1)}, bf16[32,4096]{1,0:T(8,128)(2,1)S(1)}, u32[]{:S(2)}, u32[]{:S(2)}) collective-permute-start(bf16[32,4096]{1,0:T(8,128)(2,1)} %get-tuple-element.35.refs_4_), channel_id=1, source_target_pairs={{0,270},{1,3},{2,0},{3,5},{4,2},{5,7},{6,4},{7,9},{8,6},{9,11},{10... | collective-permute-start | bytes 786440 | tf_op jit(solution)/shard_map/ppermute | solution.py:30
  6.2 23.4 %collective-permute-start.1 = (bf16[32,4096]{1,0:T(8,128)(2,1)}, bf16[32,4096]{1,0:T(8,128)(2,1)S(1)}, u32[]{:S(2)}, u32[]{:S(2)}) collective-permute-start(bf16[32,4096]{1,0:T(8,128)(2,1)} %get-tuple-element.35.refs_4_), channel_id=1, source_target_pairs={{0,2},{1,271},{2,4},{3,1},{4,6},{5,3},{6,8},{7,5},{8,10},{9,7},{10... | collective-permute-start | bytes 786440 | tf_op jit(solution)/shard_map/ppermute | solution.py:30
  15.7 13.8 %collective-permute-start = (bf16[112,256]{1,0:T(8,128)(2,1)}, bf16[112,256]{1,0:T(8,128)(2,1)S(1)}, u32[]{:S(2)}, u32[]{:S(2)}) collective-permute-start(bf16[112,256]{1,0:T(8,128)(2,1)} %get-tuple-element.34.mine), channel_id=1, source_target_pairs={{0,256},{256,0},{1,257},{257,1},{2,258},{258,2},{3,259},{259,3},{4... | collective-permute-start | bytes 172040 | tf_op jit(solution)/shard_map/ppermute | solution.py:163
  29.6 0.8 copy-start.1
  31.7 37.6 %all-to-all-start = ((bf16[16,2,2,48,256]{4,3,2,1,0:T(8,128)(2,1)}), bf16[16,2,2,48,256]{4,3,2,1,0:T(8,128)(2,1)S(1)}, u32[]{:S(2)}, u32[]{:S(2)}) async-start(bf16[16,2,2,48,256]{4,3,2,1,0:T(8,128)(2,1)} %get-tuple-element.37), calls=%async_computation | async-start | bytes 3145728 | tf_op jit(solution)/shard_map/all_to_all | solution.py:178
  38.5 13.9 %collective-permute-start.3 = (bf16[32,4096]{1,0:T(8,128)(2,1)S(1)}, bf16[32,4096]{1,0:T(8,128)(2,1)S(1)}, u32[]{:S(2)}, u32[]{:S(2)}) collective-permute-start(bf16[32,4096]{1,0:T(8,128)(2,1)S(1)} %collective-permute-done.1.refs_2_), channel_id=1, source_target_pairs={{0,2},{1,271},{2,4},{3,1},{4,6},{5,3},{6,8},{7,5},{8,10},{9,7},{10... | collective-permute-start | bytes 786440 | tf_op jit(solution)/shard_map/ppermute | solution.py:30
  44.2 14.8 %collective-permute-start.6 = (bf16[32,4096]{1,0:T(8,128)(2,1)S(1)}, bf16[32,4096]{1,0:T(8,128)(2,1)S(1)}, u32[]{:S(2)}, u32[]{:S(2)}) collective-permute-start(bf16[32,4096]{1,0:T(8,128)(2,1)S(1)} %collective-permute-done.2.refs_3_), channel_id=1, source_target_pairs={{0,270},{1,3},{2,0},{3,5},{4,2},{5,7},{6,4},{7,9},{8,6},{9,11},{10... | collective-permute-start | bytes 786440 | tf_op jit(solution)/shard_map/ppermute | solution.py:30
  46.1 25.1 %collective-permute-start.8 = (bf16[4096,256]{1,0:T(8,128)(2,1)}, bf16[4096,256]{1,0:T(8,128)(2,1)}, u32[]{:S(2)}, u32[]{:S(2)}) collective-permute-start(bf16[4096,256]{1,0:T(8,128)(2,1)} %refs_5_.3), channel_id=1, source_target_pairs={{0,1},{1,0},{2,3},{3,2},{4,5},{5,4},{6,7},{7,6},{8,9},{9,8},{10,11... | collective-permute-start | bytes 6291464 | tf_op jit(solution)/shard_map/ppermute | solution.py:165
  50.5 20.8 %collective-permute-start.9 = (bf16[256,4096]{1,0:T(8,128)(2,1)}, bf16[256,4096]{1,0:T(8,128)(2,1)}, u32[]{:S(2)}, u32[]{:S(2)}) collective-permute-start(bf16[256,4096]{1,0:T(8,128)(2,1)} %refs_7_.1), channel_id=1, source_target_pairs={{0,1},{1,0},{2,3},{3,2},{4,5},{5,4},{6,7},{7,6},{8,9},{9,8},{10,11... | collective-permute-start | bytes 6291464 | tf_op jit(solution)/shard_map/ppermute | solution.py:166
  52.4 9.4 %collective-permute-start.5 = (bf16[32,4096]{1,0:T(8,128)(2,1)S(1)}, bf16[32,4096]{1,0:T(8,128)(2,1)S(1)}, u32[]{:S(2)}, u32[]{:S(2)}) collective-permute-start(bf16[32,4096]{1,0:T(8,128)(2,1)S(1)} %collective-permute-done.3.refs_0_), channel_id=1, source_target_pairs={{0,4},{1,269},{2,6},{3,271},{4,8},{5,1},{6,10},{7,3},{8,12},{9,5},... | collective-permute-start | bytes 786440 | tf_op jit(solution)/shard_map/ppermute | solution.py:30
  55.9 13.4 %collective-permute-start.4 = (bf16[32,4096]{1,0:T(8,128)(2,1)S(1)}, bf16[32,4096]{1,0:T(8,128)(2,1)S(1)}, u32[]{:S(2)}, u32[]{:S(2)}) collective-permute-start(bf16[32,4096]{1,0:T(8,128)(2,1)S(1)} %collective-permute-done.3.refs_0_), channel_id=1, source_target_pairs={{0,2},{1,271},{2,4},{3,1},{4,6},{5,3},{6,8},{7,5},{8,10},{9,7},{10... | collective-permute-start | bytes 786440 | tf_op jit(solution)/shard_map/ppermute | solution.py:30
  59.0 10.3 %collective-permute-start.7 = (bf16[32,4096]{1,0:T(8,128)(2,1)S(1)}, bf16[32,4096]{1,0:T(8,128)(2,1)S(1)}, u32[]{:S(2)}, u32[]{:S(2)}) collective-permute-start(bf16[32,4096]{1,0:T(8,128)(2,1)S(1)} %collective-permute-done.6.refs_1_), channel_id=1, source_target_pairs={{0,270},{1,3},{2,0},{3,5},{4,2},{5,7},{6,4},{7,9},{8,6},{9,11},{10... | collective-permute-start | bytes 786440 | tf_op jit(solution)/shard_map/ppermute | solution.py:30
  69.3 5.3 %collective-permute-start.10 = (bf16[16,2,2,48,256]{4,3,2,1,0:T(8,128)(2,1)S(1)}, bf16[16,2,2,48,256]{4,3,2,1,0:T(8,128)(2,1)S(1)}, u32[]{:S(2)}, u32[]{:S(2)}) collective-permute-start(bf16[16,2,2,48,256]{4,3,2,1,0:T(8,128)(2,1)S(1)} %all-to-all-done.refs_7_.refs_9_), channel_id=1, source_target_pairs={{0,1},{1,0},{2,3},{3,2},{4,5},{5,4},{6,7},{7,6},{8,9},{9,8},{10,11... | collective-permute-start | bytes 4718600 | tf_op jit(solution)/shard_map/ppermute | solution.py:183
  74.6 14.9 %copy-start = (bf16[32,4096]{1,0:T(8,128)(2,1)S(1)}, bf16[32,4096]{1,0:T(8,128)(2,1)}, u32[]{:S(2)}) copy-start(bf16[32,4096]{1,0:T(8,128)(2,1)} %get-tuple-element.35.refs_4_) | copy-start | bytes 786436
  81.0 15.7 %collective-permute-start.11 = (bf16[32,4096]{1,0:T(8,128)(2,1)S(1)}, bf16[32,4096]{1,0:T(8,128)(2,1)S(1)}, u32[]{:S(2)}, u32[]{:S(2)}) collective-permute-start(bf16[32,4096]{1,0:T(8,128)(2,1)S(1)} %get-tuple-element.45), channel_id=1, source_target_pairs={{0,270},{1,3},{2,0},{3,5},{4,2},{5,7},{6,4},{7,9},{8,6},{9,11},{10... | collective-permute-start | bytes 786440 | tf_op jit(solution)/shard_map/ppermute | solution.py:30
  83.0 13.8 %collective-permute-start.12 = (bf16[32,4096]{1,0:T(8,128)(2,1)S(1)}, bf16[32,4096]{1,0:T(8,128)(2,1)S(1)}, u32[]{:S(2)}, u32[]{:S(2)}) collective-permute-start(bf16[32,4096]{1,0:T(8,128)(2,1)S(1)} %get-tuple-element.46), channel_id=1, source_target_pairs={{0,2},{1,271},{2,4},{3,1},{4,6},{5,3},{6,8},{7,5},{8,10},{9,7},{10... | collective-permute-start | bytes 786440 | tf_op jit(solution)/shard_map/ppermute | solution.py:30
  87.5 11.9 %collective-permute-start.13 = (bf16[32,4096]{1,0:T(8,128)(2,1)S(1)}, bf16[32,4096]{1,0:T(8,128)(2,1)S(1)}, u32[]{:S(2)}, u32[]{:S(2)}) collective-permute-start(bf16[32,4096]{1,0:T(8,128)(2,1)S(1)} %get-tuple-element.47), channel_id=1, source_target_pairs={{0,268},{1,5},{2,270},{3,7},{4,0},{5,9},{6,2},{7,11},{8,4},{9,13},... | collective-permute-start | bytes 786440 | tf_op jit(solution)/shard_map/ppermute | solution.py:30
  99.5 7.1 %collective-permute-start.15 = (bf16[32,4096]{1,0:T(8,128)(2,1)S(1)}, bf16[32,4096]{1,0:T(8,128)(2,1)S(1)}, u32[]{:S(2)}, u32[]{:S(2)}) collective-permute-start(bf16[32,4096]{1,0:T(8,128)(2,1)S(1)} %add_convert_fusion.3), channel_id=1, source_target_pairs={{0,2},{1,271},{2,4},{3,1},{4,6},{5,3},{6,8},{7,5},{8,10},{9,7},{10... | collective-permute-start | bytes 786440 | tf_op jit(solution)/shard_map/ppermute | solution.py:30
  101.5 10.8 %collective-permute-start.14 = (bf16[32,4096]{1,0:T(8,128)(2,1)S(1)}, bf16[32,4096]{1,0:T(8,128)(2,1)S(1)}, u32[]{:S(2)}, u32[]{:S(2)}) collective-permute-start(bf16[32,4096]{1,0:T(8,128)(2,1)S(1)} %add_convert_fusion.4), channel_id=1, source_target_pairs={{0,270},{1,3},{2,0},{3,5},{4,2},{5,7},{6,4},{7,9},{8,6},{9,11},{10... | collective-permute-start | bytes 786440 | tf_op jit(solution)/shard_map/ppermute | solution.py:30
  112.4 7.4 %collective-permute-start.17 = (bf16[32,4096]{1,0:T(8,128)(2,1)S(1)}, bf16[32,4096]{1,0:T(8,128)(2,1)S(1)}, u32[]{:S(2)}, u32[]{:S(2)}) collective-permute-start(bf16[32,4096]{1,0:T(8,128)(2,1)S(1)} %add_convert_fusion.1), channel_id=1, source_target_pairs={{0,2},{1,271},{2,4},{3,1},{4,6},{5,3},{6,8},{7,5},{8,10},{9,7},{10... | collective-permute-start | bytes 786440 | tf_op jit(solution)/shard_map/ppermute | solution.py:30
  115.5 9.0 %collective-permute-start.16 = (bf16[32,4096]{1,0:T(8,128)(2,1)S(1)}, bf16[32,4096]{1,0:T(8,128)(2,1)S(1)}, u32[]{:S(2)}, u32[]{:S(2)}) collective-permute-start(bf16[32,4096]{1,0:T(8,128)(2,1)S(1)} %add_convert_fusion.2), channel_id=1, source_target_pairs={{0,270},{1,3},{2,0},{3,5},{4,2},{5,7},{6,4},{7,9},{8,6},{9,11},{10... | collective-permute-start | bytes 786440 | tf_op jit(solution)/shard_map/ppermute | solution.py:30

commit v5 on v4

--- a/solution.py
+++ b/solution.py
@@ -65,16 +65,38 @@
     bound[...] = jnp.minimum(jnp.concatenate(found, axis=1), last)
 
 
-def attend_kernel(count, first, *refs):
-    blocks, outs = refs[:count], refs[count + 7 : 2 * count + 7]
-    held, sem = refs[2 * count + 7 : 2 * count + 11], refs[-1]
-    copies = [pltpu.make_async_copy(refs[count + i], held[i], sem.at[i]) for i in range(4)]
-    for copy in copies:
-        copy.start()
-    wq, wo, kv = held[:2], held[2:], refs[count + 4 : count + 6]
-    bound = refs[count + 6]
-    rows = 32 * count
-    x = jnp.concatenate([b[...] for b in blocks], axis=0)
+def attended(x, wq, kv, bias):
+    q = jnp.dot(x, wq[...], preferred_element_type=jnp.float32)
+    q = (q * HEAD_DIM**-0.5).astype(jnp.bfloat16)
+    heads = []
+    for h in range(2):
+        cols = slice(h * HEAD_DIM, (h + 1) * HEAD_DIM)
+        s = [
+            lax.dot_general(
+                q[:, cols],
+                kv[4 * t : 4 * t + 4, 0, :, :, cols].reshape(384, HEAD_DIM),
+                (((1,), (1,)), ((), ())),
+                preferred_element_type=jnp.float32,
+            )
+            for t in range(4)
+        ]
+        s = jnp.concatenate(s, axis=1) + bias
+        e = jnp.exp(s - jnp.max(s, axis=1, keepdims=True))
+        total = jnp.sum(e, axis=1, keepdims=True)
+        e = e.astype(jnp.bfloat16)
+        a = sum(
+            jnp.dot(
+                e[:, t * 384 : (t + 1) * 384],
+                kv[4 * t : 4 * t + 4, 1, :, :, cols].reshape(384, HEAD_DIM),
+                preferred_element_type=jnp.float32,
+            )
+            for t in range(4)
+        )
+        heads.append((a / total).astype(jnp.bfloat16))
+    return jnp.concatenate(heads, axis=1)
+
+
+def shade(bound, first, rows):
     column = jnp.transpose(jnp.broadcast_to(bound[...], (8, 256)))
     column = column[first : first + rows, 0:1]
     zh = lax.axis_index("zh")
@@ -82,47 +104,99 @@
     shard = lax.shift_right_logical(index * 1366, 16)
     half = (shard & 1) ^ zh
     frame = half * 768 + lax.shift_right_logical(shard, 1) * 48 + (index - shard * 48)
-    bias = jnp.where(frame.astype(jnp.float32) <= column, 0.0, MASKED)
-    groups = []
-    for g in range(2):
-        copies[g].wait()
-        q = jnp.dot(x, wq[g][...], preferred_element_type=jnp.float32)
-        q = (q * HEAD_DIM**-0.5).astype(jnp.bfloat16)
-        heads = []
-        for h in range(2):
-            cols = slice(h * HEAD_DIM, (h + 1) * HEAD_DIM)
-            s = [
-                lax.dot_general(
-                    q[:, cols],
-                    kv[g][4 * t : 4 * t + 4, 0, :, :, cols].reshape(384, HEAD_DIM),
-                    (((1,), (1,)), ((), ())),
-                    preferred_element_type=jnp.float32,
-                )
-                for t in range(4)
-            ]
-            s = jnp.concatenate(s, axis=1) + bias
-            e = jnp.exp(s - jnp.max(s, axis=1, keepdims=True))
-            total = jnp.sum(e, axis=1, keepdims=True)
-            e = e.astype(jnp.bfloat16)
-            a = sum(
-                jnp.dot(
-                    e[:, t * 384 : (t + 1) * 384],
-                    kv[g][4 * t : 4 * t + 4, 1, :, :, cols].reshape(384, HEAD_DIM),
-                    preferred_element_type=jnp.float32,
-                )
-                for t in range(4)
-            )
-            heads.append((a / total).astype(jnp.bfloat16))
-        groups.append(jnp.concatenate(heads, axis=1))
-    copies[2].wait()
-    copies[3].wait()
+    return jnp.where(frame.astype(jnp.float32) <= column, 0.0, MASKED)
+
+
+def fetch(sources, held, sem):
+    copies = [pltpu.make_async_copy(u, v, sem.at[i]) for i, (u, v) in enumerate(zip(sources, held))]
+    for copy in copies:
+        copy.start()
+    return copies
+
+
+def project(groups, wo, outs):
     for n in range(0, 4096, 1024):
         cols = slice(n, n + 1024)
         total = jnp.dot(groups[0], wo[0][:, cols], preferred_element_type=jnp.float32)
         total += jnp.dot(groups[1], wo[1][:, cols], preferred_element_type=jnp.float32)
         total = total.astype(jnp.bfloat16)
-        for i in range(count):
-            outs[i][:, cols] = total[32 * i : 32 * i + 32, :]
+        for i, out in enumerate(outs):
+            out[:, cols] = total[32 * i : 32 * i + 32, :]
+
+
+def attend_kernel(count, first, *refs):
+    blocks, outs = refs[:count], refs[count + 7 : 2 * count + 7]
+    held = refs[2 * count + 7 : 2 * count + 11]
+    copies = fetch(refs[count : count + 4], held, refs[-1])
+    x = jnp.concatenate([b[...] for b in blocks], axis=0)
+    bias = shade(refs[count + 6], first, 32 * count)
+    groups = []
+    for g in range(2):
+        copies[g].wait()
+        groups.append(attended(x, held[g], refs[count + 4 + g], bias))
+    copies[2].wait()
+    copies[3].wait()
+    project(groups, held[2:], outs)
+
+
+def begin_kernel(count, first, *refs):
+    blocks = refs[:count]
+    wq, kv, bound, out, held, sem = refs[count:]
+    (copy,) = fetch((wq,), (held,), sem)
+    x = jnp.concatenate([b[...] for b in blocks], axis=0)
+    bias = shade(bound, first, 32 * count)
+    copy.wait()
+    out[...] = attended(x, held, kv, bias)
+
+
+def finish_kernel(count, first, *refs):
+    blocks, outs = refs[:count], refs[count + 6 : 2 * count + 6]
+    kv, bound, done = refs[count + 3 : count + 6]
+    held = refs[2 * count + 6 : 2 * count + 9]
+    copies = fetch(refs[count : count + 3], held, refs[-1])
+    x = jnp.concatenate([b[...] for b in blocks], axis=0)
+    bias = shade(bound, first, 32 * count)
+    copies[0].wait()
+    groups = (done[...], attended(x, held[0], kv, bias))
+    copies[1].wait()
+    copies[2].wait()
+    project(groups, held[1:], outs)
+
+
+def begin(blocks, first, wq, kv, bound):
+    count = len(blocks)
+    rows = 32 * count
+    return pl.pallas_call(
+        functools.partial(begin_kernel, count, first),
+        out_shape=jax.ShapeDtypeStruct((rows, 256), jnp.bfloat16),
+        in_specs=[VMEM] * count + [HELD, VMEM, VMEM],
+        out_specs=VMEM,
+        scratch_shapes=[pltpu.VMEM((4096, 256), jnp.bfloat16), pltpu.SemaphoreType.DMA((1,))],
+        compiler_params=pltpu.CompilerParams(vmem_limit_bytes=50 * 2**20),
+        cost_estimate=pl.CostEstimate(
+            flops=rows * 4 * 2**20, bytes_accessed=4 * 2**20, transcendentals=rows * 3072
+        ),
+        name="begin%d" % count,
+    )(*blocks, wq, kv, bound)
+
+
+def finish(blocks, first, wq, wo, kv, bound, done):
+    count = len(blocks)
+    rows = 32 * count
+    return pl.pallas_call(
+        functools.partial(finish_kernel, count, first),
+        out_shape=[jax.ShapeDtypeStruct((32, 4096), jnp.bfloat16)] * count,
+        in_specs=[VMEM] * count + [HELD] * 3 + [VMEM] * 3,
+        out_specs=[VMEM] * count,
+        scratch_shapes=[pltpu.VMEM((4096, 256), jnp.bfloat16)]
+        + [pltpu.VMEM((256, 4096), jnp.bfloat16)] * 2
+        + [pltpu.SemaphoreType.DMA((3,))],
+        compiler_params=pltpu.CompilerParams(vmem_limit_bytes=LIMIT * 2**20),
+        cost_estimate=pl.CostEstimate(
+            flops=rows * 8 * 2**20, bytes_accessed=8 * 2**20, transcendentals=rows * 3072
+        ),
+        name="finish%d" % count,
+    )(*blocks, wq, *wo, kv, bound, done)
 
 
 def attend(blocks, first, wq, wo, kv, bound):
@@ -183,7 +257,8 @@
     kv_other = lax.ppermute(kv, "c", SWAP)
 
     given = ((wq, wq_other), (wo, wo_other), (kv, kv_other), bound)
-    far = attend([a4, a3, b3], 0, *given)
+    half = begin([a4, a3, b3], 0, wq, kv, bound)
+    far = finish([a4, a3, b3], 0, wq_other, (wo, wo_other), kv_other, bound, half)
     near = attend([a2, b2, a1, b1, own], 96, *given)
     wide = lambda v: v.astype(jnp.float32)
     thin = lambda v: v.astype(jnp.bfloat16)

time: 126 us -> 128 us (1.016)
  starting transfers between devices: 73 us -> 75.3 us
  waiting for transfers between devices: 32.5 us -> 30.7 us
  Pallas kernels: 16.8 us -> 18.4 us
    pallas_call x0 -> x2, Pallas kernels: none -> 8.03 us  [the longest x1 4.46 us: finish(): pl.pallas_call(functools.partial(finish_kernel, count, first), out_shape=...]
    pallas_call x2 -> x1, Pallas kernels: 13.7 us -> 7.25 us  [attend(): pl.pallas_call(functools.partial(attend_kernel, count, first), out_shape=...]
    ppermute x14, starting transfers between devices: 49.2 us -> 54.1 us  [along(): return lax.ppermute(x, RING + ('c',), opposite(step))]
    ppermute x1, waiting for transfers between devices: 3.35 us -> 0.01 us  [per_device(): kv_other = lax.ppermute(kv, 'c', SWAP)]
    ppermute x1, starting transfers between devices: 4.34 us -> 2.91 us  [per_device(): wq_other = lax.ppermute(wq, 'c', SWAP)]
  transfers between devices with their start and end apart: 19 -> 19, of which waited for: 9 -> 8; matrix products, arithmetic and copies ran while one was open for 0% -> 0% of each run, Pallas kernels for 6% -> 9%
where the time goes in v5:
time: 128 us; the launch traced here: 127 us
  starting transfers between devices  75.3 us (59%)
  waiting for transfers between devices  30.7 us (24%)
  Pallas kernels  18.4 us (14%)
    ppermute x14, starting transfers between devices, along(): return lax.ppermute(x, RING + ('c',), opposite(step))  54.1 us
    ppermute x14, waiting for transfers between devices, along(): return lax.ppermute(x, RING + ('c',), opposite(step))  25.2 us
    ppermute x1, starting transfers between devices, per_device(): theirs = lax.ppermute(mine, 'zh', SWAP)  7.68 us
    pallas_call x1, Pallas kernels, attend(): pl.pallas_call(functools.partial(attend_kernel, count, first), out_shape=...  7.25 us
    all_to_all x1, starting transfers between devices, per_device(): kv = lax.all_to_all(kv, ('y', 'x'), 0, 0, tiled=True)  6.75 us
    ppermute x1, waiting for transfers between devices, per_device(): theirs = lax.ppermute(mine, 'zh', SWAP)  5.51 us
    pallas_call x1, Pallas kernels, finish(): pl.pallas_call(functools.partial(finish_kernel, count, first), out_shape=...  4.46 us
    pallas_call x1, Pallas kernels, begin(): pl.pallas_call(functools.partial(begin_kernel, count, first), out_shape=j...  3.58 us
  transfers between devices with their start and end apart: 19, of which 8 were waited for; matrix products, arithmetic and copies ran while one was open for 0% of the time, Pallas kernels for 9%

profile of v5, /device:TPU:1, one launch (start us, length us, event | category | flops | bytes accessed | tf_op | source)
XLA Modules:
  0.0 127.3 jit_solution(7306689554456794702)
XLA Ops:
  1.9 11.9 %collective-permute-start.1 = (bf16[32,4096]{1,0:T(8,128)(2,1)}, bf16[32,4096]{1,0:T(8,128)(2,1)S(1)}, u32[]{:S(2)}, u32[]{:S(2)}) collective-permute-start(bf16[32,4096]{1,0:T(8,128)(2,1)} %get-tuple-element.35.refs_4_), channel_id=1, source_target_pairs={{0,2},{1,271},{2,4},{3,1},{4,6},{5,3},{6,8},{7,5},{8,10},{9,7},{10... | collective-permute-start | bytes 786440 | tf_op jit(solution)/shard_map/ppermute | solution.py:30
  15.7 7.7 %collective-permute-start = (bf16[112,256]{1,0:T(8,128)(2,1)}, bf16[112,256]{1,0:T(8,128)(2,1)S(1)}, u32[]{:S(2)}, u32[]{:S(2)}) collective-permute-start(bf16[112,256]{1,0:T(8,128)(2,1)} %get-tuple-element.34.mine), channel_id=1, source_target_pairs={{0,256},{256,0},{1,257},{257,1},{2,258},{258,2},{3,259},{259,3},{4... | collective-permute-start | bytes 172040 | tf_op jit(solution)/shard_map/ppermute | solution.py:237
  24.1 5.5 %collective-permute-done.theirs = bf16[112,256]{1,0:T(8,128)(2,1)S(1)} collective-permute-done((bf16[112,256]{1,0:T(8,128)(2,1)}, bf16[112,256]{1,0:T(8,128)(2,1)S(1)}, u32[]{:S(2)}, u32[]{:S(2)}) %collective-permute-start) | collective-permute-done | bytes 57376 | tf_op jit(solution)/shard_map/ppermute | solution.py:237
  31.7 6.8 %all-to-all-start = ((bf16[16,2,2,48,256]{4,3,2,1,0:T(8,128)(2,1)}), bf16[16,2,2,48,256]{4,3,2,1,0:T(8,128)(2,1)S(1)}, u32[]{:S(2)}, u32[]{:S(2)}) async-start(bf16[16,2,2,48,256]{4,3,2,1,0:T(8,128)(2,1)} %get-tuple-element.37), calls=%async_computation | async-start | bytes 3145728 | tf_op jit(solution)/shard_map/all_to_all | solution.py:252
  38.5 7.3 %collective-permute-start.3 = (bf16[32,4096]{1,0:T(8,128)(2,1)S(1)}, bf16[32,4096]{1,0:T(8,128)(2,1)S(1)}, u32[]{:S(2)}, u32[]{:S(2)}) collective-permute-start(bf16[32,4096]{1,0:T(8,128)(2,1)S(1)} %collective-permute-done.1.refs_2_), channel_id=1, source_target_pairs={{0,2},{1,271},{2,4},{3,1},{4,6},{5,3},{6,8},{7,5},{8,10},{9,7},{10... | collective-permute-start | bytes 786440 | tf_op jit(solution)/shard_map/ppermute | solution.py:30
  45.8 1.9 %collective-permute-start.6 = (bf16[32,4096]{1,0:T(8,128)(2,1)S(1)}, bf16[32,4096]{1,0:T(8,128)(2,1)S(1)}, u32[]{:S(2)}, u32[]{:S(2)}) collective-permute-start(bf16[32,4096]{1,0:T(8,128)(2,1)S(1)} %collective-permute-done.2.refs_3_), channel_id=1, source_target_pairs={{0,270},{1,3},{2,0},{3,5},{4,2},{5,7},{6,4},{7,9},{8,6},{9,11},{10... | collective-permute-start | bytes 786440 | tf_op jit(solution)/shard_map/ppermute | solution.py:30
  47.7 2.9 %collective-permute-start.8 = (bf16[4096,256]{1,0:T(8,128)(2,1)}, bf16[4096,256]{1,0:T(8,128)(2,1)}, u32[]{:S(2)}, u32[]{:S(2)}) collective-permute-start(bf16[4096,256]{1,0:T(8,128)(2,1)} %refs_5_.1), channel_id=1, source_target_pairs={{0,1},{1,0},{2,3},{3,2},{4,5},{5,4},{6,7},{7,6},{8,9},{9,8},{10,11... | collective-permute-start | bytes 6291464 | tf_op jit(solution)/shard_map/ppermute | solution.py:239
  50.6 1.9 %collective-permute-start.9 = (bf16[256,4096]{1,0:T(8,128)(2,1)}, bf16[256,4096]{1,0:T(8,128)(2,1)}, u32[]{:S(2)}, u32[]{:S(2)}) collective-permute-start(bf16[256,4096]{1,0:T(8,128)(2,1)} %refs_7_.1), channel_id=1, source_target_pairs={{0,1},{1,0},{2,3},{3,2},{4,5},{5,4},{6,7},{7,6},{8,9},{9,8},{10,11... | collective-permute-start | bytes 6291464 | tf_op jit(solution)/shard_map/ppermute | solution.py:240
  52.6 4.1 %collective-permute-start.4 = (bf16[32,4096]{1,0:T(8,128)(2,1)S(1)}, bf16[32,4096]{1,0:T(8,128)(2,1)S(1)}, u32[]{:S(2)}, u32[]{:S(2)}) collective-permute-start(bf16[32,4096]{1,0:T(8,128)(2,1)S(1)} %collective-permute-done.3.refs_0_), channel_id=1, source_target_pairs={{0,2},{1,271},{2,4},{3,1},{4,6},{5,3},{6,8},{7,5},{8,10},{9,7},{10... | collective-permute-start | bytes 786440 | tf_op jit(solution)/shard_map/ppermute | solution.py:30
  56.7 3.0 %collective-permute-start.5 = (bf16[32,4096]{1,0:T(8,128)(2,1)S(1)}, bf16[32,4096]{1,0:T(8,128)(2,1)S(1)}, u32[]{:S(2)}, u32[]{:S(2)}) collective-permute-start(bf16[32,4096]{1,0:T(8,128)(2,1)S(1)} %collective-permute-done.3.refs_0_), channel_id=1, source_target_pairs={{0,4},{1,269},{2,6},{3,271},{4,8},{5,1},{6,10},{7,3},{8,12},{9,5},... | collective-permute-start | bytes 786440 | tf_op jit(solution)/shard_map/ppermute | solution.py:30
  59.7 2.0 %collective-permute-start.7 = (bf16[32,4096]{1,0:T(8,128)(2,1)S(1)}, bf16[32,4096]{1,0:T(8,128)(2,1)S(1)}, u32[]{:S(2)}, u32[]{:S(2)}) collective-permute-start(bf16[32,4096]{1,0:T(8,128)(2,1)S(1)} %collective-permute-done.6.refs_1_), channel_id=1, source_target_pairs={{0,270},{1,3},{2,0},{3,5},{4,2},{5,7},{6,4},{7,9},{8,6},{9,11},{10... | collective-permute-start | bytes 786440 | tf_op jit(solution)/shard_map/ppermute | solution.py:30
  61.7 7.3 %collective-permute-done.5.refs_0_ = bf16[32,4096]{1,0:T(8,128)(2,1)S(1)} collective-permute-done((bf16[32,4096]{1,0:T(8,128)(2,1)S(1)}, bf16[32,4096]{1,0:T(8,128)(2,1)S(1)}, u32[]{:S(2)}, u32[]{:S(2)}) %collective-permute-start.5) | collective-permute-done | bytes 262176 | tf_op jit(solution)/shard_map/ppermute | solution.py:30
  72.2 3.6 %begin3.1.refs_8_ = bf16[96,256]{1,0:T(8,128)(2,1)S(1)} custom-call(bf16[32,4096]{1,0:T(8,128)(2,1)S(1)} %collective-permute-done.5.refs_0_, bf16[32,4096]{1,0:T(8,128)(2,1)S(1)} %collective-permute-done.4.refs_1_, bf16[32,4096]{1,0:T(8,128)(2,1)S(1)} %collective-permute-done.7.refs_2_, bf16[4096,256]{1,0:T(8,128)(2,1)} %refs_5_.1, ...), custom_call_target="tpu_custom_call" | custom-call | flops 402653184 | bytes 4194304 | tf_op jit(solution)/shard_map/begin3/pallas_call | solution.py:169
  75.8 4.5 %finish3.1 = (bf16[32,4096]{1,0:T(8,128)(2,1)S(1)}, bf16[32,4096]{1,0:T(8,128)(2,1)S(1)}, bf16[32,4096]{1,0:T(8,128)(2,1)S(1)}) custom-call(bf16[32,4096]{1,0:T(8,128)(2,1)S(1)} %collective-permute-done.5.refs_0_, bf16[32,4096]{1,0:T(8,128)(2,1)S(1)} %collective-permute-done.4.refs_1_, bf16[32,4096]{1,0:T(8,128)(2,1)S(1)} %collective-permute-done.7.refs_2_, ...), custom_call_target="tpu_custom_call" | custom-call | flops 805306368 | bytes 8388608 | tf_op jit(solution)/shard_map/finish3/pallas_call | solution.py:186
  80.3 2.8 %collective-permute-start.11 = (bf16[32,4096]{1,0:T(8,128)(2,1)S(1)}, bf16[32,4096]{1,0:T(8,128)(2,1)S(1)}, u32[]{:S(2)}, u32[]{:S(2)}) collective-permute-start(bf16[32,4096]{1,0:T(8,128)(2,1)S(1)} %get-tuple-element.45), channel_id=1, source_target_pairs={{0,270},{1,3},{2,0},{3,5},{4,2},{5,7},{6,4},{7,9},{8,6},{9,11},{10... | collective-permute-start | bytes 786440 | tf_op jit(solution)/shard_map/ppermute | solution.py:30
  83.1 3.7 %collective-permute-start.12 = (bf16[32,4096]{1,0:T(8,128)(2,1)S(1)}, bf16[32,4096]{1,0:T(8,128)(2,1)S(1)}, u32[]{:S(2)}, u32[]{:S(2)}) collective-permute-start(bf16[32,4096]{1,0:T(8,128)(2,1)S(1)} %get-tuple-element.46), channel_id=1, source_target_pairs={{0,2},{1,271},{2,4},{3,1},{4,6},{5,3},{6,8},{7,5},{8,10},{9,7},{10... | collective-permute-start | bytes 786440 | tf_op jit(solution)/shard_map/ppermute | solution.py:30
  86.8 1.9 %collective-permute-start.13 = (bf16[32,4096]{1,0:T(8,128)(2,1)S(1)}, bf16[32,4096]{1,0:T(8,128)(2,1)S(1)}, u32[]{:S(2)}, u32[]{:S(2)}) collective-permute-start(bf16[32,4096]{1,0:T(8,128)(2,1)S(1)} %get-tuple-element.47), channel_id=1, source_target_pairs={{0,268},{1,5},{2,270},{3,7},{4,0},{5,9},{6,2},{7,11},{8,4},{9,13},... | collective-permute-start | bytes 786440 | tf_op jit(solution)/shard_map/ppermute | solution.py:30
  88.8 7.2 %attend5.1 = (bf16[32,4096]{1,0:T(8,128)(2,1)S(1)}, bf16[32,4096]{1,0:T(8,128)(2,1)S(1)}, bf16[32,4096]{1,0:T(8,128)(2,1)S(1)}, bf16[32,4096]{1,0:T(8,128)(2,1)S(1)}, bf16[32,4096]{1,0:T(8,128)(2,1)S(1)}) custom-call(bf16[32,4096]{1,0:T(8,128)(2,1)S(1)} %collective-permute-done.3.refs_0_, bf16[32,4096]{1,0:T(8,128)(2,1)S(1)} %collective-permute-done.6.refs_1_, ...), custom_call_target="tpu_custom_call" | custom-call | flops 2013265920 | bytes 12582912 | tf_op jit(solution)/shard_map/attend5/pallas_call | solution.py:205
  96.0 3.7 %collective-permute-done.13 = bf16[32,4096]{1,0:T(8,128)(2,1)S(1)} collective-permute-done((bf16[32,4096]{1,0:T(8,128)(2,1)S(1)}, bf16[32,4096]{1,0:T(8,128)(2,1)S(1)}, u32[]{:S(2)}, u32[]{:S(2)}) %collective-permute-start.13) | collective-permute-done | bytes 262176 | tf_op jit(solution)/shard_map/ppermute | solution.py:30
  99.8 1.9 %collective-permute-start.14 = (bf16[32,4096]{1,0:T(8,128)(2,1)S(1)}, bf16[32,4096]{1,0:T(8,128)(2,1)S(1)}, u32[]{:S(2)}, u32[]{:S(2)}) collective-permute-start(bf16[32,4096]{1,0:T(8,128)(2,1)S(1)} %add_convert_fusion.4), channel_id=1, source_target_pairs={{0,270},{1,3},{2,0},{3,5},{4,2},{5,7},{6,4},{7,9},{8,6},{9,11},{10... | collective-permute-start | bytes 786440 | tf_op jit(solution)/shard_map/ppermute | solution.py:30
  101.8 5.1 %collective-permute-start.15 = (bf16[32,4096]{1,0:T(8,128)(2,1)S(1)}, bf16[32,4096]{1,0:T(8,128)(2,1)S(1)}, u32[]{:S(2)}, u32[]{:S(2)}) collective-permute-start(bf16[32,4096]{1,0:T(8,128)(2,1)S(1)} %add_convert_fusion.3), channel_id=1, source_target_pairs={{0,2},{1,271},{2,4},{3,1},{4,6},{5,3},{6,8},{7,5},{8,10},{9,7},{10... | collective-permute-start | bytes 786440 | tf_op jit(solution)/shard_map/ppermute | solution.py:30
  108.7 3.4 %collective-permute-done.15 = bf16[32,4096]{1,0:T(8,128)(2,1)S(1)} collective-permute-done((bf16[32,4096]{1,0:T(8,128)(2,1)S(1)}, bf16[32,4096]{1,0:T(8,128)(2,1)S(1)}, u32[]{:S(2)}, u32[]{:S(2)}) %collective-permute-start.15) | collective-permute-done | bytes 262176 | tf_op jit(solution)/shard_map/ppermute | solution.py:30
  112.1 4.6 %collective-permute-start.17 = (bf16[32,4096]{1,0:T(8,128)(2,1)S(1)}, bf16[32,4096]{1,0:T(8,128)(2,1)S(1)}, u32[]{:S(2)}, u32[]{:S(2)}) collective-permute-start(bf16[32,4096]{1,0:T(8,128)(2,1)S(1)} %add_convert_fusion.1), channel_id=1, source_target_pairs={{0,2},{1,271},{2,4},{3,1},{4,6},{5,3},{6,8},{7,5},{8,10},{9,7},{10... | collective-permute-start | bytes 786440 | tf_op jit(solution)/shard_map/ppermute | solution.py:30
  119.9 6.5 %collective-permute-done.16 = bf16[32,4096]{1,0:T(8,128)(2,1)S(1)} collective-permute-done((bf16[32,4096]{1,0:T(8,128)(2,1)S(1)}, bf16[32,4096]{1,0:T(8,128)(2,1)S(1)}, u32[]{:S(2)}, u32[]{:S(2)}) %collective-permute-start.16) | collective-permute-done | bytes 262176 | tf_op jit(solution)/shard_map/ppermute | solution.py:30
  (28 shorter events, 15.2 us)
Async XLA Ops:
  1.9 27.7 %collective-permute-start.1 = (bf16[32,4096]{1,0:T(8,128)(2,1)}, bf16[32,4096]{1,0:T(8,128)(2,1)S(1)}, u32[]{:S(2)}, u32[]{:S(2)}) collective-permute-start(bf16[32,4096]{1,0:T(8,128)(2,1)} %get-tuple-element.35.refs_4_), channel_id=1, source_target_pairs={{0,2},{1,271},{2,4},{3,1},{4,6},{5,3},{6,8},{7,5},{8,10},{9,7},{10... | collective-permute-start | bytes 786440 | tf_op jit(solution)/shard_map/ppermute | solution.py:30
  13.8 15.8 %collective-permute-start.2 = (bf16[32,4096]{1,0:T(8,128)(2,1)}, bf16[32,4096]{1,0:T(8,128)(2,1)S(1)}, u32[]{:S(2)}, u32[]{:S(2)}) collective-permute-start(bf16[32,4096]{1,0:T(8,128)(2,1)} %get-tuple-element.35.refs_4_), channel_id=1, source_target_pairs={{0,270},{1,3},{2,0},{3,5},{4,2},{5,7},{6,4},{7,9},{8,6},{9,11},{10... | collective-permute-start | bytes 786440 | tf_op jit(solution)/shard_map/ppermute | solution.py:30
  15.7 13.8 %collective-permute-start = (bf16[112,256]{1,0:T(8,128)(2,1)}, bf16[112,256]{1,0:T(8,128)(2,1)S(1)}, u32[]{:S(2)}, u32[]{:S(2)}) collective-permute-start(bf16[112,256]{1,0:T(8,128)(2,1)} %get-tuple-element.34.mine), channel_id=1, source_target_pairs={{0,256},{256,0},{1,257},{257,1},{2,258},{258,2},{3,259},{259,3},{4... | collective-permute-start | bytes 172040 | tf_op jit(solution)/shard_map/ppermute | solution.py:237
  29.6 0.8 copy-start.1
  31.7 38.6 %all-to-all-start = ((bf16[16,2,2,48,256]{4,3,2,1,0:T(8,128)(2,1)}), bf16[16,2,2,48,256]{4,3,2,1,0:T(8,128)(2,1)S(1)}, u32[]{:S(2)}, u32[]{:S(2)}) async-start(bf16[16,2,2,48,256]{4,3,2,1,0:T(8,128)(2,1)} %get-tuple-element.37), calls=%async_computation | async-start | bytes 3145728 | tf_op jit(solution)/shard_map/all_to_all | solution.py:252
  38.5 14.1 %collective-permute-start.3 = (bf16[32,4096]{1,0:T(8,128)(2,1)S(1)}, bf16[32,4096]{1,0:T(8,128)(2,1)S(1)}, u32[]{:S(2)}, u32[]{:S(2)}) collective-permute-start(bf16[32,4096]{1,0:T(8,128)(2,1)S(1)} %collective-permute-done.1.refs_2_), channel_id=1, source_target_pairs={{0,2},{1,271},{2,4},{3,1},{4,6},{5,3},{6,8},{7,5},{8,10},{9,7},{10... | collective-permute-start | bytes 786440 | tf_op jit(solution)/shard_map/ppermute | solution.py:30
  45.8 13.9 %collective-permute-start.6 = (bf16[32,4096]{1,0:T(8,128)(2,1)S(1)}, bf16[32,4096]{1,0:T(8,128)(2,1)S(1)}, u32[]{:S(2)}, u32[]{:S(2)}) collective-permute-start(bf16[32,4096]{1,0:T(8,128)(2,1)S(1)} %collective-permute-done.2.refs_3_), channel_id=1, source_target_pairs={{0,270},{1,3},{2,0},{3,5},{4,2},{5,7},{6,4},{7,9},{8,6},{9,11},{10... | collective-permute-start | bytes 786440 | tf_op jit(solution)/shard_map/ppermute | solution.py:30
  47.7 28.1 %collective-permute-start.8 = (bf16[4096,256]{1,0:T(8,128)(2,1)}, bf16[4096,256]{1,0:T(8,128)(2,1)}, u32[]{:S(2)}, u32[]{:S(2)}) collective-permute-start(bf16[4096,256]{1,0:T(8,128)(2,1)} %refs_5_.1), channel_id=1, source_target_pairs={{0,1},{1,0},{2,3},{3,2},{4,5},{5,4},{6,7},{7,6},{8,9},{9,8},{10,11... | collective-permute-start | bytes 6291464 | tf_op jit(solution)/shard_map/ppermute | solution.py:239
  50.6 25.2 %collective-permute-start.9 = (bf16[256,4096]{1,0:T(8,128)(2,1)}, bf16[256,4096]{1,0:T(8,128)(2,1)}, u32[]{:S(2)}, u32[]{:S(2)}) collective-permute-start(bf16[256,4096]{1,0:T(8,128)(2,1)} %refs_7_.1), channel_id=1, source_target_pairs={{0,1},{1,0},{2,3},{3,2},{4,5},{5,4},{6,7},{7,6},{8,9},{9,8},{10,11... | collective-permute-start | bytes 6291464 | tf_op jit(solution)/shard_map/ppermute | solution.py:240
  52.6 9.1 %collective-permute-start.4 = (bf16[32,4096]{1,0:T(8,128)(2,1)S(1)}, bf16[32,4096]{1,0:T(8,128)(2,1)S(1)}, u32[]{:S(2)}, u32[]{:S(2)}) collective-permute-start(bf16[32,4096]{1,0:T(8,128)(2,1)S(1)} %collective-permute-done.3.refs_0_), channel_id=1, source_target_pairs={{0,2},{1,271},{2,4},{3,1},{4,6},{5,3},{6,8},{7,5},{8,10},{9,7},{10... | collective-permute-start | bytes 786440 | tf_op jit(solution)/shard_map/ppermute | solution.py:30
  56.7 12.4 %collective-permute-start.5 = (bf16[32,4096]{1,0:T(8,128)(2,1)S(1)}, bf16[32,4096]{1,0:T(8,128)(2,1)S(1)}, u32[]{:S(2)}, u32[]{:S(2)}) collective-permute-start(bf16[32,4096]{1,0:T(8,128)(2,1)S(1)} %collective-permute-done.3.refs_0_), channel_id=1, source_target_pairs={{0,4},{1,269},{2,6},{3,271},{4,8},{5,1},{6,10},{7,3},{8,12},{9,5},... | collective-permute-start | bytes 786440 | tf_op jit(solution)/shard_map/ppermute | solution.py:30
  59.7 10.6 %collective-permute-start.7 = (bf16[32,4096]{1,0:T(8,128)(2,1)S(1)}, bf16[32,4096]{1,0:T(8,128)(2,1)S(1)}, u32[]{:S(2)}, u32[]{:S(2)}) collective-permute-start(bf16[32,4096]{1,0:T(8,128)(2,1)S(1)} %collective-permute-done.6.refs_1_), channel_id=1, source_target_pairs={{0,270},{1,3},{2,0},{3,5},{4,2},{5,7},{6,4},{7,9},{8,6},{9,11},{10... | collective-permute-start | bytes 786440 | tf_op jit(solution)/shard_map/ppermute | solution.py:30
  70.3 5.5 %collective-permute-start.10 = (bf16[16,2,2,48,256]{4,3,2,1,0:T(8,128)(2,1)S(1)}, bf16[16,2,2,48,256]{4,3,2,1,0:T(8,128)(2,1)S(1)}, u32[]{:S(2)}, u32[]{:S(2)}) collective-permute-start(bf16[16,2,2,48,256]{4,3,2,1,0:T(8,128)(2,1)S(1)} %all-to-all-done.refs_4_.refs_9_), channel_id=1, source_target_pairs={{0,1},{1,0},{2,3},{3,2},{4,5},{5,4},{6,7},{7,6},{8,9},{9,8},{10,11... | collective-permute-start | bytes 4718600 | tf_op jit(solution)/shard_map/ppermute | solution.py:257
  75.8 12.9 %copy-start = (bf16[32,4096]{1,0:T(8,128)(2,1)S(1)}, bf16[32,4096]{1,0:T(8,128)(2,1)}, u32[]{:S(2)}) copy-start(bf16[32,4096]{1,0:T(8,128)(2,1)} %get-tuple-element.35.refs_4_) | copy-start | bytes 786436
  80.3 15.7 %collective-permute-start.11 = (bf16[32,4096]{1,0:T(8,128)(2,1)S(1)}, bf16[32,4096]{1,0:T(8,128)(2,1)S(1)}, u32[]{:S(2)}, u32[]{:S(2)}) collective-permute-start(bf16[32,4096]{1,0:T(8,128)(2,1)S(1)} %get-tuple-element.45), channel_id=1, source_target_pairs={{0,270},{1,3},{2,0},{3,5},{4,2},{5,7},{6,4},{7,9},{8,6},{9,11},{10... | collective-permute-start | bytes 786440 | tf_op jit(solution)/shard_map/ppermute | solution.py:30
  83.1 12.9 %collective-permute-start.12 = (bf16[32,4096]{1,0:T(8,128)(2,1)S(1)}, bf16[32,4096]{1,0:T(8,128)(2,1)S(1)}, u32[]{:S(2)}, u32[]{:S(2)}) collective-permute-start(bf16[32,4096]{1,0:T(8,128)(2,1)S(1)} %get-tuple-element.46), channel_id=1, source_target_pairs={{0,2},{1,271},{2,4},{3,1},{4,6},{5,3},{6,8},{7,5},{8,10},{9,7},{10... | collective-permute-start | bytes 786440 | tf_op jit(solution)/shard_map/ppermute | solution.py:30
  86.8 12.9 %collective-permute-start.13 = (bf16[32,4096]{1,0:T(8,128)(2,1)S(1)}, bf16[32,4096]{1,0:T(8,128)(2,1)S(1)}, u32[]{:S(2)}, u32[]{:S(2)}) collective-permute-start(bf16[32,4096]{1,0:T(8,128)(2,1)S(1)} %get-tuple-element.47), channel_id=1, source_target_pairs={{0,268},{1,5},{2,270},{3,7},{4,0},{5,9},{6,2},{7,11},{8,4},{9,13},... | collective-permute-start | bytes 786440 | tf_op jit(solution)/shard_map/ppermute | solution.py:30
  99.8 8.9 %collective-permute-start.14 = (bf16[32,4096]{1,0:T(8,128)(2,1)S(1)}, bf16[32,4096]{1,0:T(8,128)(2,1)S(1)}, u32[]{:S(2)}, u32[]{:S(2)}) collective-permute-start(bf16[32,4096]{1,0:T(8,128)(2,1)S(1)} %add_convert_fusion.4), channel_id=1, source_target_pairs={{0,270},{1,3},{2,0},{3,5},{4,2},{5,7},{6,4},{7,9},{8,6},{9,11},{10... | collective-permute-start | bytes 786440 | tf_op jit(solution)/shard_map/ppermute | solution.py:30
  101.8 10.2 %collective-permute-start.15 = (bf16[32,4096]{1,0:T(8,128)(2,1)S(1)}, bf16[32,4096]{1,0:T(8,128)(2,1)S(1)}, u32[]{:S(2)}, u32[]{:S(2)}) collective-permute-start(bf16[32,4096]{1,0:T(8,128)(2,1)S(1)} %add_convert_fusion.3), channel_id=1, source_target_pairs={{0,2},{1,271},{2,4},{3,1},{4,6},{5,3},{6,8},{7,5},{8,10},{9,7},{10... | collective-permute-start | bytes 786440 | tf_op jit(solution)/shard_map/ppermute | solution.py:30
  112.1 7.9 %collective-permute-start.17 = (bf16[32,4096]{1,0:T(8,128)(2,1)S(1)}, bf16[32,4096]{1,0:T(8,128)(2,1)S(1)}, u32[]{:S(2)}, u32[]{:S(2)}) collective-permute-start(bf16[32,4096]{1,0:T(8,128)(2,1)S(1)} %add_convert_fusion.1), channel_id=1, source_target_pairs={{0,2},{1,271},{2,4},{3,1},{4,6},{5,3},{6,8},{7,5},{8,10},{9,7},{10... | collective-permute-start | bytes 786440 | tf_op jit(solution)/shard_map/ppermute | solution.py:30
  116.7 9.8 %collective-permute-start.16 = (bf16[32,4096]{1,0:T(8,128)(2,1)S(1)}, bf16[32,4096]{1,0:T(8,128)(2,1)S(1)}, u32[]{:S(2)}, u32[]{:S(2)}) collective-permute-start(bf16[32,4096]{1,0:T(8,128)(2,1)S(1)} %add_convert_fusion.2), channel_id=1, source_target_pairs={{0,270},{1,3},{2,0},{3,5},{4,2},{5,7},{6,4},{7,9},{8,6},{9,11},{10... | collective-permute-start | bytes 786440 | tf_op jit(solution)/shard_map/ppermute | solution.py:30

commit v6 on v5

--- a/solution.py
+++ b/solution.py
@@ -232,10 +232,10 @@
         name="prepare",
     )(tokens.reshape(rows, 4096), gain.reshape(1, 4096), keys.reshape(48, 256), values.reshape(48, 256), pos)
 
-    a1, b1 = along(own, 1), along(own, -1)
+    b1, a1 = along(own, -1), along(own, 1)
 
     theirs = lax.ppermute(mine, "zh", SWAP)
-    theirs, a1, b1 = lax.optimization_barrier((theirs, a1, b1))
+    theirs, b1, a1 = lax.optimization_barrier((theirs, b1, a1))
     wq_other = lax.ppermute(wq, "c", SWAP)
     wo_other = lax.ppermute(wo, "c", SWAP)
     kv, bound = pl.pallas_call(
@@ -253,7 +253,7 @@
     a2, b2 = along(a1, 1), along(b1, -1)
     a3, b3 = along(a2, 1), along(b2, -1)
     a4 = along(a2, 2)
-    kv, a3, a4, b3 = lax.optimization_barrier((kv, a3, a4, b3))
+    kv, a4, a3, b3 = lax.optimization_barrier((kv, a4, a3, b3))
     kv_other = lax.ppermute(kv, "c", SWAP)
 
     given = ((wq, wq_other), (wo, wo_other), (kv, kv_other), bound)
@@ -263,8 +263,8 @@
     wide = lambda v: v.astype(jnp.float32)
     thin = lambda v: v.astype(jnp.bfloat16)
     plus = lambda u, v: thin(wide(u) + wide(v))
-    ap, bp, mid = along(far[1], -1), along(far[2], 1), along(far[0], -2)
-    ap, bp, mid, near = lax.optimization_barrier((ap, bp, mid, near))
+    mid, ap, bp = along(far[0], -2), along(far[1], -1), along(far[2], 1)
+    mid, ap, bp, near = lax.optimization_barrier((mid, ap, bp, near))
     ap, bp = along(thin(wide(near[0]) + wide(ap) + wide(mid)), -1), along(plus(near[1], bp), 1)
     ap, bp = lax.optimization_barrier((ap, bp))
     ap, bp = along(plus(near[2], ap), -1), along(plus(near[3], bp), 1)

time: 128 us -> 125 us (0.977)
  waiting for transfers between devices: 30.7 us -> 26.6 us
  starting transfers between devices: 75.3 us -> 76.7 us
    ppermute x14, waiting for transfers between devices: 25.2 us -> 22.3 us  [along(): return lax.ppermute(x, RING + ('c',), opposite(step))]
    ppermute x1, starting transfers between devices: 2.91 us -> 4.34 us  [per_device(): wq_other = lax.ppermute(wq, 'c', SWAP)]
where the time goes in v6:
time: 125 us
  starting transfers between devices  76.7 us (61%)
  waiting for transfers between devices  26.6 us (21%)
  Pallas kernels  18.4 us (15%)
    ppermute x14, starting transfers between devices, along(): return lax.ppermute(x, RING + ('c',), opposite(step))  52.9 us
    ppermute x14, waiting for transfers between devices, along(): return lax.ppermute(x, RING + ('c',), opposite(step))  22.3 us
    ppermute x1, starting transfers between devices, per_device(): theirs = lax.ppermute(mine, 'zh', SWAP)  8.89 us
    pallas_call x1, Pallas kernels, attend(): pl.pallas_call(functools.partial(attend_kernel, count, first), out_shape=...  7.25 us
    all_to_all x1, starting transfers between devices, per_device(): kv = lax.all_to_all(kv, ('y', 'x'), 0, 0, tiled=True)  6.75 us
    pallas_call x1, Pallas kernels, finish(): pl.pallas_call(functools.partial(finish_kernel, count, first), out_shape=...  4.45 us
    ppermute x1, starting transfers between devices, per_device(): wq_other = lax.ppermute(wq, 'c', SWAP)  4.34 us
    ppermute x1, waiting for transfers between devices, per_device(): theirs = lax.ppermute(mine, 'zh', SWAP)  4.3 us
  transfers between devices with their start and end apart: 19, of which 8 were waited for; matrix products, arithmetic and copies ran while one was open for 0% of the time, Pallas kernels for 9%

profile of v6, /device:TPU:1, one launch (start us, length us, event | category | flops | bytes accessed | tf_op | source)
XLA Modules:
  0.0 124.6 jit_solution(2825838774560558709)
XLA Ops:
  1.9 4.4 %collective-permute-start.1 = (bf16[32,4096]{1,0:T(8,128)(2,1)}, bf16[32,4096]{1,0:T(8,128)(2,1)S(1)}, u32[]{:S(2)}, u32[]{:S(2)}) collective-permute-start(bf16[32,4096]{1,0:T(8,128)(2,1)} %get-tuple-element.35.refs_4_), channel_id=1, source_target_pairs={{0,270},{1,3},{2,0},{3,5},{4,2},{5,7},{6,4},{7,9},{8,6},{9,11},{10... | collective-permute-start | bytes 786440 | tf_op jit(solution)/shard_map/ppermute | solution.py:30
  6.2 9.5 %collective-permute-start.2 = (bf16[32,4096]{1,0:T(8,128)(2,1)}, bf16[32,4096]{1,0:T(8,128)(2,1)S(1)}, u32[]{:S(2)}, u32[]{:S(2)}) collective-permute-start(bf16[32,4096]{1,0:T(8,128)(2,1)} %get-tuple-element.35.refs_4_), channel_id=1, source_target_pairs={{0,2},{1,271},{2,4},{3,1},{4,6},{5,3},{6,8},{7,5},{8,10},{9,7},{10... | collective-permute-start | bytes 786440 | tf_op jit(solution)/shard_map/ppermute | solution.py:30
  15.7 8.9 %collective-permute-start = (bf16[112,256]{1,0:T(8,128)(2,1)}, bf16[112,256]{1,0:T(8,128)(2,1)S(1)}, u32[]{:S(2)}, u32[]{:S(2)}) collective-permute-start(bf16[112,256]{1,0:T(8,128)(2,1)} %get-tuple-element.34.mine), channel_id=1, source_target_pairs={{0,256},{256,0},{1,257},{257,1},{2,258},{258,2},{3,259},{259,3},{4... | collective-permute-start | bytes 172040 | tf_op jit(solution)/shard_map/ppermute | solution.py:237
  25.3 4.3 %collective-permute-done.theirs = bf16[112,256]{1,0:T(8,128)(2,1)S(1)} collective-permute-done((bf16[112,256]{1,0:T(8,128)(2,1)}, bf16[112,256]{1,0:T(8,128)(2,1)S(1)}, u32[]{:S(2)}, u32[]{:S(2)}) %collective-permute-start) | collective-permute-done | bytes 57376 | tf_op jit(solution)/shard_map/ppermute | solution.py:237
  31.7 6.8 %all-to-all-start = ((bf16[16,2,2,48,256]{4,3,2,1,0:T(8,128)(2,1)}), bf16[16,2,2,48,256]{4,3,2,1,0:T(8,128)(2,1)S(1)}, u32[]{:S(2)}, u32[]{:S(2)}) async-start(bf16[16,2,2,48,256]{4,3,2,1,0:T(8,128)(2,1)} %get-tuple-element.37), calls=%async_computation | async-start | bytes 3145728 | tf_op jit(solution)/shard_map/all_to_all | solution.py:252
  38.5 5.7 %collective-permute-start.3 = (bf16[32,4096]{1,0:T(8,128)(2,1)S(1)}, bf16[32,4096]{1,0:T(8,128)(2,1)S(1)}, u32[]{:S(2)}, u32[]{:S(2)}) collective-permute-start(bf16[32,4096]{1,0:T(8,128)(2,1)S(1)} %collective-permute-done.2.refs_2_), channel_id=1, source_target_pairs={{0,2},{1,271},{2,4},{3,1},{4,6},{5,3},{6,8},{7,5},{8,10},{9,7},{10... | collective-permute-start | bytes 786440 | tf_op jit(solution)/shard_map/ppermute | solution.py:30
  44.2 1.9 %collective-permute-start.6 = (bf16[32,4096]{1,0:T(8,128)(2,1)S(1)}, bf16[32,4096]{1,0:T(8,128)(2,1)S(1)}, u32[]{:S(2)}, u32[]{:S(2)}) collective-permute-start(bf16[32,4096]{1,0:T(8,128)(2,1)S(1)} %collective-permute-done.1.refs_3_), channel_id=1, source_target_pairs={{0,270},{1,3},{2,0},{3,5},{4,2},{5,7},{6,4},{7,9},{8,6},{9,11},{10... | collective-permute-start | bytes 786440 | tf_op jit(solution)/shard_map/ppermute | solution.py:30
  46.1 4.3 %collective-permute-start.8 = (bf16[4096,256]{1,0:T(8,128)(2,1)}, bf16[4096,256]{1,0:T(8,128)(2,1)}, u32[]{:S(2)}, u32[]{:S(2)}) collective-permute-start(bf16[4096,256]{1,0:T(8,128)(2,1)} %refs_5_.1), channel_id=1, source_target_pairs={{0,1},{1,0},{2,3},{3,2},{4,5},{5,4},{6,7},{7,6},{8,9},{9,8},{10,11... | collective-permute-start | bytes 6291464 | tf_op jit(solution)/shard_map/ppermute | solution.py:239
  50.5 1.9 %collective-permute-start.9 = (bf16[256,4096]{1,0:T(8,128)(2,1)}, bf16[256,4096]{1,0:T(8,128)(2,1)}, u32[]{:S(2)}, u32[]{:S(2)}) collective-permute-start(bf16[256,4096]{1,0:T(8,128)(2,1)} %refs_7_.1), channel_id=1, source_target_pairs={{0,1},{1,0},{2,3},{3,2},{4,5},{5,4},{6,7},{7,6},{8,9},{9,8},{10,11... | collective-permute-start | bytes 6291464 | tf_op jit(solution)/shard_map/ppermute | solution.py:240
  52.4 3.5 %collective-permute-start.4 = (bf16[32,4096]{1,0:T(8,128)(2,1)S(1)}, bf16[32,4096]{1,0:T(8,128)(2,1)S(1)}, u32[]{:S(2)}, u32[]{:S(2)}) collective-permute-start(bf16[32,4096]{1,0:T(8,128)(2,1)S(1)} %collective-permute-done.3.refs_0_), channel_id=1, source_target_pairs={{0,4},{1,269},{2,6},{3,271},{4,8},{5,1},{6,10},{7,3},{8,12},{9,5},... | collective-permute-start | bytes 786440 | tf_op jit(solution)/shard_map/ppermute | solution.py:30
  55.9 3.1 %collective-permute-start.5 = (bf16[32,4096]{1,0:T(8,128)(2,1)S(1)}, bf16[32,4096]{1,0:T(8,128)(2,1)S(1)}, u32[]{:S(2)}, u32[]{:S(2)}) collective-permute-start(bf16[32,4096]{1,0:T(8,128)(2,1)S(1)} %collective-permute-done.3.refs_0_), channel_id=1, source_target_pairs={{0,2},{1,271},{2,4},{3,1},{4,6},{5,3},{6,8},{7,5},{8,10},{9,7},{10... | collective-permute-start | bytes 786440 | tf_op jit(solution)/shard_map/ppermute | solution.py:30
  59.0 2.1 %collective-permute-start.7 = (bf16[32,4096]{1,0:T(8,128)(2,1)S(1)}, bf16[32,4096]{1,0:T(8,128)(2,1)S(1)}, u32[]{:S(2)}, u32[]{:S(2)}) collective-permute-start(bf16[32,4096]{1,0:T(8,128)(2,1)S(1)} %collective-permute-done.6.refs_1_), channel_id=1, source_target_pairs={{0,270},{1,3},{2,0},{3,5},{4,2},{5,7},{6,4},{7,9},{8,6},{9,11},{10... | collective-permute-start | bytes 786440 | tf_op jit(solution)/shard_map/ppermute | solution.py:30
  61.8 7.5 %collective-permute-done.5.refs_1_ = bf16[32,4096]{1,0:T(8,128)(2,1)S(1)} collective-permute-done((bf16[32,4096]{1,0:T(8,128)(2,1)S(1)}, bf16[32,4096]{1,0:T(8,128)(2,1)S(1)}, u32[]{:S(2)}, u32[]{:S(2)}) %collective-permute-start.5) | collective-permute-done | bytes 262176 | tf_op jit(solution)/shard_map/ppermute | solution.py:30
  71.2 3.6 %begin3.1.refs_8_ = bf16[96,256]{1,0:T(8,128)(2,1)S(1)} custom-call(bf16[32,4096]{1,0:T(8,128)(2,1)S(1)} %collective-permute-done.4.refs_0_, bf16[32,4096]{1,0:T(8,128)(2,1)S(1)} %collective-permute-done.5.refs_1_, bf16[32,4096]{1,0:T(8,128)(2,1)S(1)} %collective-permute-done.7.refs_2_, bf16[4096,256]{1,0:T(8,128)(2,1)} %refs_5_.1, ...), custom_call_target="tpu_custom_call" | custom-call | flops 402653184 | bytes 4194304 | tf_op jit(solution)/shard_map/begin3/pallas_call | solution.py:169
  74.9 4.5 %finish3.1 = (bf16[32,4096]{1,0:T(8,128)(2,1)S(1)}, bf16[32,4096]{1,0:T(8,128)(2,1)S(1)}, bf16[32,4096]{1,0:T(8,128)(2,1)S(1)}) custom-call(bf16[32,4096]{1,0:T(8,128)(2,1)S(1)} %collective-permute-done.4.refs_0_, bf16[32,4096]{1,0:T(8,128)(2,1)S(1)} %collective-permute-done.5.refs_1_, bf16[32,4096]{1,0:T(8,128)(2,1)S(1)} %collective-permute-done.7.refs_2_, ...), custom_call_target="tpu_custom_call" | custom-call | flops 805306368 | bytes 8388608 | tf_op jit(solution)/shard_map/finish3/pallas_call | solution.py:186
  79.3 1.9 %collective-permute-start.11 = (bf16[32,4096]{1,0:T(8,128)(2,1)S(1)}, bf16[32,4096]{1,0:T(8,128)(2,1)S(1)}, u32[]{:S(2)}, u32[]{:S(2)}) collective-permute-start(bf16[32,4096]{1,0:T(8,128)(2,1)S(1)} %get-tuple-element.45), channel_id=1, source_target_pairs={{0,268},{1,5},{2,270},{3,7},{4,0},{5,9},{6,2},{7,11},{8,4},{9,13},... | collective-permute-start | bytes 786440 | tf_op jit(solution)/shard_map/ppermute | solution.py:30
  81.2 2.8 %collective-permute-start.12 = (bf16[32,4096]{1,0:T(8,128)(2,1)S(1)}, bf16[32,4096]{1,0:T(8,128)(2,1)S(1)}, u32[]{:S(2)}, u32[]{:S(2)}) collective-permute-start(bf16[32,4096]{1,0:T(8,128)(2,1)S(1)} %get-tuple-element.46), channel_id=1, source_target_pairs={{0,270},{1,3},{2,0},{3,5},{4,2},{5,7},{6,4},{7,9},{8,6},{9,11},{10... | collective-permute-start | bytes 786440 | tf_op jit(solution)/shard_map/ppermute | solution.py:30
  84.1 3.7 %collective-permute-start.13 = (bf16[32,4096]{1,0:T(8,128)(2,1)S(1)}, bf16[32,4096]{1,0:T(8,128)(2,1)S(1)}, u32[]{:S(2)}, u32[]{:S(2)}) collective-permute-start(bf16[32,4096]{1,0:T(8,128)(2,1)S(1)} %get-tuple-element.47), channel_id=1, source_target_pairs={{0,2},{1,271},{2,4},{3,1},{4,6},{5,3},{6,8},{7,5},{8,10},{9,7},{10... | collective-permute-start | bytes 786440 | tf_op jit(solution)/shard_map/ppermute | solution.py:30
  87.8 7.2 %attend5.1 = (bf16[32,4096]{1,0:T(8,128)(2,1)S(1)}, bf16[32,4096]{1,0:T(8,128)(2,1)S(1)}, bf16[32,4096]{1,0:T(8,128)(2,1)S(1)}, bf16[32,4096]{1,0:T(8,128)(2,1)S(1)}, bf16[32,4096]{1,0:T(8,128)(2,1)S(1)}) custom-call(bf16[32,4096]{1,0:T(8,128)(2,1)S(1)} %collective-permute-done.3.refs_0_, bf16[32,4096]{1,0:T(8,128)(2,1)S(1)} %collective-permute-done.6.refs_1_, ...), custom_call_target="tpu_custom_call" | custom-call | flops 2013265920 | bytes 12582912 | tf_op jit(solution)/shard_map/attend5/pallas_call | solution.py:205
  95.8 3.1 %collective-permute-start.14 = (bf16[32,4096]{1,0:T(8,128)(2,1)S(1)}, bf16[32,4096]{1,0:T(8,128)(2,1)S(1)}, u32[]{:S(2)}, u32[]{:S(2)}) collective-permute-start(bf16[32,4096]{1,0:T(8,128)(2,1)S(1)} %add_convert_fusion.4), channel_id=1, source_target_pairs={{0,270},{1,3},{2,0},{3,5},{4,2},{5,7},{6,4},{7,9},{8,6},{9,11},{10... | collective-permute-start | bytes 786440 | tf_op jit(solution)/shard_map/ppermute | solution.py:30
  98.9 4.2 %collective-permute-start.15 = (bf16[32,4096]{1,0:T(8,128)(2,1)S(1)}, bf16[32,4096]{1,0:T(8,128)(2,1)S(1)}, u32[]{:S(2)}, u32[]{:S(2)}) collective-permute-start(bf16[32,4096]{1,0:T(8,128)(2,1)S(1)} %add_convert_fusion.3), channel_id=1, source_target_pairs={{0,2},{1,271},{2,4},{3,1},{4,6},{5,3},{6,8},{7,5},{8,10},{9,7},{10... | collective-permute-start | bytes 786440 | tf_op jit(solution)/shard_map/ppermute | solution.py:30
  104.9 4.0 %collective-permute-done.15 = bf16[32,4096]{1,0:T(8,128)(2,1)S(1)} collective-permute-done((bf16[32,4096]{1,0:T(8,128)(2,1)S(1)}, bf16[32,4096]{1,0:T(8,128)(2,1)S(1)}, u32[]{:S(2)}, u32[]{:S(2)}) %collective-permute-start.15) | collective-permute-done | bytes 262176 | tf_op jit(solution)/shard_map/ppermute | solution.py:30
  108.9 5.0 %collective-permute-start.17 = (bf16[32,4096]{1,0:T(8,128)(2,1)S(1)}, bf16[32,4096]{1,0:T(8,128)(2,1)S(1)}, u32[]{:S(2)}, u32[]{:S(2)}) collective-permute-start(bf16[32,4096]{1,0:T(8,128)(2,1)S(1)} %add_convert_fusion.1), channel_id=1, source_target_pairs={{0,2},{1,271},{2,4},{3,1},{4,6},{5,3},{6,8},{7,5},{8,10},{9,7},{10... | collective-permute-start | bytes 786440 | tf_op jit(solution)/shard_map/ppermute | solution.py:30
  117.2 6.5 %collective-permute-done.16 = bf16[32,4096]{1,0:T(8,128)(2,1)S(1)} collective-permute-done((bf16[32,4096]{1,0:T(8,128)(2,1)S(1)}, bf16[32,4096]{1,0:T(8,128)(2,1)S(1)}, u32[]{:S(2)}, u32[]{:S(2)}) %collective-permute-start.16) | collective-permute-done | bytes 262176 | tf_op jit(solution)/shard_map/ppermute | solution.py:30
  (28 shorter events, 13.2 us)
Async XLA Ops:
  1.9 27.7 %collective-permute-start.1 = (bf16[32,4096]{1,0:T(8,128)(2,1)}, bf16[32,4096]{1,0:T(8,128)(2,1)S(1)}, u32[]{:S(2)}, u32[]{:S(2)}) collective-permute-start(bf16[32,4096]{1,0:T(8,128)(2,1)} %get-tuple-element.35.refs_4_), channel_id=1, source_target_pairs={{0,270},{1,3},{2,0},{3,5},{4,2},{5,7},{6,4},{7,9},{8,6},{9,11},{10... | collective-permute-start | bytes 786440 | tf_op jit(solution)/shard_map/ppermute | solution.py:30
  6.2 23.4 %collective-permute-start.2 = (bf16[32,4096]{1,0:T(8,128)(2,1)}, bf16[32,4096]{1,0:T(8,128)(2,1)S(1)}, u32[]{:S(2)}, u32[]{:S(2)}) collective-permute-start(bf16[32,4096]{1,0:T(8,128)(2,1)} %get-tuple-element.35.refs_4_), channel_id=1, source_target_pairs={{0,2},{1,271},{2,4},{3,1},{4,6},{5,3},{6,8},{7,5},{8,10},{9,7},{10... | collective-permute-start | bytes 786440 | tf_op jit(solution)/shard_map/ppermute | solution.py:30
  15.7 13.8 %collective-permute-start = (bf16[112,256]{1,0:T(8,128)(2,1)}, bf16[112,256]{1,0:T(8,128)(2,1)S(1)}, u32[]{:S(2)}, u32[]{:S(2)}) collective-permute-start(bf16[112,256]{1,0:T(8,128)(2,1)} %get-tuple-element.34.mine), channel_id=1, source_target_pairs={{0,256},{256,0},{1,257},{257,1},{2,258},{258,2},{3,259},{259,3},{4... | collective-permute-start | bytes 172040 | tf_op jit(solution)/shard_map/ppermute | solution.py:237
  29.6 0.8 copy-start.1
  31.7 37.6 %all-to-all-start = ((bf16[16,2,2,48,256]{4,3,2,1,0:T(8,128)(2,1)}), bf16[16,2,2,48,256]{4,3,2,1,0:T(8,128)(2,1)S(1)}, u32[]{:S(2)}, u32[]{:S(2)}) async-start(bf16[16,2,2,48,256]{4,3,2,1,0:T(8,128)(2,1)} %get-tuple-element.37), calls=%async_computation | async-start | bytes 3145728 | tf_op jit(solution)/shard_map/all_to_all | solution.py:252
  38.5 13.9 %collective-permute-start.3 = (bf16[32,4096]{1,0:T(8,128)(2,1)S(1)}, bf16[32,4096]{1,0:T(8,128)(2,1)S(1)}, u32[]{:S(2)}, u32[]{:S(2)}) collective-permute-start(bf16[32,4096]{1,0:T(8,128)(2,1)S(1)} %collective-permute-done.2.refs_2_), channel_id=1, source_target_pairs={{0,2},{1,271},{2,4},{3,1},{4,6},{5,3},{6,8},{7,5},{8,10},{9,7},{10... | collective-permute-start | bytes 786440 | tf_op jit(solution)/shard_map/ppermute | solution.py:30
  44.2 14.8 %collective-permute-start.6 = (bf16[32,4096]{1,0:T(8,128)(2,1)S(1)}, bf16[32,4096]{1,0:T(8,128)(2,1)S(1)}, u32[]{:S(2)}, u32[]{:S(2)}) collective-permute-start(bf16[32,4096]{1,0:T(8,128)(2,1)S(1)} %collective-permute-done.1.refs_3_), channel_id=1, source_target_pairs={{0,270},{1,3},{2,0},{3,5},{4,2},{5,7},{6,4},{7,9},{8,6},{9,11},{10... | collective-permute-start | bytes 786440 | tf_op jit(solution)/shard_map/ppermute | solution.py:30
  46.1 28.7 %collective-permute-start.8 = (bf16[4096,256]{1,0:T(8,128)(2,1)}, bf16[4096,256]{1,0:T(8,128)(2,1)}, u32[]{:S(2)}, u32[]{:S(2)}) collective-permute-start(bf16[4096,256]{1,0:T(8,128)(2,1)} %refs_5_.1), channel_id=1, source_target_pairs={{0,1},{1,0},{2,3},{3,2},{4,5},{5,4},{6,7},{7,6},{8,9},{9,8},{10,11... | collective-permute-start | bytes 6291464 | tf_op jit(solution)/shard_map/ppermute | solution.py:239
  50.5 24.4 %collective-permute-start.9 = (bf16[256,4096]{1,0:T(8,128)(2,1)}, bf16[256,4096]{1,0:T(8,128)(2,1)}, u32[]{:S(2)}, u32[]{:S(2)}) collective-permute-start(bf16[256,4096]{1,0:T(8,128)(2,1)} %refs_7_.1), channel_id=1, source_target_pairs={{0,1},{1,0},{2,3},{3,2},{4,5},{5,4},{6,7},{7,6},{8,9},{9,8},{10,11... | collective-permute-start | bytes 6291464 | tf_op jit(solution)/shard_map/ppermute | solution.py:240
  52.4 9.4 %collective-permute-start.4 = (bf16[32,4096]{1,0:T(8,128)(2,1)S(1)}, bf16[32,4096]{1,0:T(8,128)(2,1)S(1)}, u32[]{:S(2)}, u32[]{:S(2)}) collective-permute-start(bf16[32,4096]{1,0:T(8,128)(2,1)S(1)} %collective-permute-done.3.refs_0_), channel_id=1, source_target_pairs={{0,4},{1,269},{2,6},{3,271},{4,8},{5,1},{6,10},{7,3},{8,12},{9,5},... | collective-permute-start | bytes 786440 | tf_op jit(solution)/shard_map/ppermute | solution.py:30
  55.9 13.4 %collective-permute-start.5 = (bf16[32,4096]{1,0:T(8,128)(2,1)S(1)}, bf16[32,4096]{1,0:T(8,128)(2,1)S(1)}, u32[]{:S(2)}, u32[]{:S(2)}) collective-permute-start(bf16[32,4096]{1,0:T(8,128)(2,1)S(1)} %collective-permute-done.3.refs_0_), channel_id=1, source_target_pairs={{0,2},{1,271},{2,4},{3,1},{4,6},{5,3},{6,8},{7,5},{8,10},{9,7},{10... | collective-permute-start | bytes 786440 | tf_op jit(solution)/shard_map/ppermute | solution.py:30
  59.0 10.3 %collective-permute-start.7 = (bf16[32,4096]{1,0:T(8,128)(2,1)S(1)}, bf16[32,4096]{1,0:T(8,128)(2,1)S(1)}, u32[]{:S(2)}, u32[]{:S(2)}) collective-permute-start(bf16[32,4096]{1,0:T(8,128)(2,1)S(1)} %collective-permute-done.6.refs_1_), channel_id=1, source_target_pairs={{0,270},{1,3},{2,0},{3,5},{4,2},{5,7},{6,4},{7,9},{8,6},{9,11},{10... | collective-permute-start | bytes 786440 | tf_op jit(solution)/shard_map/ppermute | solution.py:30
  69.3 5.5 %collective-permute-start.10 = (bf16[16,2,2,48,256]{4,3,2,1,0:T(8,128)(2,1)S(1)}, bf16[16,2,2,48,256]{4,3,2,1,0:T(8,128)(2,1)S(1)}, u32[]{:S(2)}, u32[]{:S(2)}) collective-permute-start(bf16[16,2,2,48,256]{4,3,2,1,0:T(8,128)(2,1)S(1)} %all-to-all-done.refs_4_.refs_9_), channel_id=1, source_target_pairs={{0,1},{1,0},{2,3},{3,2},{4,5},{5,4},{6,7},{7,6},{8,9},{9,8},{10,11... | collective-permute-start | bytes 4718600 | tf_op jit(solution)/shard_map/ppermute | solution.py:257
  74.8 13.0 %copy-start = (bf16[32,4096]{1,0:T(8,128)(2,1)S(1)}, bf16[32,4096]{1,0:T(8,128)(2,1)}, u32[]{:S(2)}) copy-start(bf16[32,4096]{1,0:T(8,128)(2,1)} %get-tuple-element.35.refs_4_) | copy-start | bytes 786436
  79.3 15.7 %collective-permute-start.11 = (bf16[32,4096]{1,0:T(8,128)(2,1)S(1)}, bf16[32,4096]{1,0:T(8,128)(2,1)S(1)}, u32[]{:S(2)}, u32[]{:S(2)}) collective-permute-start(bf16[32,4096]{1,0:T(8,128)(2,1)S(1)} %get-tuple-element.45), channel_id=1, source_target_pairs={{0,268},{1,5},{2,270},{3,7},{4,0},{5,9},{6,2},{7,11},{8,4},{9,13},... | collective-permute-start | bytes 786440 | tf_op jit(solution)/shard_map/ppermute | solution.py:30
  81.2 13.8 %collective-permute-start.12 = (bf16[32,4096]{1,0:T(8,128)(2,1)S(1)}, bf16[32,4096]{1,0:T(8,128)(2,1)S(1)}, u32[]{:S(2)}, u32[]{:S(2)}) collective-permute-start(bf16[32,4096]{1,0:T(8,128)(2,1)S(1)} %get-tuple-element.46), channel_id=1, source_target_pairs={{0,270},{1,3},{2,0},{3,5},{4,2},{5,7},{6,4},{7,9},{8,6},{9,11},{10... | collective-permute-start | bytes 786440 | tf_op jit(solution)/shard_map/ppermute | solution.py:30
  84.1 11.6 %collective-permute-start.13 = (bf16[32,4096]{1,0:T(8,128)(2,1)S(1)}, bf16[32,4096]{1,0:T(8,128)(2,1)S(1)}, u32[]{:S(2)}, u32[]{:S(2)}) collective-permute-start(bf16[32,4096]{1,0:T(8,128)(2,1)S(1)} %get-tuple-element.47), channel_id=1, source_target_pairs={{0,2},{1,271},{2,4},{3,1},{4,6},{5,3},{6,8},{7,5},{8,10},{9,7},{10... | collective-permute-start | bytes 786440 | tf_op jit(solution)/shard_map/ppermute | solution.py:30
  95.8 9.1 %collective-permute-start.14 = (bf16[32,4096]{1,0:T(8,128)(2,1)S(1)}, bf16[32,4096]{1,0:T(8,128)(2,1)S(1)}, u32[]{:S(2)}, u32[]{:S(2)}) collective-permute-start(bf16[32,4096]{1,0:T(8,128)(2,1)S(1)} %add_convert_fusion.4), channel_id=1, source_target_pairs={{0,270},{1,3},{2,0},{3,5},{4,2},{5,7},{6,4},{7,9},{8,6},{9,11},{10... | collective-permute-start | bytes 786440 | tf_op jit(solution)/shard_map/ppermute | solution.py:30
  98.9 9.9 %collective-permute-start.15 = (bf16[32,4096]{1,0:T(8,128)(2,1)S(1)}, bf16[32,4096]{1,0:T(8,128)(2,1)S(1)}, u32[]{:S(2)}, u32[]{:S(2)}) collective-permute-start(bf16[32,4096]{1,0:T(8,128)(2,1)S(1)} %add_convert_fusion.3), channel_id=1, source_target_pairs={{0,2},{1,271},{2,4},{3,1},{4,6},{5,3},{6,8},{7,5},{8,10},{9,7},{10... | collective-permute-start | bytes 786440 | tf_op jit(solution)/shard_map/ppermute | solution.py:30
  108.9 8.3 %collective-permute-start.17 = (bf16[32,4096]{1,0:T(8,128)(2,1)S(1)}, bf16[32,4096]{1,0:T(8,128)(2,1)S(1)}, u32[]{:S(2)}, u32[]{:S(2)}) collective-permute-start(bf16[32,4096]{1,0:T(8,128)(2,1)S(1)} %add_convert_fusion.1), channel_id=1, source_target_pairs={{0,2},{1,271},{2,4},{3,1},{4,6},{5,3},{6,8},{7,5},{8,10},{9,7},{10... | collective-permute-start | bytes 786440 | tf_op jit(solution)/shard_map/ppermute | solution.py:30
  114.0 9.8 %collective-permute-start.16 = (bf16[32,4096]{1,0:T(8,128)(2,1)S(1)}, bf16[32,4096]{1,0:T(8,128)(2,1)S(1)}, u32[]{:S(2)}, u32[]{:S(2)}) collective-permute-start(bf16[32,4096]{1,0:T(8,128)(2,1)S(1)} %add_convert_fusion.2), channel_id=1, source_target_pairs={{0,270},{1,3},{2,0},{3,5},{4,2},{5,7},{6,4},{7,9},{8,6},{9,11},{10... | collective-permute-start | bytes 786440 | tf_op jit(solution)/shard_map/ppermute | solution.py:30

commit v7 on v4

--- a/solution.py
+++ b/solution.py
@@ -188,8 +188,8 @@
     wide = lambda v: v.astype(jnp.float32)
     thin = lambda v: v.astype(jnp.bfloat16)
     plus = lambda u, v: thin(wide(u) + wide(v))
-    ap, bp, mid = along(far[1], -1), along(far[2], 1), along(far[0], -2)
-    ap, bp, mid, near = lax.optimization_barrier((ap, bp, mid, near))
+    mid, ap, bp = along(far[0], -2), along(far[1], -1), along(far[2], 1)
+    mid, ap, bp, near = lax.optimization_barrier((mid, ap, bp, near))
     ap, bp = along(thin(wide(near[0]) + wide(ap) + wide(mid)), -1), along(plus(near[1], bp), 1)
     ap, bp = lax.optimization_barrier((ap, bp))
     ap, bp = along(plus(near[2], ap), -1), along(plus(near[3], bp), 1)

time: 126 us -> 124 us (0.984)
  waiting for transfers between devices: 32.5 us -> 28.9 us
  starting transfers between devices: 73 us -> 75 us
    ppermute x14, waiting for transfers between devices: 24.9 us -> 21.2 us  [along(): return lax.ppermute(x, RING + ('c',), opposite(step))]
    ppermute x14, starting transfers between devices: 49.2 us -> 51.2 us  [along(): return lax.ppermute(x, RING + ('c',), opposite(step))]
where the time goes in v7:
time: 124 us
  starting transfers between devices  75 us (60%)
  waiting for transfers between devices  28.9 us (23%)
  Pallas kernels  16.8 us (14%)
    ppermute x14, starting transfers between devices, along(): return lax.ppermute(x, RING + ('c',), opposite(step))  51.2 us
    ppermute x14, waiting for transfers between devices, along(): return lax.ppermute(x, RING + ('c',), opposite(step))  21.2 us
    pallas_call x2, Pallas kernels, attend(): pl.pallas_call(functools.partial(attend_kernel, count, first), out_shape=...  13.7 us
    ppermute x1, starting transfers between devices, per_device(): theirs = lax.ppermute(mine, 'zh', SWAP)  8.89 us
    all_to_all x1, starting transfers between devices, per_device(): kv = lax.all_to_all(kv, ('y', 'x'), 0, 0, tiled=True)  6.75 us
    ppermute x1, starting transfers between devices, per_device(): wq_other = lax.ppermute(wq, 'c', SWAP)  4.34 us
    ppermute x1, waiting for transfers between devices, per_device(): theirs = lax.ppermute(mine, 'zh', SWAP)  4.3 us
    ppermute x1, waiting for transfers between devices, per_device(): kv_other = lax.ppermute(kv, 'c', SWAP)  3.35 us
  transfers between devices with their start and end apart: 19, of which 9 were waited for; matrix products, arithmetic and copies ran while one was open for 0% of the time, Pallas kernels for 6%

profile of v7, /device:TPU:1, one launch (start us, length us, event | category | flops | bytes accessed | tf_op | source)
XLA Modules:
  0.0 123.5 jit_solution(17869843846496922327)
XLA Ops:
  1.9 4.4 %collective-permute-start.2 = (bf16[32,4096]{1,0:T(8,128)(2,1)}, bf16[32,4096]{1,0:T(8,128)(2,1)S(1)}, u32[]{:S(2)}, u32[]{:S(2)}) collective-permute-start(bf16[32,4096]{1,0:T(8,128)(2,1)} %get-tuple-element.35.refs_4_), channel_id=1, source_target_pairs={{0,270},{1,3},{2,0},{3,5},{4,2},{5,7},{6,4},{7,9},{8,6},{9,11},{10... | collective-permute-start | bytes 786440 | tf_op jit(solution)/shard_map/ppermute | solution.py:30
  6.2 9.5 %collective-permute-start.1 = (bf16[32,4096]{1,0:T(8,128)(2,1)}, bf16[32,4096]{1,0:T(8,128)(2,1)S(1)}, u32[]{:S(2)}, u32[]{:S(2)}) collective-permute-start(bf16[32,4096]{1,0:T(8,128)(2,1)} %get-tuple-element.35.refs_4_), channel_id=1, source_target_pairs={{0,2},{1,271},{2,4},{3,1},{4,6},{5,3},{6,8},{7,5},{8,10},{9,7},{10... | collective-permute-start | bytes 786440 | tf_op jit(solution)/shard_map/ppermute | solution.py:30
  15.7 8.9 %collective-permute-start = (bf16[112,256]{1,0:T(8,128)(2,1)}, bf16[112,256]{1,0:T(8,128)(2,1)S(1)}, u32[]{:S(2)}, u32[]{:S(2)}) collective-permute-start(bf16[112,256]{1,0:T(8,128)(2,1)} %get-tuple-element.34.mine), channel_id=1, source_target_pairs={{0,256},{256,0},{1,257},{257,1},{2,258},{258,2},{3,259},{259,3},{4... | collective-permute-start | bytes 172040 | tf_op jit(solution)/shard_map/ppermute | solution.py:163
  25.3 4.3 %collective-permute-done.theirs = bf16[112,256]{1,0:T(8,128)(2,1)S(1)} collective-permute-done((bf16[112,256]{1,0:T(8,128)(2,1)}, bf16[112,256]{1,0:T(8,128)(2,1)S(1)}, u32[]{:S(2)}, u32[]{:S(2)}) %collective-permute-start) | collective-permute-done | bytes 57376 | tf_op jit(solution)/shard_map/ppermute | solution.py:163
  31.7 6.8 %all-to-all-start = ((bf16[16,2,2,48,256]{4,3,2,1,0:T(8,128)(2,1)}), bf16[16,2,2,48,256]{4,3,2,1,0:T(8,128)(2,1)S(1)}, u32[]{:S(2)}, u32[]{:S(2)}) async-start(bf16[16,2,2,48,256]{4,3,2,1,0:T(8,128)(2,1)} %get-tuple-element.37), calls=%async_computation | async-start | bytes 3145728 | tf_op jit(solution)/shard_map/all_to_all | solution.py:178
  38.5 5.7 %collective-permute-start.3 = (bf16[32,4096]{1,0:T(8,128)(2,1)S(1)}, bf16[32,4096]{1,0:T(8,128)(2,1)S(1)}, u32[]{:S(2)}, u32[]{:S(2)}) collective-permute-start(bf16[32,4096]{1,0:T(8,128)(2,1)S(1)} %collective-permute-done.1.refs_2_), channel_id=1, source_target_pairs={{0,2},{1,271},{2,4},{3,1},{4,6},{5,3},{6,8},{7,5},{8,10},{9,7},{10... | collective-permute-start | bytes 786440 | tf_op jit(solution)/shard_map/ppermute | solution.py:30
  44.2 1.9 %collective-permute-start.6 = (bf16[32,4096]{1,0:T(8,128)(2,1)S(1)}, bf16[32,4096]{1,0:T(8,128)(2,1)S(1)}, u32[]{:S(2)}, u32[]{:S(2)}) collective-permute-start(bf16[32,4096]{1,0:T(8,128)(2,1)S(1)} %collective-permute-done.2.refs_3_), channel_id=1, source_target_pairs={{0,270},{1,3},{2,0},{3,5},{4,2},{5,7},{6,4},{7,9},{8,6},{9,11},{10... | collective-permute-start | bytes 786440 | tf_op jit(solution)/shard_map/ppermute | solution.py:30
  46.1 4.3 %collective-permute-start.8 = (bf16[4096,256]{1,0:T(8,128)(2,1)}, bf16[4096,256]{1,0:T(8,128)(2,1)}, u32[]{:S(2)}, u32[]{:S(2)}) collective-permute-start(bf16[4096,256]{1,0:T(8,128)(2,1)} %refs_5_.3), channel_id=1, source_target_pairs={{0,1},{1,0},{2,3},{3,2},{4,5},{5,4},{6,7},{7,6},{8,9},{9,8},{10,11... | collective-permute-start | bytes 6291464 | tf_op jit(solution)/shard_map/ppermute | solution.py:165
  50.5 1.9 %collective-permute-start.9 = (bf16[256,4096]{1,0:T(8,128)(2,1)}, bf16[256,4096]{1,0:T(8,128)(2,1)}, u32[]{:S(2)}, u32[]{:S(2)}) collective-permute-start(bf16[256,4096]{1,0:T(8,128)(2,1)} %refs_7_.1), channel_id=1, source_target_pairs={{0,1},{1,0},{2,3},{3,2},{4,5},{5,4},{6,7},{7,6},{8,9},{9,8},{10,11... | collective-permute-start | bytes 6291464 | tf_op jit(solution)/shard_map/ppermute | solution.py:166
  52.4 3.5 %collective-permute-start.5 = (bf16[32,4096]{1,0:T(8,128)(2,1)S(1)}, bf16[32,4096]{1,0:T(8,128)(2,1)S(1)}, u32[]{:S(2)}, u32[]{:S(2)}) collective-permute-start(bf16[32,4096]{1,0:T(8,128)(2,1)S(1)} %collective-permute-done.3.refs_0_), channel_id=1, source_target_pairs={{0,4},{1,269},{2,6},{3,271},{4,8},{5,1},{6,10},{7,3},{8,12},{9,5},... | collective-permute-start | bytes 786440 | tf_op jit(solution)/shard_map/ppermute | solution.py:30
  55.9 3.1 %collective-permute-start.4 = (bf16[32,4096]{1,0:T(8,128)(2,1)S(1)}, bf16[32,4096]{1,0:T(8,128)(2,1)S(1)}, u32[]{:S(2)}, u32[]{:S(2)}) collective-permute-start(bf16[32,4096]{1,0:T(8,128)(2,1)S(1)} %collective-permute-done.3.refs_0_), channel_id=1, source_target_pairs={{0,2},{1,271},{2,4},{3,1},{4,6},{5,3},{6,8},{7,5},{8,10},{9,7},{10... | collective-permute-start | bytes 786440 | tf_op jit(solution)/shard_map/ppermute | solution.py:30
  59.0 2.1 %collective-permute-start.7 = (bf16[32,4096]{1,0:T(8,128)(2,1)S(1)}, bf16[32,4096]{1,0:T(8,128)(2,1)S(1)}, u32[]{:S(2)}, u32[]{:S(2)}) collective-permute-start(bf16[32,4096]{1,0:T(8,128)(2,1)S(1)} %collective-permute-done.6.refs_1_), channel_id=1, source_target_pairs={{0,270},{1,3},{2,0},{3,5},{4,2},{5,7},{6,4},{7,9},{8,6},{9,11},{10... | collective-permute-start | bytes 786440 | tf_op jit(solution)/shard_map/ppermute | solution.py:30
  61.8 7.5 %collective-permute-done.4.refs_1_ = bf16[32,4096]{1,0:T(8,128)(2,1)S(1)} collective-permute-done((bf16[32,4096]{1,0:T(8,128)(2,1)S(1)}, bf16[32,4096]{1,0:T(8,128)(2,1)S(1)}, u32[]{:S(2)}, u32[]{:S(2)}) %collective-permute-start.4) | collective-permute-done | bytes 262176 | tf_op jit(solution)/shard_map/ppermute | solution.py:30
  71.3 3.4 %collective-permute-done.10.refs_8_.refs_10_ = bf16[16,2,2,48,256]{4,3,2,1,0:T(8,128)(2,1)S(1)} collective-permute-done((bf16[16,2,2,48,256]{4,3,2,1,0:T(8,128)(2,1)S(1)}, bf16[16,2,2,48,256]{4,3,2,1,0:T(8,128)(2,1)S(1)}, u32[]{:S(2)}, u32[]{:S(2)}) %collective-permute-start.10) | collective-permute-done | bytes 1572896 | tf_op jit(solution)/shard_map/ppermute | solution.py:183
  74.6 6.4 %attend3.1 = (bf16[32,4096]{1,0:T(8,128)(2,1)S(1)}, bf16[32,4096]{1,0:T(8,128)(2,1)S(1)}, bf16[32,4096]{1,0:T(8,128)(2,1)S(1)}) custom-call(bf16[32,4096]{1,0:T(8,128)(2,1)S(1)} %collective-permute-done.5.refs_0_, bf16[32,4096]{1,0:T(8,128)(2,1)S(1)} %collective-permute-done.4.refs_1_, bf16[32,4096]{1,0:T(8,128)(2,1)S(1)} %collective-permute-done.7.refs_2_, ...), custom_call_target="tpu_custom_call" | custom-call | flops 1207959552 | bytes 12582912 | tf_op jit(solution)/shard_map/attend3/pallas_call | solution.py:131
  83.0 2.4 %collective-permute-start.12 = (bf16[32,4096]{1,0:T(8,128)(2,1)S(1)}, bf16[32,4096]{1,0:T(8,128)(2,1)S(1)}, u32[]{:S(2)}, u32[]{:S(2)}) collective-permute-start(bf16[32,4096]{1,0:T(8,128)(2,1)S(1)} %get-tuple-element.46), channel_id=1, source_target_pairs={{0,270},{1,3},{2,0},{3,5},{4,2},{5,7},{6,4},{7,9},{8,6},{9,11},{10... | collective-permute-start | bytes 786440 | tf_op jit(solution)/shard_map/ppermute | solution.py:30
  85.4 4.0 %collective-permute-start.13 = (bf16[32,4096]{1,0:T(8,128)(2,1)S(1)}, bf16[32,4096]{1,0:T(8,128)(2,1)S(1)}, u32[]{:S(2)}, u32[]{:S(2)}) collective-permute-start(bf16[32,4096]{1,0:T(8,128)(2,1)S(1)} %get-tuple-element.47), channel_id=1, source_target_pairs={{0,2},{1,271},{2,4},{3,1},{4,6},{5,3},{6,8},{7,5},{8,10},{9,7},{10... | collective-permute-start | bytes 786440 | tf_op jit(solution)/shard_map/ppermute | solution.py:30
  89.5 7.2 %attend5.1 = (bf16[32,4096]{1,0:T(8,128)(2,1)S(1)}, bf16[32,4096]{1,0:T(8,128)(2,1)S(1)}, bf16[32,4096]{1,0:T(8,128)(2,1)S(1)}, bf16[32,4096]{1,0:T(8,128)(2,1)S(1)}, bf16[32,4096]{1,0:T(8,128)(2,1)S(1)}) custom-call(bf16[32,4096]{1,0:T(8,128)(2,1)S(1)} %collective-permute-done.3.refs_0_, bf16[32,4096]{1,0:T(8,128)(2,1)S(1)} %collective-permute-done.6.refs_1_, ...), custom_call_target="tpu_custom_call" | custom-call | flops 2013265920 | bytes 12582912 | tf_op jit(solution)/shard_map/attend5/pallas_call | solution.py:131
  97.5 5.3 %collective-permute-start.15 = (bf16[32,4096]{1,0:T(8,128)(2,1)S(1)}, bf16[32,4096]{1,0:T(8,128)(2,1)S(1)}, u32[]{:S(2)}, u32[]{:S(2)}) collective-permute-start(bf16[32,4096]{1,0:T(8,128)(2,1)S(1)} %add_convert_fusion.3), channel_id=1, source_target_pairs={{0,2},{1,271},{2,4},{3,1},{4,6},{5,3},{6,8},{7,5},{8,10},{9,7},{10... | collective-permute-start | bytes 786440 | tf_op jit(solution)/shard_map/ppermute | solution.py:30
  106.1 5.1 %collective-permute-done.14 = bf16[32,4096]{1,0:T(8,128)(2,1)S(1)} collective-permute-done((bf16[32,4096]{1,0:T(8,128)(2,1)S(1)}, bf16[32,4096]{1,0:T(8,128)(2,1)S(1)}, u32[]{:S(2)}, u32[]{:S(2)}) %collective-permute-start.14) | collective-permute-done | bytes 262176 | tf_op jit(solution)/shard_map/ppermute | solution.py:30
  111.3 3.0 %collective-permute-start.17 = (bf16[32,4096]{1,0:T(8,128)(2,1)S(1)}, bf16[32,4096]{1,0:T(8,128)(2,1)S(1)}, u32[]{:S(2)}, u32[]{:S(2)}) collective-permute-start(bf16[32,4096]{1,0:T(8,128)(2,1)S(1)} %add_convert_fusion.1), channel_id=1, source_target_pairs={{0,2},{1,271},{2,4},{3,1},{4,6},{5,3},{6,8},{7,5},{8,10},{9,7},{10... | collective-permute-start | bytes 786440 | tf_op jit(solution)/shard_map/ppermute | solution.py:30
  114.4 2.3 %collective-permute-start.16 = (bf16[32,4096]{1,0:T(8,128)(2,1)S(1)}, bf16[32,4096]{1,0:T(8,128)(2,1)S(1)}, u32[]{:S(2)}, u32[]{:S(2)}) collective-permute-start(bf16[32,4096]{1,0:T(8,128)(2,1)S(1)} %add_convert_fusion.2), channel_id=1, source_target_pairs={{0,270},{1,3},{2,0},{3,5},{4,2},{5,7},{6,4},{7,9},{8,6},{9,11},{10... | collective-permute-start | bytes 786440 | tf_op jit(solution)/shard_map/ppermute | solution.py:30
  116.7 2.7 %collective-permute-done.17 = bf16[32,4096]{1,0:T(8,128)(2,1)S(1)} collective-permute-done((bf16[32,4096]{1,0:T(8,128)(2,1)S(1)}, bf16[32,4096]{1,0:T(8,128)(2,1)S(1)}, u32[]{:S(2)}, u32[]{:S(2)}) %collective-permute-start.17) | collective-permute-done | bytes 262176 | tf_op jit(solution)/shard_map/ppermute | solution.py:30
  119.4 3.4 %collective-permute-done.16 = bf16[32,4096]{1,0:T(8,128)(2,1)S(1)} collective-permute-done((bf16[32,4096]{1,0:T(8,128)(2,1)S(1)}, bf16[32,4096]{1,0:T(8,128)(2,1)S(1)}, u32[]{:S(2)}, u32[]{:S(2)}) %collective-permute-start.16) | collective-permute-done | bytes 262176 | tf_op jit(solution)/shard_map/ppermute | solution.py:30
  (27 shorter events, 13.4 us)
Async XLA Ops:
  1.9 27.7 %collective-permute-start.2 = (bf16[32,4096]{1,0:T(8,128)(2,1)}, bf16[32,4096]{1,0:T(8,128)(2,1)S(1)}, u32[]{:S(2)}, u32[]{:S(2)}) collective-permute-start(bf16[32,4096]{1,0:T(8,128)(2,1)} %get-tuple-element.35.refs_4_), channel_id=1, source_target_pairs={{0,270},{1,3},{2,0},{3,5},{4,2},{5,7},{6,4},{7,9},{8,6},{9,11},{10... | collective-permute-start | bytes 786440 | tf_op jit(solution)/shard_map/ppermute | solution.py:30
  6.2 23.4 %collective-permute-start.1 = (bf16[32,4096]{1,0:T(8,128)(2,1)}, bf16[32,4096]{1,0:T(8,128)(2,1)S(1)}, u32[]{:S(2)}, u32[]{:S(2)}) collective-permute-start(bf16[32,4096]{1,0:T(8,128)(2,1)} %get-tuple-element.35.refs_4_), channel_id=1, source_target_pairs={{0,2},{1,271},{2,4},{3,1},{4,6},{5,3},{6,8},{7,5},{8,10},{9,7},{10... | collective-permute-start | bytes 786440 | tf_op jit(solution)/shard_map/ppermute | solution.py:30
  15.7 13.8 %collective-permute-start = (bf16[112,256]{1,0:T(8,128)(2,1)}, bf16[112,256]{1,0:T(8,128)(2,1)S(1)}, u32[]{:S(2)}, u32[]{:S(2)}) collective-permute-start(bf16[112,256]{1,0:T(8,128)(2,1)} %get-tuple-element.34.mine), channel_id=1, source_target_pairs={{0,256},{256,0},{1,257},{257,1},{2,258},{258,2},{3,259},{259,3},{4... | collective-permute-start | bytes 172040 | tf_op jit(solution)/shard_map/ppermute | solution.py:163
  29.6 0.8 copy-start.1
  31.7 37.6 %all-to-all-start = ((bf16[16,2,2,48,256]{4,3,2,1,0:T(8,128)(2,1)}), bf16[16,2,2,48,256]{4,3,2,1,0:T(8,128)(2,1)S(1)}, u32[]{:S(2)}, u32[]{:S(2)}) async-start(bf16[16,2,2,48,256]{4,3,2,1,0:T(8,128)(2,1)} %get-tuple-element.37), calls=%async_computation | async-start | bytes 3145728 | tf_op jit(solution)/shard_map/all_to_all | solution.py:178
  38.5 13.9 %collective-permute-start.3 = (bf16[32,4096]{1,0:T(8,128)(2,1)S(1)}, bf16[32,4096]{1,0:T(8,128)(2,1)S(1)}, u32[]{:S(2)}, u32[]{:S(2)}) collective-permute-start(bf16[32,4096]{1,0:T(8,128)(2,1)S(1)} %collective-permute-done.1.refs_2_), channel_id=1, source_target_pairs={{0,2},{1,271},{2,4},{3,1},{4,6},{5,3},{6,8},{7,5},{8,10},{9,7},{10... | collective-permute-start | bytes 786440 | tf_op jit(solution)/shard_map/ppermute | solution.py:30
  44.2 14.8 %collective-permute-start.6 = (bf16[32,4096]{1,0:T(8,128)(2,1)S(1)}, bf16[32,4096]{1,0:T(8,128)(2,1)S(1)}, u32[]{:S(2)}, u32[]{:S(2)}) collective-permute-start(bf16[32,4096]{1,0:T(8,128)(2,1)S(1)} %collective-permute-done.2.refs_3_), channel_id=1, source_target_pairs={{0,270},{1,3},{2,0},{3,5},{4,2},{5,7},{6,4},{7,9},{8,6},{9,11},{10... | collective-permute-start | bytes 786440 | tf_op jit(solution)/shard_map/ppermute | solution.py:30
  46.1 25.1 %collective-permute-start.8 = (bf16[4096,256]{1,0:T(8,128)(2,1)}, bf16[4096,256]{1,0:T(8,128)(2,1)}, u32[]{:S(2)}, u32[]{:S(2)}) collective-permute-start(bf16[4096,256]{1,0:T(8,128)(2,1)} %refs_5_.3), channel_id=1, source_target_pairs={{0,1},{1,0},{2,3},{3,2},{4,5},{5,4},{6,7},{7,6},{8,9},{9,8},{10,11... | collective-permute-start | bytes 6291464 | tf_op jit(solution)/shard_map/ppermute | solution.py:165
  50.5 20.8 %collective-permute-start.9 = (bf16[256,4096]{1,0:T(8,128)(2,1)}, bf16[256,4096]{1,0:T(8,128)(2,1)}, u32[]{:S(2)}, u32[]{:S(2)}) collective-permute-start(bf16[256,4096]{1,0:T(8,128)(2,1)} %refs_7_.1), channel_id=1, source_target_pairs={{0,1},{1,0},{2,3},{3,2},{4,5},{5,4},{6,7},{7,6},{8,9},{9,8},{10,11... | collective-permute-start | bytes 6291464 | tf_op jit(solution)/shard_map/ppermute | solution.py:166
  52.4 9.4 %collective-permute-start.5 = (bf16[32,4096]{1,0:T(8,128)(2,1)S(1)}, bf16[32,4096]{1,0:T(8,128)(2,1)S(1)}, u32[]{:S(2)}, u32[]{:S(2)}) collective-permute-start(bf16[32,4096]{1,0:T(8,128)(2,1)S(1)} %collective-permute-done.3.refs_0_), channel_id=1, source_target_pairs={{0,4},{1,269},{2,6},{3,271},{4,8},{5,1},{6,10},{7,3},{8,12},{9,5},... | collective-permute-start | bytes 786440 | tf_op jit(solution)/shard_map/ppermute | solution.py:30
  55.9 13.4 %collective-permute-start.4 = (bf16[32,4096]{1,0:T(8,128)(2,1)S(1)}, bf16[32,4096]{1,0:T(8,128)(2,1)S(1)}, u32[]{:S(2)}, u32[]{:S(2)}) collective-permute-start(bf16[32,4096]{1,0:T(8,128)(2,1)S(1)} %collective-permute-done.3.refs_0_), channel_id=1, source_target_pairs={{0,2},{1,271},{2,4},{3,1},{4,6},{5,3},{6,8},{7,5},{8,10},{9,7},{10... | collective-permute-start | bytes 786440 | tf_op jit(solution)/shard_map/ppermute | solution.py:30
  59.0 10.3 %collective-permute-start.7 = (bf16[32,4096]{1,0:T(8,128)(2,1)S(1)}, bf16[32,4096]{1,0:T(8,128)(2,1)S(1)}, u32[]{:S(2)}, u32[]{:S(2)}) collective-permute-start(bf16[32,4096]{1,0:T(8,128)(2,1)S(1)} %collective-permute-done.6.refs_1_), channel_id=1, source_target_pairs={{0,270},{1,3},{2,0},{3,5},{4,2},{5,7},{6,4},{7,9},{8,6},{9,11},{10... | collective-permute-start | bytes 786440 | tf_op jit(solution)/shard_map/ppermute | solution.py:30
  69.3 5.3 %collective-permute-start.10 = (bf16[16,2,2,48,256]{4,3,2,1,0:T(8,128)(2,1)S(1)}, bf16[16,2,2,48,256]{4,3,2,1,0:T(8,128)(2,1)S(1)}, u32[]{:S(2)}, u32[]{:S(2)}) collective-permute-start(bf16[16,2,2,48,256]{4,3,2,1,0:T(8,128)(2,1)S(1)} %all-to-all-done.refs_7_.refs_9_), channel_id=1, source_target_pairs={{0,1},{1,0},{2,3},{3,2},{4,5},{5,4},{6,7},{7,6},{8,9},{9,8},{10,11... | collective-permute-start | bytes 4718600 | tf_op jit(solution)/shard_map/ppermute | solution.py:183
  74.6 14.9 %copy-start = (bf16[32,4096]{1,0:T(8,128)(2,1)S(1)}, bf16[32,4096]{1,0:T(8,128)(2,1)}, u32[]{:S(2)}) copy-start(bf16[32,4096]{1,0:T(8,128)(2,1)} %get-tuple-element.35.refs_4_) | copy-start | bytes 786436
  81.0 15.7 %collective-permute-start.11 = (bf16[32,4096]{1,0:T(8,128)(2,1)S(1)}, bf16[32,4096]{1,0:T(8,128)(2,1)S(1)}, u32[]{:S(2)}, u32[]{:S(2)}) collective-permute-start(bf16[32,4096]{1,0:T(8,128)(2,1)S(1)} %get-tuple-element.45), channel_id=1, source_target_pairs={{0,268},{1,5},{2,270},{3,7},{4,0},{5,9},{6,2},{7,11},{8,4},{9,13},... | collective-permute-start | bytes 786440 | tf_op jit(solution)/shard_map/ppermute | solution.py:30
  83.0 13.8 %collective-permute-start.12 = (bf16[32,4096]{1,0:T(8,128)(2,1)S(1)}, bf16[32,4096]{1,0:T(8,128)(2,1)S(1)}, u32[]{:S(2)}, u32[]{:S(2)}) collective-permute-start(bf16[32,4096]{1,0:T(8,128)(2,1)S(1)} %get-tuple-element.46), channel_id=1, source_target_pairs={{0,270},{1,3},{2,0},{3,5},{4,2},{5,7},{6,4},{7,9},{8,6},{9,11},{10... | collective-permute-start | bytes 786440 | tf_op jit(solution)/shard_map/ppermute | solution.py:30
  85.4 12.0 %collective-permute-start.13 = (bf16[32,4096]{1,0:T(8,128)(2,1)S(1)}, bf16[32,4096]{1,0:T(8,128)(2,1)S(1)}, u32[]{:S(2)}, u32[]{:S(2)}) collective-permute-start(bf16[32,4096]{1,0:T(8,128)(2,1)S(1)} %get-tuple-element.47), channel_id=1, source_target_pairs={{0,2},{1,271},{2,4},{3,1},{4,6},{5,3},{6,8},{7,5},{8,10},{9,7},{10... | collective-permute-start | bytes 786440 | tf_op jit(solution)/shard_map/ppermute | solution.py:30
  97.5 8.6 %collective-permute-start.15 = (bf16[32,4096]{1,0:T(8,128)(2,1)S(1)}, bf16[32,4096]{1,0:T(8,128)(2,1)S(1)}, u32[]{:S(2)}, u32[]{:S(2)}) collective-permute-start(bf16[32,4096]{1,0:T(8,128)(2,1)S(1)} %add_convert_fusion.3), channel_id=1, source_target_pairs={{0,2},{1,271},{2,4},{3,1},{4,6},{5,3},{6,8},{7,5},{8,10},{9,7},{10... | collective-permute-start | bytes 786440 | tf_op jit(solution)/shard_map/ppermute | solution.py:30
  102.9 8.3 %collective-permute-start.14 = (bf16[32,4096]{1,0:T(8,128)(2,1)S(1)}, bf16[32,4096]{1,0:T(8,128)(2,1)S(1)}, u32[]{:S(2)}, u32[]{:S(2)}) collective-permute-start(bf16[32,4096]{1,0:T(8,128)(2,1)S(1)} %add_convert_fusion.4), channel_id=1, source_target_pairs={{0,270},{1,3},{2,0},{3,5},{4,2},{5,7},{6,4},{7,9},{8,6},{9,11},{10... | collective-permute-start | bytes 786440 | tf_op jit(solution)/shard_map/ppermute | solution.py:30
  111.3 8.0 %collective-permute-start.17 = (bf16[32,4096]{1,0:T(8,128)(2,1)S(1)}, bf16[32,4096]{1,0:T(8,128)(2,1)S(1)}, u32[]{:S(2)}, u32[]{:S(2)}) collective-permute-start(bf16[32,4096]{1,0:T(8,128)(2,1)S(1)} %add_convert_fusion.1), channel_id=1, source_target_pairs={{0,2},{1,271},{2,4},{3,1},{4,6},{5,3},{6,8},{7,5},{8,10},{9,7},{10... | collective-permute-start | bytes 786440 | tf_op jit(solution)/shard_map/ppermute | solution.py:30
  114.4 8.3 %collective-permute-start.16 = (bf16[32,4096]{1,0:T(8,128)(2,1)S(1)}, bf16[32,4096]{1,0:T(8,128)(2,1)S(1)}, u32[]{:S(2)}, u32[]{:S(2)}) collective-permute-start(bf16[32,4096]{1,0:T(8,128)(2,1)S(1)} %add_convert_fusion.2), channel_id=1, source_target_pairs={{0,270},{1,3},{2,0},{3,5},{4,2},{5,7},{6,4},{7,9},{8,6},{9,11},{10... | collective-permute-start | bytes 786440 | tf_op jit(solution)/shard_map/ppermute | solution.py:30

commit v8 on v7

--- a/solution.py
+++ b/solution.py
@@ -191,7 +191,6 @@
     mid, ap, bp = along(far[0], -2), along(far[1], -1), along(far[2], 1)
     mid, ap, bp, near = lax.optimization_barrier((mid, ap, bp, near))
     ap, bp = along(thin(wide(near[0]) + wide(ap) + wide(mid)), -1), along(plus(near[1], bp), 1)
-    ap, bp = lax.optimization_barrier((ap, bp))
     ap, bp = along(plus(near[2], ap), -1), along(plus(near[3], bp), 1)
     out = wide(near[4]) + wide(ap) + wide(bp)
     return thin(out).reshape(rows, 1, 4096)

time: 124 us -> 122 us (0.984)
  waiting for transfers between devices: 28.9 us -> 25.2 us
  starting transfers between devices: 75 us -> 76.7 us
    ppermute x14, waiting for transfers between devices: 21.2 us -> 17.5 us  [along(): return lax.ppermute(x, RING + ('c',), opposite(step))]
    ppermute x14, starting transfers between devices: 51.2 us -> 52.8 us  [along(): return lax.ppermute(x, RING + ('c',), opposite(step))]
  transfers between devices with their start and end apart: 19 -> 19, of which waited for: 9 -> 8; matrix products, arithmetic and copies ran while one was open for 0% -> 0% of each run, Pallas kernels for 6% -> 6%
where the time goes in v8:
time: 122 us; the launch traced here: 121 us
  starting transfers between devices  76.7 us (63%)
  waiting for transfers between devices  25.2 us (21%)
  Pallas kernels  16.8 us (14%)
    ppermute x14, starting transfers between devices, along(): return lax.ppermute(x, RING + ('c',), opposite(step))  52.8 us
    ppermute x14, waiting for transfers between devices, along(): return lax.ppermute(x, RING + ('c',), opposite(step))  17.5 us
    pallas_call x2, Pallas kernels, attend(): pl.pallas_call(functools.partial(attend_kernel, count, first), out_shape=...  13.7 us
    ppermute x1, starting transfers between devices, per_device(): theirs = lax.ppermute(mine, 'zh', SWAP)  8.89 us
    all_to_all x1, starting transfers between devices, per_device(): kv = lax.all_to_all(kv, ('y', 'x'), 0, 0, tiled=True)  6.75 us
    ppermute x1, starting transfers between devices, per_device(): wq_other = lax.ppermute(wq, 'c', SWAP)  4.34 us
    ppermute x1, waiting for transfers between devices, per_device(): theirs = lax.ppermute(mine, 'zh', SWAP)  4.3 us
    ppermute x1, waiting for transfers between devices, per_device(): kv_other = lax.ppermute(kv, 'c', SWAP)  3.35 us
  transfers between devices with their start and end apart: 19, of which 8 were waited for; matrix products, arithmetic and copies ran while one was open for 0% of the time, Pallas kernels for 6%

profile of v8, /device:TPU:1, one launch (start us, length us, event | category | flops | bytes accessed | tf_op | source)
XLA Modules:
  0.0 121.5 jit_solution(18313461021442991433)
XLA Ops:
  1.9 4.4 %collective-permute-start.2 = (bf16[32,4096]{1,0:T(8,128)(2,1)}, bf16[32,4096]{1,0:T(8,128)(2,1)S(1)}, u32[]{:S(2)}, u32[]{:S(2)}) collective-permute-start(bf16[32,4096]{1,0:T(8,128)(2,1)} %get-tuple-element.33.refs_4_), channel_id=1, source_target_pairs={{0,270},{1,3},{2,0},{3,5},{4,2},{5,7},{6,4},{7,9},{8,6},{9,11},{10... | collective-permute-start | bytes 786440 | tf_op jit(solution)/shard_map/ppermute | solution.py:30
  6.2 9.5 %collective-permute-start.1 = (bf16[32,4096]{1,0:T(8,128)(2,1)}, bf16[32,4096]{1,0:T(8,128)(2,1)S(1)}, u32[]{:S(2)}, u32[]{:S(2)}) collective-permute-start(bf16[32,4096]{1,0:T(8,128)(2,1)} %get-tuple-element.33.refs_4_), channel_id=1, source_target_pairs={{0,2},{1,271},{2,4},{3,1},{4,6},{5,3},{6,8},{7,5},{8,10},{9,7},{10... | collective-permute-start | bytes 786440 | tf_op jit(solution)/shard_map/ppermute | solution.py:30
  15.7 8.9 %collective-permute-start = (bf16[112,256]{1,0:T(8,128)(2,1)}, bf16[112,256]{1,0:T(8,128)(2,1)S(1)}, u32[]{:S(2)}, u32[]{:S(2)}) collective-permute-start(bf16[112,256]{1,0:T(8,128)(2,1)} %get-tuple-element.32.mine), channel_id=1, source_target_pairs={{0,256},{256,0},{1,257},{257,1},{2,258},{258,2},{3,259},{259,3},{4... | collective-permute-start | bytes 172040 | tf_op jit(solution)/shard_map/ppermute | solution.py:163
  25.3 4.3 %collective-permute-done.theirs = bf16[112,256]{1,0:T(8,128)(2,1)S(1)} collective-permute-done((bf16[112,256]{1,0:T(8,128)(2,1)}, bf16[112,256]{1,0:T(8,128)(2,1)S(1)}, u32[]{:S(2)}, u32[]{:S(2)}) %collective-permute-start) | collective-permute-done | bytes 57376 | tf_op jit(solution)/shard_map/ppermute | solution.py:163
  31.7 6.8 %all-to-all-start = ((bf16[16,2,2,48,256]{4,3,2,1,0:T(8,128)(2,1)}), bf16[16,2,2,48,256]{4,3,2,1,0:T(8,128)(2,1)S(1)}, u32[]{:S(2)}, u32[]{:S(2)}) async-start(bf16[16,2,2,48,256]{4,3,2,1,0:T(8,128)(2,1)} %get-tuple-element.35), calls=%async_computation | async-start | bytes 3145728 | tf_op jit(solution)/shard_map/all_to_all | solution.py:178
  38.5 5.7 %collective-permute-start.3 = (bf16[32,4096]{1,0:T(8,128)(2,1)S(1)}, bf16[32,4096]{1,0:T(8,128)(2,1)S(1)}, u32[]{:S(2)}, u32[]{:S(2)}) collective-permute-start(bf16[32,4096]{1,0:T(8,128)(2,1)S(1)} %collective-permute-done.1.refs_2_), channel_id=1, source_target_pairs={{0,2},{1,271},{2,4},{3,1},{4,6},{5,3},{6,8},{7,5},{8,10},{9,7},{10... | collective-permute-start | bytes 786440 | tf_op jit(solution)/shard_map/ppermute | solution.py:30
  44.2 1.9 %collective-permute-start.6 = (bf16[32,4096]{1,0:T(8,128)(2,1)S(1)}, bf16[32,4096]{1,0:T(8,128)(2,1)S(1)}, u32[]{:S(2)}, u32[]{:S(2)}) collective-permute-start(bf16[32,4096]{1,0:T(8,128)(2,1)S(1)} %collective-permute-done.2.refs_3_), channel_id=1, source_target_pairs={{0,270},{1,3},{2,0},{3,5},{4,2},{5,7},{6,4},{7,9},{8,6},{9,11},{10... | collective-permute-start | bytes 786440 | tf_op jit(solution)/shard_map/ppermute | solution.py:30
  46.1 4.3 %collective-permute-start.8 = (bf16[4096,256]{1,0:T(8,128)(2,1)}, bf16[4096,256]{1,0:T(8,128)(2,1)}, u32[]{:S(2)}, u32[]{:S(2)}) collective-permute-start(bf16[4096,256]{1,0:T(8,128)(2,1)} %refs_5_.3), channel_id=1, source_target_pairs={{0,1},{1,0},{2,3},{3,2},{4,5},{5,4},{6,7},{7,6},{8,9},{9,8},{10,11... | collective-permute-start | bytes 6291464 | tf_op jit(solution)/shard_map/ppermute | solution.py:165
  50.5 1.9 %collective-permute-start.9 = (bf16[256,4096]{1,0:T(8,128)(2,1)}, bf16[256,4096]{1,0:T(8,128)(2,1)}, u32[]{:S(2)}, u32[]{:S(2)}) collective-permute-start(bf16[256,4096]{1,0:T(8,128)(2,1)} %refs_7_.1), channel_id=1, source_target_pairs={{0,1},{1,0},{2,3},{3,2},{4,5},{5,4},{6,7},{7,6},{8,9},{9,8},{10,11... | collective-permute-start | bytes 6291464 | tf_op jit(solution)/shard_map/ppermute | solution.py:166
  52.4 3.5 %collective-permute-start.5 = (bf16[32,4096]{1,0:T(8,128)(2,1)S(1)}, bf16[32,4096]{1,0:T(8,128)(2,1)S(1)}, u32[]{:S(2)}, u32[]{:S(2)}) collective-permute-start(bf16[32,4096]{1,0:T(8,128)(2,1)S(1)} %collective-permute-done.3.refs_0_), channel_id=1, source_target_pairs={{0,4},{1,269},{2,6},{3,271},{4,8},{5,1},{6,10},{7,3},{8,12},{9,5},... | collective-permute-start | bytes 786440 | tf_op jit(solution)/shard_map/ppermute | solution.py:30
  55.9 3.1 %collective-permute-start.4 = (bf16[32,4096]{1,0:T(8,128)(2,1)S(1)}, bf16[32,4096]{1,0:T(8,128)(2,1)S(1)}, u32[]{:S(2)}, u32[]{:S(2)}) collective-permute-start(bf16[32,4096]{1,0:T(8,128)(2,1)S(1)} %collective-permute-done.3.refs_0_), channel_id=1, source_target_pairs={{0,2},{1,271},{2,4},{3,1},{4,6},{5,3},{6,8},{7,5},{8,10},{9,7},{10... | collective-permute-start | bytes 786440 | tf_op jit(solution)/shard_map/ppermute | solution.py:30
  59.0 2.1 %collective-permute-start.7 = (bf16[32,4096]{1,0:T(8,128)(2,1)S(1)}, bf16[32,4096]{1,0:T(8,128)(2,1)S(1)}, u32[]{:S(2)}, u32[]{:S(2)}) collective-permute-start(bf16[32,4096]{1,0:T(8,128)(2,1)S(1)} %collective-permute-done.6.refs_1_), channel_id=1, source_target_pairs={{0,270},{1,3},{2,0},{3,5},{4,2},{5,7},{6,4},{7,9},{8,6},{9,11},{10... | collective-permute-start | bytes 786440 | tf_op jit(solution)/shard_map/ppermute | solution.py:30
  61.8 7.5 %collective-permute-done.4.refs_1_ = bf16[32,4096]{1,0:T(8,128)(2,1)S(1)} collective-permute-done((bf16[32,4096]{1,0:T(8,128)(2,1)S(1)}, bf16[32,4096]{1,0:T(8,128)(2,1)S(1)}, u32[]{:S(2)}, u32[]{:S(2)}) %collective-permute-start.4) | collective-permute-done | bytes 262176 | tf_op jit(solution)/shard_map/ppermute | solution.py:30
  71.3 3.4 %collective-permute-done.10.refs_8_.refs_10_ = bf16[16,2,2,48,256]{4,3,2,1,0:T(8,128)(2,1)S(1)} collective-permute-done((bf16[16,2,2,48,256]{4,3,2,1,0:T(8,128)(2,1)S(1)}, bf16[16,2,2,48,256]{4,3,2,1,0:T(8,128)(2,1)S(1)}, u32[]{:S(2)}, u32[]{:S(2)}) %collective-permute-start.10) | collective-permute-done | bytes 1572896 | tf_op jit(solution)/shard_map/ppermute | solution.py:183
  74.6 6.4 %attend3.1 = (bf16[32,4096]{1,0:T(8,128)(2,1)S(1)}, bf16[32,4096]{1,0:T(8,128)(2,1)S(1)}, bf16[32,4096]{1,0:T(8,128)(2,1)S(1)}) custom-call(bf16[32,4096]{1,0:T(8,128)(2,1)S(1)} %collective-permute-done.5.refs_0_, bf16[32,4096]{1,0:T(8,128)(2,1)S(1)} %collective-permute-done.4.refs_1_, bf16[32,4096]{1,0:T(8,128)(2,1)S(1)} %collective-permute-done.7.refs_2_, ...), custom_call_target="tpu_custom_call" | custom-call | flops 1207959552 | bytes 12582912 | tf_op jit(solution)/shard_map/attend3/pallas_call | solution.py:131
  81.0 1.9 %collective-permute-start.11 = (bf16[32,4096]{1,0:T(8,128)(2,1)S(1)}, bf16[32,4096]{1,0:T(8,128)(2,1)S(1)}, u32[]{:S(2)}, u32[]{:S(2)}) collective-permute-start(bf16[32,4096]{1,0:T(8,128)(2,1)S(1)} %get-tuple-element.43), channel_id=1, source_target_pairs={{0,268},{1,5},{2,270},{3,7},{4,0},{5,9},{6,2},{7,11},{8,4},{9,13},... | collective-permute-start | bytes 786440 | tf_op jit(solution)/shard_map/ppermute | solution.py:30
  83.0 2.4 %collective-permute-start.12 = (bf16[32,4096]{1,0:T(8,128)(2,1)S(1)}, bf16[32,4096]{1,0:T(8,128)(2,1)S(1)}, u32[]{:S(2)}, u32[]{:S(2)}) collective-permute-start(bf16[32,4096]{1,0:T(8,128)(2,1)S(1)} %get-tuple-element.44), channel_id=1, source_target_pairs={{0,270},{1,3},{2,0},{3,5},{4,2},{5,7},{6,4},{7,9},{8,6},{9,11},{10... | collective-permute-start | bytes 786440 | tf_op jit(solution)/shard_map/ppermute | solution.py:30
  85.4 4.0 %collective-permute-start.13 = (bf16[32,4096]{1,0:T(8,128)(2,1)S(1)}, bf16[32,4096]{1,0:T(8,128)(2,1)S(1)}, u32[]{:S(2)}, u32[]{:S(2)}) collective-permute-start(bf16[32,4096]{1,0:T(8,128)(2,1)S(1)} %get-tuple-element.45), channel_id=1, source_target_pairs={{0,2},{1,271},{2,4},{3,1},{4,6},{5,3},{6,8},{7,5},{8,10},{9,7},{10... | collective-permute-start | bytes 786440 | tf_op jit(solution)/shard_map/ppermute | solution.py:30
  89.5 7.2 %attend5.1 = (bf16[32,4096]{1,0:T(8,128)(2,1)S(1)}, bf16[32,4096]{1,0:T(8,128)(2,1)S(1)}, bf16[32,4096]{1,0:T(8,128)(2,1)S(1)}, bf16[32,4096]{1,0:T(8,128)(2,1)S(1)}, bf16[32,4096]{1,0:T(8,128)(2,1)S(1)}) custom-call(bf16[32,4096]{1,0:T(8,128)(2,1)S(1)} %collective-permute-done.3.refs_0_, bf16[32,4096]{1,0:T(8,128)(2,1)S(1)} %collective-permute-done.6.refs_1_, ...), custom_call_target="tpu_custom_call" | custom-call | flops 2013265920 | bytes 12582912 | tf_op jit(solution)/shard_map/attend5/pallas_call | solution.py:131
  97.5 5.3 %collective-permute-start.16 = (bf16[32,4096]{1,0:T(8,128)(2,1)S(1)}, bf16[32,4096]{1,0:T(8,128)(2,1)S(1)}, u32[]{:S(2)}, u32[]{:S(2)}) collective-permute-start(bf16[32,4096]{1,0:T(8,128)(2,1)S(1)} %add_convert_fusion.2), channel_id=1, source_target_pairs={{0,2},{1,271},{2,4},{3,1},{4,6},{5,3},{6,8},{7,5},{8,10},{9,7},{10... | collective-permute-start | bytes 786440 | tf_op jit(solution)/shard_map/ppermute | solution.py:30
  102.9 1.9 %collective-permute-start.14 = (bf16[32,4096]{1,0:T(8,128)(2,1)S(1)}, bf16[32,4096]{1,0:T(8,128)(2,1)S(1)}, u32[]{:S(2)}, u32[]{:S(2)}) collective-permute-start(bf16[32,4096]{1,0:T(8,128)(2,1)S(1)} %add_convert_fusion.4), channel_id=1, source_target_pairs={{0,270},{1,3},{2,0},{3,5},{4,2},{5,7},{6,4},{7,9},{8,6},{9,11},{10... | collective-permute-start | bytes 786440 | tf_op jit(solution)/shard_map/ppermute | solution.py:30
  106.2 5.0 %collective-permute-start.17 = (bf16[32,4096]{1,0:T(8,128)(2,1)S(1)}, bf16[32,4096]{1,0:T(8,128)(2,1)S(1)}, u32[]{:S(2)}, u32[]{:S(2)}) collective-permute-start(bf16[32,4096]{1,0:T(8,128)(2,1)S(1)} %add_convert_fusion.1), channel_id=1, source_target_pairs={{0,2},{1,271},{2,4},{3,1},{4,6},{5,3},{6,8},{7,5},{8,10},{9,7},{10... | collective-permute-start | bytes 786440 | tf_op jit(solution)/shard_map/ppermute | solution.py:30
  111.3 1.9 %collective-permute-start.15 = (bf16[32,4096]{1,0:T(8,128)(2,1)S(1)}, bf16[32,4096]{1,0:T(8,128)(2,1)S(1)}, u32[]{:S(2)}, u32[]{:S(2)}) collective-permute-start(bf16[32,4096]{1,0:T(8,128)(2,1)S(1)} %add_convert_fusion.3), channel_id=1, source_target_pairs={{0,270},{1,3},{2,0},{3,5},{4,2},{5,7},{6,4},{7,9},{8,6},{9,11},{10... | collective-permute-start | bytes 786440 | tf_op jit(solution)/shard_map/ppermute | solution.py:30
  114.5 6.1 %collective-permute-done.15 = bf16[32,4096]{1,0:T(8,128)(2,1)S(1)} collective-permute-done((bf16[32,4096]{1,0:T(8,128)(2,1)S(1)}, bf16[32,4096]{1,0:T(8,128)(2,1)S(1)}, u32[]{:S(2)}, u32[]{:S(2)}) %collective-permute-start.15) | collective-permute-done | bytes 262176 | tf_op jit(solution)/shard_map/ppermute | solution.py:30
  (27 shorter events, 10.9 us)
Async XLA Ops:
  1.9 27.7 %collective-permute-start.2 = (bf16[32,4096]{1,0:T(8,128)(2,1)}, bf16[32,4096]{1,0:T(8,128)(2,1)S(1)}, u32[]{:S(2)}, u32[]{:S(2)}) collective-permute-start(bf16[32,4096]{1,0:T(8,128)(2,1)} %get-tuple-element.33.refs_4_), channel_id=1, source_target_pairs={{0,270},{1,3},{2,0},{3,5},{4,2},{5,7},{6,4},{7,9},{8,6},{9,11},{10... | collective-permute-start | bytes 786440 | tf_op jit(solution)/shard_map/ppermute | solution.py:30
  6.2 23.4 %collective-permute-start.1 = (bf16[32,4096]{1,0:T(8,128)(2,1)}, bf16[32,4096]{1,0:T(8,128)(2,1)S(1)}, u32[]{:S(2)}, u32[]{:S(2)}) collective-permute-start(bf16[32,4096]{1,0:T(8,128)(2,1)} %get-tuple-element.33.refs_4_), channel_id=1, source_target_pairs={{0,2},{1,271},{2,4},{3,1},{4,6},{5,3},{6,8},{7,5},{8,10},{9,7},{10... | collective-permute-start | bytes 786440 | tf_op jit(solution)/shard_map/ppermute | solution.py:30
  15.7 13.8 %collective-permute-start = (bf16[112,256]{1,0:T(8,128)(2,1)}, bf16[112,256]{1,0:T(8,128)(2,1)S(1)}, u32[]{:S(2)}, u32[]{:S(2)}) collective-permute-start(bf16[112,256]{1,0:T(8,128)(2,1)} %get-tuple-element.32.mine), channel_id=1, source_target_pairs={{0,256},{256,0},{1,257},{257,1},{2,258},{258,2},{3,259},{259,3},{4... | collective-permute-start | bytes 172040 | tf_op jit(solution)/shard_map/ppermute | solution.py:163
  29.6 0.8 copy-start.1
  31.7 37.6 %all-to-all-start = ((bf16[16,2,2,48,256]{4,3,2,1,0:T(8,128)(2,1)}), bf16[16,2,2,48,256]{4,3,2,1,0:T(8,128)(2,1)S(1)}, u32[]{:S(2)}, u32[]{:S(2)}) async-start(bf16[16,2,2,48,256]{4,3,2,1,0:T(8,128)(2,1)} %get-tuple-element.35), calls=%async_computation | async-start | bytes 3145728 | tf_op jit(solution)/shard_map/all_to_all | solution.py:178
  38.5 13.9 %collective-permute-start.3 = (bf16[32,4096]{1,0:T(8,128)(2,1)S(1)}, bf16[32,4096]{1,0:T(8,128)(2,1)S(1)}, u32[]{:S(2)}, u32[]{:S(2)}) collective-permute-start(bf16[32,4096]{1,0:T(8,128)(2,1)S(1)} %collective-permute-done.1.refs_2_), channel_id=1, source_target_pairs={{0,2},{1,271},{2,4},{3,1},{4,6},{5,3},{6,8},{7,5},{8,10},{9,7},{10... | collective-permute-start | bytes 786440 | tf_op jit(solution)/shard_map/ppermute | solution.py:30
  44.2 14.8 %collective-permute-start.6 = (bf16[32,4096]{1,0:T(8,128)(2,1)S(1)}, bf16[32,4096]{1,0:T(8,128)(2,1)S(1)}, u32[]{:S(2)}, u32[]{:S(2)}) collective-permute-start(bf16[32,4096]{1,0:T(8,128)(2,1)S(1)} %collective-permute-done.2.refs_3_), channel_id=1, source_target_pairs={{0,270},{1,3},{2,0},{3,5},{4,2},{5,7},{6,4},{7,9},{8,6},{9,11},{10... | collective-permute-start | bytes 786440 | tf_op jit(solution)/shard_map/ppermute | solution.py:30
  46.1 25.1 %collective-permute-start.8 = (bf16[4096,256]{1,0:T(8,128)(2,1)}, bf16[4096,256]{1,0:T(8,128)(2,1)}, u32[]{:S(2)}, u32[]{:S(2)}) collective-permute-start(bf16[4096,256]{1,0:T(8,128)(2,1)} %refs_5_.3), channel_id=1, source_target_pairs={{0,1},{1,0},{2,3},{3,2},{4,5},{5,4},{6,7},{7,6},{8,9},{9,8},{10,11... | collective-permute-start | bytes 6291464 | tf_op jit(solution)/shard_map/ppermute | solution.py:165
  50.5 20.8 %collective-permute-start.9 = (bf16[256,4096]{1,0:T(8,128)(2,1)}, bf16[256,4096]{1,0:T(8,128)(2,1)}, u32[]{:S(2)}, u32[]{:S(2)}) collective-permute-start(bf16[256,4096]{1,0:T(8,128)(2,1)} %refs_7_.1), channel_id=1, source_target_pairs={{0,1},{1,0},{2,3},{3,2},{4,5},{5,4},{6,7},{7,6},{8,9},{9,8},{10,11... | collective-permute-start | bytes 6291464 | tf_op jit(solution)/shard_map/ppermute | solution.py:166
  52.4 9.4 %collective-permute-start.5 = (bf16[32,4096]{1,0:T(8,128)(2,1)S(1)}, bf16[32,4096]{1,0:T(8,128)(2,1)S(1)}, u32[]{:S(2)}, u32[]{:S(2)}) collective-permute-start(bf16[32,4096]{1,0:T(8,128)(2,1)S(1)} %collective-permute-done.3.refs_0_), channel_id=1, source_target_pairs={{0,4},{1,269},{2,6},{3,271},{4,8},{5,1},{6,10},{7,3},{8,12},{9,5},... | collective-permute-start | bytes 786440 | tf_op jit(solution)/shard_map/ppermute | solution.py:30
  55.9 13.4 %collective-permute-start.4 = (bf16[32,4096]{1,0:T(8,128)(2,1)S(1)}, bf16[32,4096]{1,0:T(8,128)(2,1)S(1)}, u32[]{:S(2)}, u32[]{:S(2)}) collective-permute-start(bf16[32,4096]{1,0:T(8,128)(2,1)S(1)} %collective-permute-done.3.refs_0_), channel_id=1, source_target_pairs={{0,2},{1,271},{2,4},{3,1},{4,6},{5,3},{6,8},{7,5},{8,10},{9,7},{10... | collective-permute-start | bytes 786440 | tf_op jit(solution)/shard_map/ppermute | solution.py:30
  59.0 10.3 %collective-permute-start.7 = (bf16[32,4096]{1,0:T(8,128)(2,1)S(1)}, bf16[32,4096]{1,0:T(8,128)(2,1)S(1)}, u32[]{:S(2)}, u32[]{:S(2)}) collective-permute-start(bf16[32,4096]{1,0:T(8,128)(2,1)S(1)} %collective-permute-done.6.refs_1_), channel_id=1, source_target_pairs={{0,270},{1,3},{2,0},{3,5},{4,2},{5,7},{6,4},{7,9},{8,6},{9,11},{10... | collective-permute-start | bytes 786440 | tf_op jit(solution)/shard_map/ppermute | solution.py:30
  69.3 5.3 %collective-permute-start.10 = (bf16[16,2,2,48,256]{4,3,2,1,0:T(8,128)(2,1)S(1)}, bf16[16,2,2,48,256]{4,3,2,1,0:T(8,128)(2,1)S(1)}, u32[]{:S(2)}, u32[]{:S(2)}) collective-permute-start(bf16[16,2,2,48,256]{4,3,2,1,0:T(8,128)(2,1)S(1)} %all-to-all-done.refs_7_.refs_9_), channel_id=1, source_target_pairs={{0,1},{1,0},{2,3},{3,2},{4,5},{5,4},{6,7},{7,6},{8,9},{9,8},{10,11... | collective-permute-start | bytes 4718600 | tf_op jit(solution)/shard_map/ppermute | solution.py:183
  74.6 14.9 %copy-start = (bf16[32,4096]{1,0:T(8,128)(2,1)S(1)}, bf16[32,4096]{1,0:T(8,128)(2,1)}, u32[]{:S(2)}) copy-start(bf16[32,4096]{1,0:T(8,128)(2,1)} %get-tuple-element.33.refs_4_) | copy-start | bytes 786436
  81.0 15.7 %collective-permute-start.11 = (bf16[32,4096]{1,0:T(8,128)(2,1)S(1)}, bf16[32,4096]{1,0:T(8,128)(2,1)S(1)}, u32[]{:S(2)}, u32[]{:S(2)}) collective-permute-start(bf16[32,4096]{1,0:T(8,128)(2,1)S(1)} %get-tuple-element.43), channel_id=1, source_target_pairs={{0,268},{1,5},{2,270},{3,7},{4,0},{5,9},{6,2},{7,11},{8,4},{9,13},... | collective-permute-start | bytes 786440 | tf_op jit(solution)/shard_map/ppermute | solution.py:30
  83.0 13.8 %collective-permute-start.12 = (bf16[32,4096]{1,0:T(8,128)(2,1)S(1)}, bf16[32,4096]{1,0:T(8,128)(2,1)S(1)}, u32[]{:S(2)}, u32[]{:S(2)}) collective-permute-start(bf16[32,4096]{1,0:T(8,128)(2,1)S(1)} %get-tuple-element.44), channel_id=1, source_target_pairs={{0,270},{1,3},{2,0},{3,5},{4,2},{5,7},{6,4},{7,9},{8,6},{9,11},{10... | collective-permute-start | bytes 786440 | tf_op jit(solution)/shard_map/ppermute | solution.py:30
  85.4 12.0 %collective-permute-start.13 = (bf16[32,4096]{1,0:T(8,128)(2,1)S(1)}, bf16[32,4096]{1,0:T(8,128)(2,1)S(1)}, u32[]{:S(2)}, u32[]{:S(2)}) collective-permute-start(bf16[32,4096]{1,0:T(8,128)(2,1)S(1)} %get-tuple-element.45), channel_id=1, source_target_pairs={{0,2},{1,271},{2,4},{3,1},{4,6},{5,3},{6,8},{7,5},{8,10},{9,7},{10... | collective-permute-start | bytes 786440 | tf_op jit(solution)/shard_map/ppermute | solution.py:30
  97.5 8.6 %collective-permute-start.16 = (bf16[32,4096]{1,0:T(8,128)(2,1)S(1)}, bf16[32,4096]{1,0:T(8,128)(2,1)S(1)}, u32[]{:S(2)}, u32[]{:S(2)}) collective-permute-start(bf16[32,4096]{1,0:T(8,128)(2,1)S(1)} %add_convert_fusion.2), channel_id=1, source_target_pairs={{0,2},{1,271},{2,4},{3,1},{4,6},{5,3},{6,8},{7,5},{8,10},{9,7},{10... | collective-permute-start | bytes 786440 | tf_op jit(solution)/shard_map/ppermute | solution.py:30
  102.9 8.3 %collective-permute-start.14 = (bf16[32,4096]{1,0:T(8,128)(2,1)S(1)}, bf16[32,4096]{1,0:T(8,128)(2,1)S(1)}, u32[]{:S(2)}, u32[]{:S(2)}) collective-permute-start(bf16[32,4096]{1,0:T(8,128)(2,1)S(1)} %add_convert_fusion.4), channel_id=1, source_target_pairs={{0,270},{1,3},{2,0},{3,5},{4,2},{5,7},{6,4},{7,9},{8,6},{9,11},{10... | collective-permute-start | bytes 786440 | tf_op jit(solution)/shard_map/ppermute | solution.py:30
  106.2 8.3 %collective-permute-start.17 = (bf16[32,4096]{1,0:T(8,128)(2,1)S(1)}, bf16[32,4096]{1,0:T(8,128)(2,1)S(1)}, u32[]{:S(2)}, u32[]{:S(2)}) collective-permute-start(bf16[32,4096]{1,0:T(8,128)(2,1)S(1)} %add_convert_fusion.1), channel_id=1, source_target_pairs={{0,2},{1,271},{2,4},{3,1},{4,6},{5,3},{6,8},{7,5},{8,10},{9,7},{10... | collective-permute-start | bytes 786440 | tf_op jit(solution)/shard_map/ppermute | solution.py:30
  111.3 9.3 %collective-permute-start.15 = (bf16[32,4096]{1,0:T(8,128)(2,1)S(1)}, bf16[32,4096]{1,0:T(8,128)(2,1)S(1)}, u32[]{:S(2)}, u32[]{:S(2)}) collective-permute-start(bf16[32,4096]{1,0:T(8,128)(2,1)S(1)} %add_convert_fusion.3), channel_id=1, source_target_pairs={{0,270},{1,3},{2,0},{3,5},{4,2},{5,7},{6,4},{7,9},{8,6},{9,11},{10... | collective-permute-start | bytes 786440 | tf_op jit(solution)/shard_map/ppermute | solution.py:30
